TPU v7x, 256 devices: a whole 4x4x8 slice. The times are simulated.
256 devices in a mesh: section: 64 (over y, x, z_hi, core), tensor: 4 (over z_lo).
Axes of the slice: x: 4, y: 4, z: 8 (z_hi: 2, z_lo: 4; z = z_hi * 4 + z_lo), core: 2. Of those that a mesh axis runs over, the one named last changes fastest.
Arguments:
- fwd_in: bfloat16 [64, 256, 2048], P('section', None, 'tensor'), may hold values from -24 to 24
- bwd_in: bfloat16 [64, 256, 2048], P('section', None, 'tensor'), may hold values from -24 to 24
- cotangent: bfloat16 [64, 256, 2048], P('section', None, 'tensor'), may hold values from -6 to 6
- enc_saved: bfloat16 [256, 2048], P(None, 'tensor'), may hold values from -24 to 24
- norm_gain: bfloat16 [64, 2048], P('section', 'tensor'), may hold values from 0.099609375 to 1.8984375
- final_gain: bfloat16 [2048], P('tensor'), may hold values from 0.099609375 to 1.8984375
- w_qkv: bfloat16 [64, 2048, 3, 2048], P('section', None, None, 'tensor'), may hold values from -0.125 to 0.125
- w_out: bfloat16 [64, 2048, 2048], P('section', 'tensor'), may hold values from -0.375 to 0.375
Outputs:
- fwd_out: bfloat16 [64, 256, 2048], P('section', None, 'tensor')
- grad_in: bfloat16 [64, 256, 2048], P('section', None, 'tensor')
All inputs are finite; a program needn't handle non-finite values.
Results may differ from a plain program's by a relative error of at most 0.017.
Values may be sent and summed in bfloat16 or wider, within the bound.
No kernel may reach another device: no remote copies, remote signals or barrier semaphores. Data moves between devices by JAX's collectives and lax.ppermute only.
A program may use at most 128 MiB of HBM per device.

v0:
```python
import jax
import jax.numpy as jnp
from jax import lax
from jax.sharding import PartitionSpec as P

HEAD_DIM = 256
NY, NX, NZ, NC, NT = 4, 4, 2, 2, 4
SECTION_COUNT = NY * NX * NZ * NC
ENC_SECTIONS = SECTION_COUNT // 2
LAST = ENC_SECTIONS - 1

epsilon = 1e-06
f32 = jnp.float32
bf16 = jnp.bfloat16

PLACES = [
    (y, x, z, c, t)
    for y in range(NY)
    for x in range(NX)
    for z in range(NZ)
    for c in range(NC)
    for t in range(NT)
]


def place_index(place):
    y, x, z, c, t = place
    return (((y * NX + x) * NZ + z) * NC + c) * NT + t


def section_of(place):
    return place_index(place) // NT


def move(value, route):
    pairs = []
    for place in PLACES:
        target = route(*place)
        if target is not None:
            pairs.append((place_index(place), place_index(target)))
    return lax.ppermute(value, ("section", "tensor"), pairs)


def is_dec(y):
    return y >= NY // 2


def everyone(y, z):
    return True


def encoders(y, z):
    return y < NY // 2


def decoders(y, z):
    return y >= NY // 2


def top_row(y, z):
    return y == 1 and z == 1


def swap_x(value, k, who):
    return move(value, lambda y, x, z, c, t: (y, x ^ k, z, c, t) if who(y, z) else None)


def swap_core(value, who):
    return move(value, lambda y, x, z, c, t: (y, x, z, 1 - c, t) if who(y, z) else None)


def swap_t(value, k, who):
    return move(value, lambda y, x, z, c, t: (y, x, z, c, t ^ k) if who(y, z) else None)


def after(value, *others):
    return lax.optimization_barrier((value,) + others)[0]


def tie(value, other):
    return lax.optimization_barrier((value, other))


def line_scatter(total, row_part, who):
    rows, width = total.shape[0], total.shape[1] // NT
    give = total[:, 2 * width :]
    if row_part is not None:
        high = row_part.astype(bf16)
        low = (row_part - high.astype(f32)).astype(bf16)
        extra = jnp.concatenate([high, low]).reshape(1, 2 * rows)
        extra = jnp.pad(extra, ((0, 0), (0, 2 * width - 2 * rows))) if 2 * rows < 2 * width else extra
        give = jnp.concatenate([give, extra], axis=0)
    got = swap_t(give, 1, who).astype(f32)
    pair = total[:, : 2 * width].astype(f32) + got[:rows]
    give = pair[:, width:].astype(bf16)
    if row_part is not None:
        sums = row_part + got[rows, :rows] + got[rows, rows : 2 * rows]
        high = sums.astype(bf16)
        low = (sums - high.astype(f32)).astype(bf16)
        extra = jnp.concatenate([high, low]).reshape(2 * rows // width, width)
        give = jnp.concatenate([give, extra], axis=0)
    got = swap_t(give, 2, who).astype(f32)
    summed = pair[:, :width] + got[:rows]
    if row_part is None:
        return summed, None
    tail = got[rows:].reshape(2 * rows)
    return summed, (sums + tail[:rows] + tail[rows:]).reshape(rows, 1)


def inverse_rms(values):
    return lax.rsqrt(jnp.mean(values * values, axis=-1, keepdims=True) + epsilon)


def scale_rows(values, inverse, gain_row):
    return (values * inverse * gain_row).astype(bf16)


def mm(a, b):
    return jnp.dot(a, b, preferred_element_type=f32)


def mm_t(a, b):
    return lax.dot_general(a, b, (((1,), (1,)), ((), ())), preferred_element_type=f32)


def t_mm(a, b):
    return lax.dot_general(a, b, (((0,), (0,)), ((), ())), preferred_element_type=f32)


def heads_of(matrix):
    return [matrix[:, h * HEAD_DIM : (h + 1) * HEAD_DIM] for h in range(matrix.shape[1] // HEAD_DIM)]


def softmax_rows(queries, keys):
    weights = jnp.exp(mm_t(queries, keys) * HEAD_DIM ** (-0.5))
    return weights / jnp.sum(weights, axis=-1, keepdims=True)


def attend_out(q, k, v, w_proj):
    mixed = [
        mm(softmax_rows(qh, kh).astype(bf16), vh).astype(bf16)
        for qh, kh, vh in zip(heads_of(q), heads_of(k), heads_of(v))
    ]
    return mm(jnp.concatenate(mixed, axis=1), w_proj)


def attend_back(q, k, v, upstream, w_proj):
    grad_mix = mm_t(upstream, w_proj).astype(bf16)
    dq, dk, dv = [], [], []
    for qh, kh, vh, gh in zip(heads_of(q), heads_of(k), heads_of(v), heads_of(grad_mix)):
        weights = softmax_rows(qh, kh)
        dv.append(t_mm(weights.astype(bf16), gh).astype(bf16))
        grad_weights = mm_t(gh, vh)
        grad_scores = (
            weights
            * (grad_weights - jnp.sum(weights * grad_weights, axis=-1, keepdims=True))
            * HEAD_DIM ** (-0.5)
        ).astype(bf16)
        dq.append(mm(grad_scores, kh).astype(bf16))
        dk.append(t_mm(grad_scores, qh).astype(bf16))
    return [jnp.concatenate(parts, axis=1) for parts in (dq, dk, dv)]


def gather_rows(own, who):
    half = jnp.concatenate([own] + [swap_x(own, k, who) for k in range(1, NX)], axis=0)
    return jnp.concatenate([half, swap_core(half, who)], axis=0)


def following(kind):
    def go(y, x, z, c, t):
        s = section_of((y, x, z, c, t))
        n = ((s + 1) % SECTION_COUNT) * NT + t
        return None if s == LAST or is_dec(y) != kind else PLACES[n]

    return go


def body(fwd_in, bwd_in, cotangent, enc_saved, norm_gain, final_gain, w_qkv, w_out):
    section_index = lax.axis_index("section")
    t = lax.axis_index("tensor")
    core = section_index % NC
    x_at = section_index // (NC * NZ) % NX
    dec = section_index >= ENC_SECTIONS
    last = section_index == LAST
    fwd_shard, bwd_shard, cot_shard = fwd_in[0], bwd_in[0], cotangent[0]
    rows, width = fwd_shard.shape
    full = width * NT
    part = rows // (NX * NC)
    half = rows // NC

    own_rows = lax.dynamic_slice_in_dim(enc_saved, (x_at * NC + core) * part, part, 0)
    a_shard = jnp.concatenate(
        [jnp.where(dec, bwd_shard, fwd_shard), own_rows, norm_gain, final_gain[None]], axis=0
    )
    b_shard = jnp.where(dec, cot_shard, bwd_shard)
    a_far = swap_t(a_shard, 2, everyone)
    a_pair = jnp.concatenate([a_shard, a_far], axis=1)
    b_far = swap_t(after(b_shard, a_far), 2, everyone)
    a_near = swap_t(a_pair, 1, everyone)
    b_pair = jnp.concatenate([b_shard, b_far], axis=1)
    a_all = jnp.concatenate([a_pair, a_near], axis=1)
    small = a_all[rows:].astype(f32)
    saved, gain, final = small[:part], small[part : part + 1], small[part + 1 :]

    order = [t, t ^ 2, t ^ 1, t ^ 3]
    w_in = w_qkv[0]
    turned = [lax.dynamic_slice_in_dim(w_in, o * width, width, 0) for o in order]
    w_q, w_k, w_v = (jnp.concatenate([w[:, i] for w in turned], axis=0) for i in range(3))
    w_o = jnp.concatenate([lax.dynamic_slice_in_dim(w_out[0], o * width, width, 1) for o in order], axis=1)

    a_values = a_all[:rows].astype(f32)
    a_inverse = inverse_rms(a_values)
    a_normed = scale_rows(a_values, a_inverse, gain)
    def project(normed, source):
        return mm(normed, w_q).astype(bf16), mm(source, w_k).astype(bf16), mm(source, w_v).astype(bf16)

    def enc_phase1(_):
        b_near = swap_t(b_pair, 1, encoders)
        out = attend_out(*project(a_normed, a_normed), w_o).astype(bf16)
        out, b_near = tie(out, b_near)
        summed, _ = line_scatter(out, None, encoders)
        enc_y = (fwd_shard.astype(f32) + summed).astype(bf16)
        blocks = enc_y.reshape(NX, NC, part, width)
        passed, c_shard = tie(swap_core(blocks[:, 0], top_row), cot_shard)
        blocks = jnp.where(core == 1, blocks[:, 1], passed)
        c_far = swap_t(c_shard, 2, encoders)
        top = blocks[NX - 1]
        for k in range(1, NX):
            top = jnp.where(x_at ^ (NX - 1) == k, swap_x(blocks[(NX - 1) ^ k], k, top_row), top)
        return enc_y, top, b_near, c_far, out, out[:part]

    def dec_phase1(_):
        b_near = swap_t(b_pair, 1, decoders)
        c_far = swap_t(fwd_shard, 2, decoders)
        q = mm(a_normed, w_q).astype(bf16)
        saved_rows, q = tie(scale_rows(saved, inverse_rms(saved), final), q)
        saved_half = jnp.concatenate([saved_rows] + [swap_x(saved_rows, k, decoders) for k in range(1, NX)], axis=0)
        saved_half, b_near, c_far = lax.optimization_barrier((saved_half, b_near, c_far))
        saved_normed = jnp.concatenate([saved_half, swap_core(saved_half, decoders)], axis=0)
        k, v = mm(saved_normed, w_k).astype(bf16), mm(saved_normed, w_v).astype(bf16)
        c_near = swap_t(jnp.concatenate([fwd_shard, c_far], axis=1), 1, decoders)
        b_full = jnp.concatenate([b_pair, b_near], axis=1)
        dq, dk, dv = attend_back(q, k, v, b_full, w_o)
        dc = (mm_t(dk, w_k) + mm_t(dv, w_v)).astype(bf16)
        dn = mm_t(dq, w_q).astype(bf16)
        acc = dc[:half].astype(f32) + swap_core(dc[half:], decoders).astype(f32)
        acc16 = acc.astype(bf16)
        total = acc[:part]
        for k in range(1, NX):
            total = total + swap_x(acc16[k * part : (k + 1) * part], k, decoders).astype(f32)
        total, c_near = tie(total.astype(bf16), c_near)
        return fwd_shard, fwd_shard[:part], c_near, c_far, dn, total

    enc_y, top, near, c_far, dn, total = lax.cond(~dec, enc_phase1, dec_phase1, 0)

    arrivals = [
        move(total, lambda y, x, z, c, tt: (1, x, z, c, tt) if y == y_from else None) for y_from in (2, 3)
    ]
    dc_from2, dc_from3 = arrivals
    arrivals = [
        move(top, lambda y, x, z, c, tt: (y_to, x, z_to, c, tt) if y == 1 and z == 1 else None)
        for y_to in (2, 3)
        for z_to in (0, 1)
    ]
    top = sum(arrivals)

    def enc_phase2(_):
        b_full = jnp.concatenate([b_pair, near], axis=1)
        first_row = lambda y, z: y == 1
        dc_sum = dc_from2.astype(f32) + dc_from3.astype(f32)
        pair = dc_sum[:, : 2 * width] + swap_t(dc_sum[:, 2 * width :].astype(bf16), 1, first_row).astype(f32)
        mine = pair[:, :width] + swap_t(pair[:, width:].astype(bf16), 2, first_row).astype(f32)
        mine16 = mine.astype(bf16)
        mine = mine + move(
            mine16, lambda y, x, z, c, tt: (y, x, 1, c, tt) if y == 1 and z == 0 else None
        ).astype(f32)
        mine = mine.astype(bf16)
        pair = jnp.concatenate([mine, swap_t(mine, 2, top_row)], axis=1)
        u = jnp.concatenate([pair, swap_t(pair, 1, top_row)], axis=1)
        c_pair = jnp.concatenate([cot_shard, c_far], axis=1)
        c_pair, u = tie(c_pair, u)
        c_near = swap_t(c_pair, 1, encoders)
        u = final * u.astype(f32)
        r = inverse_rms(saved)
        block = (r * u - saved * r**3 * jnp.mean(u * saved, axis=-1, keepdims=True)).astype(bf16)
        slots = jnp.concatenate([block] + [swap_x(block, k, top_row) for k in range(1, NX)], axis=0)
        slots, c_near, y_out = lax.optimization_barrier((slots, c_near, enc_y))
        c_full = jnp.concatenate([c_pair, c_near], axis=1)
        swapped = swap_core(slots, top_row)
        pieces = []
        for xi in range(NX):
            k = xi ^ (NX - 1)
            pieces += [swapped[k * part : (k + 1) * part], slots[k * part : (k + 1) * part]]
        returned_full = jnp.concatenate(pieces, axis=0)
        sent = move(y_out, following(False))
        values = b_full.astype(f32)
        inverse = inverse_rms(values)
        normed = scale_rows(values, inverse, gain)
        q, k, v = project(normed, normed)
        upstream = jnp.where(last, returned_full, c_full)
        dq, dk, dv = attend_back(q, k, v, upstream, w_o)
        term = (mm_t(dq, w_q) + mm_t(dk, w_k) + mm_t(dv, w_v)).astype(bf16)
        term, sent = tie(term, sent)
        summed, row_sum = line_scatter(term, jnp.sum(gain * term.astype(f32) * values, axis=-1), encoders)
        return sent, summed, row_sum, inverse, upstream[:, :width]

    def dec_phase2(_):
        c_full = jnp.concatenate([fwd_shard, c_far, near], axis=1)
        all_top = jnp.concatenate([top, swap_t(top, 2, decoders)], axis=1)
        all_top = jnp.concatenate([all_top, swap_t(all_top, 1, decoders)], axis=1).astype(f32)
        row_part = jnp.sum(gain * dn.astype(f32) * a_values, axis=-1)
        dn_tied, all_top = tie(dn, all_top)
        dn_sum, row_sum = line_scatter(dn_tied, row_part, decoders)
        top_full = gather_rows(scale_rows(all_top, inverse_rms(all_top), final), decoders)
        values = c_full.astype(f32)
        normed = scale_rows(values, inverse_rms(values), gain)
        out = attend_out(*project(normed, top_full), w_o).astype(bf16)
        out, dn_sum = tie(out, dn_sum)
        summed, _ = line_scatter(out, None, decoders)
        dec_y = (fwd_shard.astype(f32) + summed).astype(bf16)
        return dec_y, dn_sum, row_sum, a_inverse, cot_shard

    sent, summed, row_sum, inverse, upstream = lax.cond(dec, dec_phase2, enc_phase2, 0)
    arrived = move(sent, following(True))
    from_enc = (~dec) & (section_index > 0)
    fwd_out = jnp.where(from_enc, sent, arrived)[None]
    grad_in = (
        upstream.astype(f32)
        + inverse * (gain[:, :width] * summed)
        - bwd_shard.astype(f32) * inverse**3 * (row_sum / full)
    ).astype(bf16)[None]
    return (fwd_out, grad_in)


def solution(mesh):
    in_specs = (
        P("section", None, "tensor"),
        P("section", None, "tensor"),
        P("section", None, "tensor"),
        P(None, "tensor"),
        P("section", "tensor"),
        P("tensor"),
        P("section", None, None, "tensor"),
        P("section", "tensor", None),
    )
    out_specs = (P("section", None, "tensor"), P("section", None, "tensor"))
    return jax.shard_map(body, mesh=mesh, in_specs=in_specs, out_specs=out_specs, check_vma=False)
```

profile of v0, /device:TPU:11, one launch (start us, length us, event | category | flops | bytes accessed | tf_op | source)
XLA Modules:
  0.0 243.4 jit_solution(385007826619771194)
XLA Ops:
  1.6 1.9 bitcast_select_fusion
  3.5 1.4 pad_maximum_fusion.28
  4.9 3.0 %collective-permute-start.42 = (bf16[290,512]{1,0:T(8,128)(2,1)}, bf16[290,512]{1,0:T(8,128)(2,1)S(1)}, u32[]{:S(2)}, u32[]{:S(2)}) collective-permute-start(bf16[290,512]{1,0:T(8,128)(2,1)} %pad_maximum_fusion.28), channel_id=1, source_target_pairs={{0,2},{1,3},{2,0},{3,1},{4,6},{5,7},{6,4},{7,5},{8,10},{9,11},{10,... | collective-permute-start | bytes 890888 | tf_op jit(solution)/shard_map/ppermute | solution.py:41
  7.9 1.7 dynamic-slice_bitcast_fusion.7
  9.5 3.3 %dynamic-slice_bitcast_fusion.3 = (bf16[512,3,512]{2,0,1:T(8,128)(2,1)S(1)}, bf16[512,3,512]{2,0,1:T(8,128)(2,1)S(1)}, bf16[512,3,512]{2,0,1:T(8,128)(2,1)S(1)}, bf16[512,3,512]{2,0,1:T(8,128)(2,1)S(1)}) fusion(bf16[1,2048,3,512]{3,1,2,0:T(8,128)(2,1)} %param.18, s32[]{:T(128)S(6)} %select_n.96, s32[]{:T(128)S(6)} %select_n.97, s32[]{:T(128)S(6)} %select_n.99, ...), kind=kLoop, calls=%fused_computation.301 | loop fusion | bytes 12582928 | tf_op jit(solution)/shard_map/dynamic_slice | solution.py:207
  12.8 1.4 slice_bitcast_fusion.12
  14.2 1.8 slice_bitcast_fusion.10
  16.0 1.6 pad_maximum_fusion.19
  17.8 3.7 %collective-permute-done.42 = bf16[290,512]{1,0:T(8,128)(2,1)S(1)} collective-permute-done((bf16[290,512]{1,0:T(8,128)(2,1)}, bf16[290,512]{1,0:T(8,128)(2,1)S(1)}, u32[]{:S(2)}, u32[]{:S(2)}) %collective-permute-start.42) | collective-permute-done | bytes 296992 | tf_op jit(solution)/shard_map/ppermute | solution.py:41
  21.6 1.4 collective-permute-start.44
  23.9 3.0 %collective-permute-start.43 = (bf16[256,512]{1,0:T(8,128)(2,1)S(1)}, bf16[256,512]{1,0:T(8,128)(2,1)S(1)}, u32[]{:S(2)}, u32[]{:S(2)}) collective-permute-start(bf16[256,512]{1,0:T(8,128)(2,1)S(1)} %copy-done.28), channel_id=1, source_target_pairs={{0,2},{1,3},{2,0},{3,1},{4,6},{5,7},{6,4},{7,5},{8,10},{9,11},{10,... | collective-permute-start | bytes 786440 | tf_op jit(solution)/shard_map/ppermute | solution.py:41
  26.9 1.5 pad_maximum_fusion.17
  28.4 12.7 %collective-permute-done.43 = bf16[256,512]{1,0:T(8,128)(2,1)S(1)} collective-permute-done((bf16[256,512]{1,0:T(8,128)(2,1)S(1)}, bf16[256,512]{1,0:T(8,128)(2,1)S(1)}, u32[]{:S(2)}, u32[]{:S(2)}) %collective-permute-start.43) | collective-permute-done | bytes 262176 | tf_op jit(solution)/shard_map/ppermute | solution.py:41
  43.8 68.4 %conditional.3 = (bf16[256,512]{1,0:T(8,128)(2,1)}, bf16[32,512]{1,0:T(8,128)(2,1)S(1)}, bf16[256,1024]{1,0:T(8,128)(2,1)}, bf16[256,512]{1,0:T(8,128)(2,1)}, bf...) conditional(s32[]{:T(128)} %convert_element_type.341, (bf16[256,512]{1,0:T(8,128)(2,1)S(1)}, ...), branch_computations={%region_1.7_spmd, %region_7.10_spmd} | conditional | flops 4106353664 | bytes 56841192 | solution.py:254
  43.8 6.1 %collective-permute-start.11 = (bf16[256,1024]{1,0:T(8,128)(2,1)S(1)}, bf16[256,1024]{1,0:T(8,128)(2,1)}, u32[]{:S(2)}, u32[]{:S(2)}) collective-permute-start(bf16[256,1024]{1,0:T(8,128)(2,1)S(1)} %get-tuple-element.145), channel_id=1, source_target_pairs={{0,1},{1,0},{2,3},{3,2},{4,5},{5,4},{6,7},{7,6},{8,9},{9,8},{10,11... | collective-permute-start | bytes 1572872 | tf_op jit(solution)/shard_map/cond/branch_1_fun/ppermute | solution.py:41
  50.0 2.3 convolution_convert_fusion.14
  54.7 1.7 convolution_convert_fusion.11
  56.4 4.7 %collective-permute-done.11 = bf16[256,1024]{1,0:T(8,128)(2,1)} collective-permute-done((bf16[256,1024]{1,0:T(8,128)(2,1)S(1)}, bf16[256,1024]{1,0:T(8,128)(2,1)}, u32[]{:S(2)}, u32[]{:S(2)}) %collective-permute-start.11) | collective-permute-done | bytes 524320 | tf_op jit(solution)/shard_map/cond/branch_1_fun/ppermute | solution.py:41
  61.1 1.1 slice.245
  62.2 3.0 %collective-permute-start.12 = (bf16[256,1024]{1,0:T(8,128)(2,1)S(1)}, bf16[256,1024]{1,0:T(8,128)(2,1)S(1)}, u32[]{:S(2)}, u32[]{:S(2)}) collective-permute-start(bf16[256,1024]{1,0:T(8,128)(2,1)S(1)} %slice.245), channel_id=1, source_target_pairs={{0,1},{1,0},{2,3},{3,2},{4,5},{5,4},{6,7},{7,6},{8,9},{9,8},{10,11... | collective-permute-start | bytes 1572872 | tf_op jit(solution)/shard_map/cond/branch_1_fun/ppermute | solution.py:41
  65.3 10.6 %collective-permute-done.12 = bf16[256,1024]{1,0:T(8,128)(2,1)S(1)} collective-permute-done((bf16[256,1024]{1,0:T(8,128)(2,1)S(1)}, bf16[256,1024]{1,0:T(8,128)(2,1)S(1)}, u32[]{:S(2)}, u32[]{:S(2)}) %collective-permute-start.12) | collective-permute-done | bytes 524320 | tf_op jit(solution)/shard_map/cond/branch_1_fun/ppermute | solution.py:41
  75.9 1.2 convert_add_fusion.1
  77.2 2.2 collective-permute-start.13
  79.4 13.8 %collective-permute-done.13 = bf16[256,512]{1,0:T(8,128)(2,1)S(1)} collective-permute-done((bf16[256,512]{1,0:T(8,128)(2,1)S(1)}, bf16[256,512]{1,0:T(8,128)(2,1)S(1)}, u32[]{:S(2)}, u32[]{:S(2)}) %collective-permute-start.13) | collective-permute-done | bytes 262176 | tf_op jit(solution)/shard_map/cond/branch_1_fun/ppermute | solution.py:41
  93.2 0.8 fusion.45
  94.0 1.6 slice_bitcast_fusion
  95.6 1.3 collective-permute-start.14
  96.9 1.9 collective-permute-start.18
  98.8 0.9 fusion.49
  101.0 1.3 collective-permute-start.17
  102.3 1.3 collective-permute-start.16
  103.6 1.3 collective-permute-start.15
  104.8 0.9 slice.254
  106.6 5.6 %collective-permute-done.18 = bf16[256,512]{1,0:T(8,128)(2,1)} collective-permute-done((bf16[256,512]{1,0:T(8,128)(2,1)}, bf16[256,512]{1,0:T(8,128)(2,1)}, u32[]{:S(2)}, u32[]{:S(2)}) %collective-permute-start.18) | collective-permute-done | bytes 262176 | tf_op jit(solution)/shard_map/cond/branch_1_fun/ppermute | solution.py:41
  114.4 1.4 collective-permute-start.46
  115.8 1.3 collective-permute-start.45
  117.1 1.6 fusion.137
  120.0 2.5 %collective-permute-done.46 = bf16[32,2048]{1,0:T(8,128)(2,1)S(1)} collective-permute-done((bf16[32,2048]{1,0:T(8,128)(2,1)S(1)}, bf16[32,2048]{1,0:T(8,128)(2,1)S(1)}, u32[]{:S(2)}, u32[]{:S(2)}) %collective-permute-start.46) | collective-permute-done | bytes 131104 | tf_op jit(solution)/shard_map/ppermute | solution.py:41
  122.5 3.2 %collective-permute-done.45 = bf16[32,2048]{1,0:T(8,128)(2,1)S(1)} collective-permute-done((bf16[32,2048]{1,0:T(8,128)(2,1)S(1)}, bf16[32,2048]{1,0:T(8,128)(2,1)S(1)}, u32[]{:S(2)}, u32[]{:S(2)}) %collective-permute-start.45) | collective-permute-done | bytes 131104 | tf_op jit(solution)/shard_map/ppermute | solution.py:41
  125.7 114.2 %conditional.5 = (bf16[256,512]{1,0:T(8,128)(2,1)S(1)}, f32[256,512]{1,0:T(8,128)S(1)}, f32[256,1]{0,1:T(1,128)S(1)}, f32[256,1]{0,1:T(1,128)S(1)}, f32[256,512]{1,0:T(8,128)S(1)}) conditional(s32[]{:T(128)} %convert_element_type.340, (bf16[256,1024]{1,0:T(8,128)(2,1)S(1)}, bf16[256,1024]{1,0:T(8,128)(2,1)}, f32[1,2048]{1,0:T(1,128)S(1)}, ...), branch_computations={%region_10.19_spmd, %region_19.25_spmd} | conditional | flops 4128456704 | bytes 93346760
  125.8 1.9 collective-permute-start.19
  127.7 1.3 fusion.63
  129.0 1.7 collective-permute-done.19
  130.8 2.9 %collective-permute-start.20 = (bf16[32,512]{1,0:T(8,128)(2,1)S(1)}, bf16[32,512]{1,0:T(8,128)(2,1)S(1)}, u32[]{:S(2)}, u32[]{:S(2)}) collective-permute-start(bf16[32,512]{1,0:T(8,128)(2,1)S(1)} %slice.606), channel_id=1, source_target_pairs={{64,66},{65,67},{66,64},{67,65},{68,70},{69,71},{70,68},{71,69},{7... | collective-permute-start | bytes 98312 | tf_op jit(solution)/shard_map/cond/branch_0_fun/ppermute | solution.py:41
  133.8 2.6 %collective-permute-done.20 = bf16[32,512]{1,0:T(8,128)(2,1)S(1)} collective-permute-done((bf16[32,512]{1,0:T(8,128)(2,1)S(1)}, bf16[32,512]{1,0:T(8,128)(2,1)S(1)}, u32[]{:S(2)}, u32[]{:S(2)}) %collective-permute-start.20) | collective-permute-done | bytes 32800 | tf_op jit(solution)/shard_map/cond/branch_0_fun/ppermute | solution.py:41
  136.4 9.3 %collective-permute-start.21 = (bf16[32,512]{1,0:T(8,128)(2,1)S(1)}, bf16[32,512]{1,0:T(8,128)(2,1)S(1)}, u32[]{:S(2)}, u32[]{:S(2)}) collective-permute-start(bf16[32,512]{1,0:T(8,128)(2,1)S(1)} %fusion.99), channel_id=1, source_target_pairs={{64,72},{65,73},{66,74},{67,75},{68,76},{69,77},{70,78},{71,79},{8... | collective-permute-start | bytes 98312 | tf_op jit(solution)/shard_map/cond/branch_0_fun/ppermute | solution.py:41
  145.7 1.8 convolution_convert_fusion.19
  148.2 2.6 %convolution_convert_fusion.20 = bf16[256,512]{1,0:T(8,128)(2,1)S(1)} fusion(bf16[2048,512]{1,0:T(8,128)(2,1)} %get-tuple-element.156, f32[2048]{0:T(1024)S(1)} %bitcast.182, f32[256]{0:T(256)S(1)} %add_rsqrt_fusion.1, bf16[256,1024]{1,0:T(8,128)(2,1)} %get-tuple-element.154, bf16[256,1024]{1,0:T(8,128)(2,1)S(1)} %get-tuple-element.153), kind=kOutput, calls=%fused_computation.123 | convolution fusion | flops 540672000 | bytes 3417088 | tf_op jit(solution)/shard_map/cond/branch_0_fun/dot_general | solution.py:119
  151.5 1.1 pad_maximum_fusion.3
  152.7 1.9 collective-permute-start.27
  154.6 1.1 multiply_reduce_fusion.6
  155.8 1.1 subtract_convert_fusion
  159.2 5.0 %collective-permute-done.27 = bf16[256,1024]{1,0:T(8,128)(2,1)S(1)} collective-permute-done((bf16[256,1024]{1,0:T(8,128)(2,1)S(1)}, bf16[256,1024]{1,0:T(8,128)(2,1)S(1)}, u32[]{:S(2)}, u32[]{:S(2)}) %collective-permute-start.27) | collective-permute-done | bytes 524320 | tf_op jit(solution)/shard_map/cond/branch_0_fun/ppermute | solution.py:41
  165.1 1.8 convolution_convert_fusion.17
  166.9 31.7 %collective-permute-start.29 = (bf16[256,512]{1,0:T(8,128)(2,1)}, bf16[256,512]{1,0:T(8,128)(2,1)S(1)}, u32[]{:S(2)}, u32[]{:S(2)}) collective-permute-start(bf16[256,512]{1,0:T(8,128)(2,1)} %get-tuple-element.172), channel_id=1, source_target_pairs={{0,4},{1,5},{2,6},{3,7},{4,8},{5,9},{6,10},{7,11},{8,12},{9,13},{1... | collective-permute-start | bytes 786440 | tf_op jit(solution)/shard_map/cond/branch_0_fun/ppermute | solution.py:41
  199.2 1.1 copy-done.6
  203.0 2.3 fusion.71
  206.8 1.5 fusion.66
  208.4 2.0 collective-permute-start.30
  210.5 11.7 %collective-permute-done.30 = bf16[257,1024]{1,0:T(8,128)(2,1)S(1)} collective-permute-done((bf16[257,1024]{1,0:T(8,128)(2,1)S(1)}, bf16[257,1024]{1,0:T(8,128)(2,1)S(1)}, u32[]{:S(2)}, u32[]{:S(2)}) %collective-permute-start.30) | collective-permute-done | bytes 526368 | tf_op jit(solution)/shard_map/cond/branch_0_fun/ppermute | solution.py:41
  222.5 4.1 %collective-permute-start.31 = (bf16[257,512]{1,0:T(8,128)(2,1)S(1)}, bf16[257,512]{1,0:T(8,128)(2,1)S(1)}, u32[]{:S(2)}, u32[]{:S(2)}) collective-permute-start(bf16[257,512]{1,0:T(8,128)(2,1)S(1)} %pad_maximum_fusion.5), channel_id=1, source_target_pairs={{0,2},{1,3},{2,0},{3,1},{4,6},{5,7},{6,4},{7,5},{8,10},{9,11},{10,... | collective-permute-start | bytes 789512 | tf_op jit(solution)/shard_map/cond/branch_0_fun/ppermute | solution.py:41
  226.6 12.8 %collective-permute-done.31 = bf16[257,512]{1,0:T(8,128)(2,1)S(1)} collective-permute-done((bf16[257,512]{1,0:T(8,128)(2,1)S(1)}, bf16[257,512]{1,0:T(8,128)(2,1)S(1)}, u32[]{:S(2)}, u32[]{:S(2)}) %collective-permute-start.31) | collective-permute-done | bytes 263200 | tf_op jit(solution)/shard_map/cond/branch_0_fun/ppermute | solution.py:41
  239.9 0.8 collective-permute-start.51
  240.8 1.9 fusion.138
  (165 shorter events, 23.2 us)
Async XLA Ops:
  0.6 1.0 copy-start
  1.6 19.9 %copy-start.13 = (bf16[32,512]{1,0:T(8,128)(2,1)}, bf16[32,512]{1,0:T(8,128)(2,1)S(1)}, u32[]{:S(2)}) copy-start(bf16[32,512]{1,0:T(8,128)(2,1)S(1)} %constant_dynamic-slice_fusion) | copy-start | bytes 98308
  4.9 16.6 %collective-permute-start.42 = (bf16[290,512]{1,0:T(8,128)(2,1)}, bf16[290,512]{1,0:T(8,128)(2,1)S(1)}, u32[]{:S(2)}, u32[]{:S(2)}) collective-permute-start(bf16[290,512]{1,0:T(8,128)(2,1)} %pad_maximum_fusion.28), channel_id=1, source_target_pairs={{0,2},{1,3},{2,0},{3,1},{4,6},{5,7},{6,4},{7,5},{8,10},{9,11},{10,... | collective-permute-start | bytes 890888 | tf_op jit(solution)/shard_map/ppermute | solution.py:41
  16.0 1.6 copy-start.26
  16.0 1.6 copy-start.27
  17.6 3.9 %copy-start.30 = (bf16[1,512]{1,0:T(2,128)(2,1)S(1)}, bf16[1,512]{1,0:T(2,128)(2,1)}, u32[]{:S(2)}) copy-start(bf16[1,512]{1,0:T(2,128)(2,1)} %param.16) | copy-start | bytes 3076
  17.6 5.4 %copy-start.22 = (bf16[512,512]{1,0:T(8,128)(2,1)S(1)}, bf16[512,512]{1,0:T(8,128)(2,1)}, u32[]{:S(2)}) copy-start(bf16[512,512]{1,0:T(8,128)(2,1)} %get-tuple-element.295) | copy-start | bytes 1572868
  17.6 5.4 %copy-start.23 = (bf16[512,512]{1,0:T(8,128)(2,1)S(1)}, bf16[512,512]{1,0:T(8,128)(2,1)}, u32[]{:S(2)}) copy-start(bf16[512,512]{1,0:T(8,128)(2,1)} %get-tuple-element.311) | copy-start | bytes 1572868
  17.6 5.4 %copy-start.24 = (bf16[512,512]{1,0:T(8,128)(2,1)S(1)}, bf16[512,512]{1,0:T(8,128)(2,1)}, u32[]{:S(2)}) copy-start(bf16[512,512]{1,0:T(8,128)(2,1)} %get-tuple-element.301) | copy-start | bytes 1572868
  17.6 5.3 %copy-start.25 = (bf16[512,512]{1,0:T(8,128)(2,1)S(1)}, bf16[512,512]{1,0:T(8,128)(2,1)}, u32[]{:S(2)}) copy-start(bf16[512,512]{1,0:T(8,128)(2,1)} %get-tuple-element.308) | copy-start | bytes 1572868
  17.8 26.0 %copy-start.2 = (bf16[2048,512]{1,0:T(8,128)(2,1)}, bf16[2048,512]{1,0:T(8,128)(2,1)S(1)}, u32[]{:S(2)}) copy-start(bf16[2048,512]{1,0:T(8,128)(2,1)S(1)} %pad_maximum_fusion.20) | copy-start | bytes 6291460
  21.6 19.6 %collective-permute-start.44 = (bf16[290,1024]{1,0:T(8,128)(2,1)S(1)}, bf16[290,1024]{1,0:T(8,128)(2,1)S(1)}, u32[]{:S(2)}, u32[]{:S(2)}) collective-permute-start(bf16[290,1024]{1,0:T(8,128)(2,1)S(1)} %pad_maximum_fusion.26), channel_id=1, source_target_pairs={{0,1},{1,0},{2,3},{3,2},{4,5},{5,4},{6,7},{7,6},{8,9},{9,8},{10,11... | collective-permute-start | bytes 1781768 | tf_op jit(solution)/shard_map/ppermute | solution.py:41
  23.0 1.0 copy-start.28
  23.0 3.9 %copy-start.18 = (bf16[512,512]{1,0:T(8,128)(2,1)S(1)}, bf16[512,512]{1,0:T(8,128)(2,1)}, u32[]{:S(2)}) copy-start(bf16[512,512]{1,0:T(8,128)(2,1)} %get-tuple-element.296) | copy-start | bytes 1572868
  23.0 3.9 %copy-start.19 = (bf16[512,512]{1,0:T(8,128)(2,1)S(1)}, bf16[512,512]{1,0:T(8,128)(2,1)}, u32[]{:S(2)}) copy-start(bf16[512,512]{1,0:T(8,128)(2,1)} %get-tuple-element.310) | copy-start | bytes 1572868
  23.0 3.9 %copy-start.20 = (bf16[512,512]{1,0:T(8,128)(2,1)S(1)}, bf16[512,512]{1,0:T(8,128)(2,1)}, u32[]{:S(2)}) copy-start(bf16[512,512]{1,0:T(8,128)(2,1)} %get-tuple-element.302) | copy-start | bytes 1572868
  23.0 3.9 %copy-start.21 = (bf16[512,512]{1,0:T(8,128)(2,1)S(1)}, bf16[512,512]{1,0:T(8,128)(2,1)}, u32[]{:S(2)}) copy-start(bf16[512,512]{1,0:T(8,128)(2,1)} %get-tuple-element.307) | copy-start | bytes 1572868
  23.9 17.2 %collective-permute-start.43 = (bf16[256,512]{1,0:T(8,128)(2,1)S(1)}, bf16[256,512]{1,0:T(8,128)(2,1)S(1)}, u32[]{:S(2)}, u32[]{:S(2)}) collective-permute-start(bf16[256,512]{1,0:T(8,128)(2,1)S(1)} %copy-done.28), channel_id=1, source_target_pairs={{0,2},{1,3},{2,0},{3,1},{4,6},{5,7},{6,4},{7,5},{8,10},{9,11},{10,... | collective-permute-start | bytes 786440 | tf_op jit(solution)/shard_map/ppermute | solution.py:41
  26.9 14.3 %copy-start.14 = (bf16[32,512]{1,0:T(8,128)(2,1)S(1)}, bf16[32,512]{1,0:T(8,128)(2,1)}, u32[]{:S(2)}) copy-start(bf16[32,512]{1,0:T(8,128)(2,1)} %copy-done.13) | copy-start | bytes 98308
  41.2 2.6 %copy-start.9 = (bf16[256,1024]{1,0:T(8,128)(2,1)}, bf16[256,1024]{1,0:T(8,128)(2,1)S(1)}, u32[]{:S(2)}) copy-start(bf16[256,1024]{1,0:T(8,128)(2,1)S(1)} %pad_maximum_fusion.27) | copy-start | bytes 1572868
  41.5 0.6 copy-start.31
  42.1 1.7 copy-start.5
  42.1 1.7 copy-start.8
  43.8 17.3 %collective-permute-start.11 = (bf16[256,1024]{1,0:T(8,128)(2,1)S(1)}, bf16[256,1024]{1,0:T(8,128)(2,1)}, u32[]{:S(2)}, u32[]{:S(2)}) collective-permute-start(bf16[256,1024]{1,0:T(8,128)(2,1)S(1)} %get-tuple-element.145), channel_id=1, source_target_pairs={{0,1},{1,0},{2,3},{3,2},{4,5},{5,4},{6,7},{7,6},{8,9},{9,8},{10,11... | collective-permute-start | bytes 1572872 | tf_op jit(solution)/shard_map/cond/branch_1_fun/ppermute | solution.py:41
  62.2 13.7 %collective-permute-start.12 = (bf16[256,1024]{1,0:T(8,128)(2,1)S(1)}, bf16[256,1024]{1,0:T(8,128)(2,1)S(1)}, u32[]{:S(2)}, u32[]{:S(2)}) collective-permute-start(bf16[256,1024]{1,0:T(8,128)(2,1)S(1)} %slice.245), channel_id=1, source_target_pairs={{0,1},{1,0},{2,3},{3,2},{4,5},{5,4},{6,7},{7,6},{8,9},{9,8},{10,11... | collective-permute-start | bytes 1572872 | tf_op jit(solution)/shard_map/cond/branch_1_fun/ppermute | solution.py:41
  77.2 16.0 %collective-permute-start.13 = (bf16[256,512]{1,0:T(8,128)(2,1)S(1)}, bf16[256,512]{1,0:T(8,128)(2,1)S(1)}, u32[]{:S(2)}, u32[]{:S(2)}) collective-permute-start(bf16[256,512]{1,0:T(8,128)(2,1)S(1)} %slice.603), channel_id=1, source_target_pairs={{0,2},{1,3},{2,0},{3,1},{4,6},{5,7},{6,4},{7,5},{8,10},{9,11},{10,... | collective-permute-start | bytes 786440 | tf_op jit(solution)/shard_map/cond/branch_1_fun/ppermute | solution.py:41
  95.6 1.3 collective-permute-start.14
  96.9 15.3 %collective-permute-start.18 = (bf16[256,512]{1,0:T(8,128)(2,1)}, bf16[256,512]{1,0:T(8,128)(2,1)}, u32[]{:S(2)}, u32[]{:S(2)}) collective-permute-start(bf16[256,512]{1,0:T(8,128)(2,1)} %get-tuple-element.152), channel_id=1, source_target_pairs={{0,2},{1,3},{2,0},{3,1},{4,6},{5,7},{6,4},{7,5},{8,10},{9,11},{10,... | collective-permute-start | bytes 786440 | tf_op jit(solution)/shard_map/cond/branch_1_fun/ppermute | solution.py:41
  99.7 0.7 copy-start.29
  101.0 4.7 %collective-permute-start.17 = (bf16[32,512]{1,0:T(8,128)(2,1)}, bf16[32,512]{1,0:T(8,128)(2,1)}, u32[]{:S(2)}, u32[]{:S(2)}) collective-permute-start(bf16[32,512]{1,0:T(8,128)(2,1)} %get-tuple-element.251), channel_id=1, source_target_pairs={{72,88},{73,89},{74,90},{75,91},{76,92},{77,93},{78,94},{79,95},{8... | collective-permute-start | bytes 98312 | tf_op jit(solution)/shard_map/cond/branch_1_fun/ppermute | solution.py:41
  102.3 3.5 %collective-permute-start.16 = (bf16[32,512]{1,0:T(8,128)(2,1)}, bf16[32,512]{1,0:T(8,128)(2,1)}, u32[]{:S(2)}, u32[]{:S(2)}) collective-permute-start(bf16[32,512]{1,0:T(8,128)(2,1)} %get-tuple-element.252), channel_id=1, source_target_pairs={{72,104},{73,105},{74,106},{75,107},{76,108},{77,109},{78,110},{79... | collective-permute-start | bytes 98312 | tf_op jit(solution)/shard_map/cond/branch_1_fun/ppermute | solution.py:41
  103.6 2.2 collective-permute-start.15
  112.2 7.2 %copy-start.15 = (bf16[32,512]{1,0:T(8,128)(2,1)S(1)}, bf16[32,512]{1,0:T(8,128)(2,1)}, u32[]{:S(2)}) copy-start(bf16[32,512]{1,0:T(8,128)(2,1)} %copy-done.13) | copy-start | bytes 98308
  112.2 6.5 %collective-permute-start.50 = (bf16[32,512]{1,0:T(8,128)(2,1)S(1)}, bf16[32,512]{1,0:T(8,128)(2,1)S(1)}, u32[]{:S(2)}, u32[]{:S(2)}) collective-permute-start(bf16[32,512]{1,0:T(8,128)(2,1)S(1)} %get-tuple-element.216), channel_id=1, source_target_pairs={{72,200},{73,201},{74,202},{75,203},{76,204},{77,205},{78,206},{79... | collective-permute-start | bytes 98312 | tf_op jit(solution)/shard_map/ppermute | solution.py:41
  113.0 7.0 %collective-permute-start.49 = (bf16[32,512]{1,0:T(8,128)(2,1)S(1)}, bf16[32,512]{1,0:T(8,128)(2,1)S(1)}, u32[]{:S(2)}, u32[]{:S(2)}) collective-permute-start(bf16[32,512]{1,0:T(8,128)(2,1)S(1)} %get-tuple-element.216), channel_id=1, source_target_pairs={{72,192},{73,193},{74,194},{75,195},{76,196},{77,197},{78,198},{79... | collective-permute-start | bytes 98312 | tf_op jit(solution)/shard_map/ppermute | solution.py:41
  113.7 6.3 %collective-permute-start.48 = (bf16[32,512]{1,0:T(8,128)(2,1)S(1)}, bf16[32,512]{1,0:T(8,128)(2,1)S(1)}, u32[]{:S(2)}, u32[]{:S(2)}) collective-permute-start(bf16[32,512]{1,0:T(8,128)(2,1)S(1)} %get-tuple-element.216), channel_id=1, source_target_pairs={{72,136},{73,137},{74,138},{75,139},{76,140},{77,141},{78,142},{79... | collective-permute-start | bytes 98312 | tf_op jit(solution)/shard_map/ppermute | solution.py:41
  114.4 11.4 %copy-start.10 = (bf16[256,1024]{1,0:T(8,128)(2,1)S(1)}, bf16[256,1024]{1,0:T(8,128)(2,1)}, u32[]{:S(2)}) copy-start(bf16[256,1024]{1,0:T(8,128)(2,1)} %copy-done.9) | copy-start | bytes 1572868
  114.4 8.2 %collective-permute-start.46 = (bf16[32,2048]{1,0:T(8,128)(2,1)S(1)}, bf16[32,2048]{1,0:T(8,128)(2,1)S(1)}, u32[]{:S(2)}, u32[]{:S(2)}) collective-permute-start(bf16[32,2048]{1,0:T(8,128)(2,1)S(1)} %get-tuple-element.214), channel_id=1, source_target_pairs={{192,64},{193,65},{194,66},{195,67},{196,68},{197,69},{198,70},{19... | collective-permute-start | bytes 393224 | tf_op jit(solution)/shard_map/ppermute | solution.py:41
  115.8 9.9 %collective-permute-start.45 = (bf16[32,2048]{1,0:T(8,128)(2,1)S(1)}, bf16[32,2048]{1,0:T(8,128)(2,1)S(1)}, u32[]{:S(2)}, u32[]{:S(2)}) collective-permute-start(bf16[32,2048]{1,0:T(8,128)(2,1)S(1)} %get-tuple-element.214), channel_id=1, source_target_pairs={{128,64},{129,65},{130,66},{131,67},{132,68},{133,69},{134,70},{13... | collective-permute-start | bytes 393224 | tf_op jit(solution)/shard_map/ppermute | solution.py:41
  118.7 1.3 collective-permute-start.47
  125.7 115.0 %copy-start.33 = (f32[1,512]{1,0:T(1,128)S(1)}, f32[1,512]{1,0:T(1,128)}, u32[]{:S(2)}) copy-start(f32[1,512]{1,0:T(1,128)} %maximum_convert_fusion.4) | copy-start | bytes 6148
  125.7 22.5 %copy-start.11 = (bf16[256,1024]{1,0:T(8,128)(2,1)}, bf16[256,1024]{1,0:T(8,128)(2,1)S(1)}, u32[]{:S(2)}) copy-start(bf16[256,1024]{1,0:T(8,128)(2,1)S(1)} %get-tuple-element.153) | copy-start | bytes 1572868
  125.8 5.0 %collective-permute-start.19 = (bf16[32,1024]{1,0:T(8,128)(2,1)S(1)}, bf16[32,1024]{1,0:T(8,128)(2,1)S(1)}, u32[]{:S(2)}, u32[]{:S(2)}) collective-permute-start(bf16[32,1024]{1,0:T(8,128)(2,1)S(1)} %slice.605), channel_id=1, source_target_pairs={{64,65},{65,64},{66,67},{67,66},{68,69},{69,68},{70,71},{71,70},{7... | collective-permute-start | bytes 196616 | tf_op jit(solution)/shard_map/cond/branch_0_fun/ppermute | solution.py:41
  130.8 5.6 %collective-permute-start.20 = (bf16[32,512]{1,0:T(8,128)(2,1)S(1)}, bf16[32,512]{1,0:T(8,128)(2,1)S(1)}, u32[]{:S(2)}, u32[]{:S(2)}) collective-permute-start(bf16[32,512]{1,0:T(8,128)(2,1)S(1)} %slice.606), channel_id=1, source_target_pairs={{64,66},{65,67},{66,64},{67,65},{68,70},{69,71},{70,68},{71,69},{7... | collective-permute-start | bytes 98312 | tf_op jit(solution)/shard_map/cond/branch_0_fun/ppermute | solution.py:41
  136.4 11.1 %collective-permute-start.21 = (bf16[32,512]{1,0:T(8,128)(2,1)S(1)}, bf16[32,512]{1,0:T(8,128)(2,1)S(1)}, u32[]{:S(2)}, u32[]{:S(2)}) collective-permute-start(bf16[32,512]{1,0:T(8,128)(2,1)S(1)} %fusion.99), channel_id=1, source_target_pairs={{64,72},{65,73},{66,74},{67,75},{68,76},{69,77},{70,78},{71,79},{8... | collective-permute-start | bytes 98312 | tf_op jit(solution)/shard_map/cond/branch_0_fun/ppermute | solution.py:41
  147.5 3.3 %collective-permute-start.22 = (bf16[32,512]{1,0:T(8,128)(2,1)S(1)}, bf16[32,512]{1,0:T(8,128)(2,1)S(1)}, u32[]{:S(2)}, u32[]{:S(2)}) collective-permute-start(bf16[32,512]{1,0:T(8,128)(2,1)S(1)} %add_convert_fusion), channel_id=1, source_target_pairs={{72,74},{73,75},{74,72},{75,73},{76,78},{77,79},{78,76},{79,77},{8... | collective-permute-start | bytes 98312 | tf_op jit(solution)/shard_map/cond/branch_0_fun/ppermute | solution.py:41
  148.2 3.3 %copy-start.16 = (bf16[256,512]{1,0:T(8,128)(2,1)S(1)}, bf16[256,512]{1,0:T(8,128)(2,1)}, u32[]{:S(2)}) copy-start(bf16[256,512]{1,0:T(8,128)(2,1)} %get-tuple-element.161) | copy-start | bytes 786436
  150.8 1.9 collective-permute-start.23
  151.5 13.6 %copy-start.3 = (bf16[2048,512]{1,0:T(8,128)(2,1)S(1)}, bf16[2048,512]{1,0:T(8,128)(2,1)}, u32[]{:S(2)}) copy-start(bf16[2048,512]{1,0:T(8,128)(2,1)} %get-tuple-element.171) | copy-start | bytes 6291460
  151.5 13.6 %copy-start.12 = (bf16[256,1024]{1,0:T(8,128)(2,1)S(1)}, bf16[256,1024]{1,0:T(8,128)(2,1)}, u32[]{:S(2)}) copy-start(bf16[256,1024]{1,0:T(8,128)(2,1)} %copy-done.11) | copy-start | bytes 1572868
  152.7 11.4 %collective-permute-start.27 = (bf16[256,1024]{1,0:T(8,128)(2,1)S(1)}, bf16[256,1024]{1,0:T(8,128)(2,1)S(1)}, u32[]{:S(2)}, u32[]{:S(2)}) collective-permute-start(bf16[256,1024]{1,0:T(8,128)(2,1)S(1)} %pad_maximum_fusion.3), channel_id=1, source_target_pairs={{0,1},{1,0},{2,3},{3,2},{4,5},{5,4},{6,7},{7,6},{8,9},{9,8},{10,11... | collective-permute-start | bytes 1572872 | tf_op jit(solution)/shard_map/cond/branch_0_fun/ppermute | solution.py:41
  156.8 2.3 collective-permute-start.26
  157.5 1.6 collective-permute-start.25
  158.2 1.0 collective-permute-start.24
  164.2 34.5 %collective-permute-start.28 = (bf16[128,2048]{1,0:T(8,128)(2,1)S(1)}, bf16[128,2048]{1,0:T(8,128)(2,1)S(1)}, u32[]{:S(2)}, u32[]{:S(2)}) collective-permute-start(bf16[128,2048]{1,0:T(8,128)(2,1)S(1)} %pad_maximum_fusion.4), channel_id=1, source_target_pairs={{72,76},{73,77},{74,78},{75,79},{76,72},{77,73},{78,74},{79,75},{8... | collective-permute-start | bytes 1572872 | tf_op jit(solution)/shard_map/cond/branch_0_fun/ppermute | solution.py:41
  166.9 39.9 %collective-permute-start.29 = (bf16[256,512]{1,0:T(8,128)(2,1)}, bf16[256,512]{1,0:T(8,128)(2,1)S(1)}, u32[]{:S(2)}, u32[]{:S(2)}) collective-permute-start(bf16[256,512]{1,0:T(8,128)(2,1)} %get-tuple-element.172), channel_id=1, source_target_pairs={{0,4},{1,5},{2,6},{3,7},{4,8},{5,9},{6,10},{7,11},{8,12},{9,13},{1... | collective-permute-start | bytes 786440 | tf_op jit(solution)/shard_map/cond/branch_0_fun/ppermute | solution.py:41
  198.8 1.6 copy-start.6
  208.4 13.7 %collective-permute-start.30 = (bf16[257,1024]{1,0:T(8,128)(2,1)S(1)}, bf16[257,1024]{1,0:T(8,128)(2,1)S(1)}, u32[]{:S(2)}, u32[]{:S(2)}) collective-permute-start(bf16[257,1024]{1,0:T(8,128)(2,1)S(1)} %fusion.70), channel_id=1, source_target_pairs={{0,1},{1,0},{2,3},{3,2},{4,5},{5,4},{6,7},{7,6},{8,9},{9,8},{10,11... | collective-permute-start | bytes 1579016 | tf_op jit(solution)/shard_map/cond/branch_0_fun/ppermute | solution.py:41
  222.5 16.9 %collective-permute-start.31 = (bf16[257,512]{1,0:T(8,128)(2,1)S(1)}, bf16[257,512]{1,0:T(8,128)(2,1)S(1)}, u32[]{:S(2)}, u32[]{:S(2)}) collective-permute-start(bf16[257,512]{1,0:T(8,128)(2,1)S(1)} %pad_maximum_fusion.5), channel_id=1, source_target_pairs={{0,2},{1,3},{2,0},{3,1},{4,6},{5,7},{6,4},{7,5},{8,10},{9,11},{10,... | collective-permute-start | bytes 789512 | tf_op jit(solution)/shard_map/cond/branch_0_fun/ppermute | solution.py:41
  239.9 3.5 %copy-start.1 = (bf16[256,512]{1,0:T(8,128)(2,1)S(1)}, bf16[256,512]{1,0:T(8,128)(2,1)}, u32[]{:S(2)}) copy-start(bf16[256,512]{1,0:T(8,128)(2,1)} %param.15) | copy-start | bytes 786436
  239.9 2.7 %collective-permute-start.51 = (bf16[256,512]{1,0:T(8,128)(2,1)S(1)}, bf16[256,512]{1,0:T(8,128)(2,1)S(1)}, u32[]{:S(2)}, u32[]{:S(2)}) collective-permute-start(bf16[256,512]{1,0:T(8,128)(2,1)S(1)} %get-tuple-element.218), channel_id=1, source_target_pairs={{128,132},{129,133},{130,134},{131,135},{132,136},{133,137},{134,1... | collective-permute-start | bytes 786440 | tf_op jit(solution)/shard_map/ppermute | solution.py:41
where the time goes:
time: 245 us; the launch traced here: 243 us
  waiting for transfers between devices  90.8 us (37%)
  starting transfers between devices  90 us (37%)
  other arithmetic  23.3 us (10%)
  matrix products  19.3 us (8%)
  local copies, waits for them, and re-layouts  17.9 us (7%)
    ppermute x31, waiting for transfers between devices, move(): return lax.ppermute(value, ('section', 'tensor'), pairs)  90.8 us
    ppermute x31, starting transfers between devices, move(): return lax.ppermute(value, ('section', 'tensor'), pairs)  90 us
    dot_general x11, matrix products, mm(): return jnp.dot(a, b, preferred_element_type=f32)  12.4 us
    dot_general x10, matrix products, mm_t(): lax.dot_general(a, b, (((1,), (1,)), ((), ())), preferred_element_type=f32)  6.14 us
  transfers between devices with their start and end apart: 31, of which 13 were waited for; matrix products, arithmetic and copies ran while one was open for 18% of the time, Pallas kernels for 0%

commit v1 on v0

--- a/solution.py
+++ b/solution.py
@@ -81,30 +81,39 @@
     return lax.optimization_barrier((value, other))
 
 
-def line_scatter(total, row_part, who):
-    rows, width = total.shape[0], total.shape[1] // NT
-    give = total[:, 2 * width :]
+def high_low(row_part, columns):
+    high = row_part.astype(bf16)
+    both = jnp.concatenate([high, (row_part - high.astype(f32)).astype(bf16)])
+    spare = -both.shape[0] % columns
+    return jnp.pad(both, (0, spare)).reshape(-1, columns)
+
+
+def scatter_near(total, row_part, who):
+    rows, half = total.shape[0], total.shape[1] // 2
+    give = total[:, half:]
     if row_part is not None:
-        high = row_part.astype(bf16)
-        low = (row_part - high.astype(f32)).astype(bf16)
-        extra = jnp.concatenate([high, low]).reshape(1, 2 * rows)
-        extra = jnp.pad(extra, ((0, 0), (0, 2 * width - 2 * rows))) if 2 * rows < 2 * width else extra
-        give = jnp.concatenate([give, extra], axis=0)
+        give = jnp.concatenate([give, high_low(row_part, half)], axis=0)
     got = swap_t(give, 1, who).astype(f32)
-    pair = total[:, : 2 * width].astype(f32) + got[:rows]
+    pair = total[:, :half].astype(f32) + got[:rows]
+    if row_part is None:
+        return pair, None
+    tail = got[rows:].reshape(-1)
+    return pair, row_part + tail[:rows] + tail[rows : 2 * rows]
+
+
+def scatter_far(pair, sums, who, beside=None):
+    rows, width = pair.shape[0], pair.shape[1] // 2
     give = pair[:, width:].astype(bf16)
-    if row_part is not None:
-        sums = row_part + got[rows, :rows] + got[rows, rows : 2 * rows]
-        high = sums.astype(bf16)
-        low = (sums - high.astype(f32)).astype(bf16)
-        extra = jnp.concatenate([high, low]).reshape(2 * rows // width, width)
-        give = jnp.concatenate([give, extra], axis=0)
+    if sums is not None:
+        give = jnp.concatenate([give, high_low(sums, width)], axis=0)
+    if beside is not None:
+        give, beside = tie(give, beside)
     got = swap_t(give, 2, who).astype(f32)
     summed = pair[:, :width] + got[:rows]
-    if row_part is None:
-        return summed, None
-    tail = got[rows:].reshape(2 * rows)
-    return summed, (sums + tail[:rows] + tail[rows:]).reshape(rows, 1)
+    if sums is not None:
+        tail = got[rows:].reshape(-1)
+        sums = (sums + tail[:rows] + tail[rows : 2 * rows]).reshape(rows, 1)
+    return summed, sums, beside
 
 
 def inverse_rms(values):
@@ -218,7 +227,7 @@
         b_near = swap_t(b_pair, 1, encoders)
         out = attend_out(*project(a_normed, a_normed), w_o).astype(bf16)
         out, b_near = tie(out, b_near)
-        summed, _ = line_scatter(out, None, encoders)
+        summed, _, _ = scatter_far(*scatter_near(out, None, encoders), encoders)
         enc_y = (fwd_shard.astype(f32) + summed).astype(bf16)
         blocks = enc_y.reshape(NX, NC, part, width)
         passed, c_shard = tie(swap_core(blocks[:, 0], top_row), cot_shard)
@@ -226,8 +235,11 @@
         c_far = swap_t(c_shard, 2, encoders)
         top = blocks[NX - 1]
         for k in range(1, NX):
-            top = jnp.where(x_at ^ (NX - 1) == k, swap_x(blocks[(NX - 1) ^ k], k, top_row), top)
-        return enc_y, top, b_near, c_far, out, out[:part]
+            sent = move(
+                blocks[(NX - 1) ^ k], lambda y, x, z, c, tt: (y, x ^ k, z, c, tt) if top_row(y, z) and x == NX - 1 else None
+            )
+            top = jnp.where(x_at ^ (NX - 1) == k, sent, top)
+        return enc_y, top, b_near, c_far, out, out[:part, : 2 * width]
 
     def dec_phase1(_):
         b_near = swap_t(b_pair, 1, decoders)
@@ -248,7 +260,9 @@
         total = acc[:part]
         for k in range(1, NX):
             total = total + swap_x(acc16[k * part : (k + 1) * part], k, decoders).astype(f32)
-        total, c_near = tie(total.astype(bf16), c_near)
+        total, c_near = tie(total, c_near)
+        total = total[:, : 2 * width] + swap_t(total[:, 2 * width :].astype(bf16), 1, decoders).astype(f32)
+        total = total.astype(bf16)
         return fwd_shard, fwd_shard[:part], c_near, c_far, dn, total
 
     enc_y, top, near, c_far, dn, total = lax.cond(~dec, enc_phase1, dec_phase1, 0)
@@ -267,8 +281,7 @@
     def enc_phase2(_):
         b_full = jnp.concatenate([b_pair, near], axis=1)
         first_row = lambda y, z: y == 1
-        dc_sum = dc_from2.astype(f32) + dc_from3.astype(f32)
-        pair = dc_sum[:, : 2 * width] + swap_t(dc_sum[:, 2 * width :].astype(bf16), 1, first_row).astype(f32)
+        pair = dc_from2.astype(f32) + dc_from3.astype(f32)
         mine = pair[:, :width] + swap_t(pair[:, width:].astype(bf16), 2, first_row).astype(f32)
         mine16 = mine.astype(bf16)
         mine = mine + move(
@@ -278,13 +291,18 @@
         pair = jnp.concatenate([mine, swap_t(mine, 2, top_row)], axis=1)
         u = jnp.concatenate([pair, swap_t(pair, 1, top_row)], axis=1)
         c_pair = jnp.concatenate([cot_shard, c_far], axis=1)
-        c_pair, u = tie(c_pair, u)
+        c_pair, u, y_out = lax.optimization_barrier((c_pair, u, enc_y))
         c_near = swap_t(c_pair, 1, encoders)
         u = final * u.astype(f32)
         r = inverse_rms(saved)
         block = (r * u - saved * r**3 * jnp.mean(u * saved, axis=-1, keepdims=True)).astype(bf16)
-        slots = jnp.concatenate([block] + [swap_x(block, k, top_row) for k in range(1, NX)], axis=0)
-        slots, c_near, y_out = lax.optimization_barrier((slots, c_near, enc_y))
+        slots = [block]
+        for k in range(1, NX):
+            slots.append(
+                move(block, lambda y, x, z, c, tt: (y, NX - 1, z, c, tt) if top_row(y, z) and x ^ k == NX - 1 else None)
+            )
+        slots = jnp.concatenate(slots, axis=0)
+        slots, c_near = tie(slots, c_near)
         c_full = jnp.concatenate([c_pair, c_near], axis=1)
         swapped = swap_core(slots, top_row)
         pieces = []
@@ -301,7 +319,8 @@
         dq, dk, dv = attend_back(q, k, v, upstream, w_o)
         term = (mm_t(dq, w_q) + mm_t(dk, w_k) + mm_t(dv, w_v)).astype(bf16)
         term, sent = tie(term, sent)
-        summed, row_sum = line_scatter(term, jnp.sum(gain * term.astype(f32) * values, axis=-1), encoders)
+        near_half = scatter_near(term, jnp.sum(gain * term.astype(f32) * values, axis=-1), encoders)
+        summed, row_sum, _ = scatter_far(*near_half, encoders)
         return sent, summed, row_sum, inverse, upstream[:, :width]
 
     def dec_phase2(_):
@@ -310,13 +329,14 @@
         all_top = jnp.concatenate([all_top, swap_t(all_top, 1, decoders)], axis=1).astype(f32)
         row_part = jnp.sum(gain * dn.astype(f32) * a_values, axis=-1)
         dn_tied, all_top = tie(dn, all_top)
-        dn_sum, row_sum = line_scatter(dn_tied, row_part, decoders)
+        dn_pair, row_part = scatter_near(dn_tied, row_part, decoders)
         top_full = gather_rows(scale_rows(all_top, inverse_rms(all_top), final), decoders)
         values = c_full.astype(f32)
         normed = scale_rows(values, inverse_rms(values), gain)
         out = attend_out(*project(normed, top_full), w_o).astype(bf16)
-        out, dn_sum = tie(out, dn_sum)
-        summed, _ = line_scatter(out, None, decoders)
+        dn_sum, row_sum, out = scatter_far(dn_pair, row_part, decoders, out)
+        out_pair, _ = scatter_near(out, None, decoders)
+        summed, _, dn_sum = scatter_far(out_pair, None, decoders, dn_sum)
         dec_y = (fwd_shard.astype(f32) + summed).astype(bf16)
         return dec_y, dn_sum, row_sum, a_inverse, cot_shard
 

time: 245 us -> 235 us (0.959)
  the two profiles are of different devices: /device:TPU:11 before, /device:TPU:15 now
where the time goes in v1:
time: 235 us; the launch traced here: 233 us
  starting transfers between devices  85.7 us (36%)
  waiting for transfers between devices  84.8 us (36%)
  other arithmetic  23.1 us (10%)
  matrix products  19.3 us (8%)
  local copies, waits for them, and re-layouts  18.4 us (8%)
    ppermute x30, starting transfers between devices, move(): return lax.ppermute(value, ('section', 'tensor'), pairs)  85.7 us
    ppermute x30, waiting for transfers between devices, move(): return lax.ppermute(value, ('section', 'tensor'), pairs)  84.8 us
    dot_general x11, matrix products, mm(): return jnp.dot(a, b, preferred_element_type=f32)  12.5 us
    dot_general x10, matrix products, mm_t(): lax.dot_general(a, b, (((1,), (1,)), ((), ())), preferred_element_type=f32)  6.13 us
  transfers between devices with their start and end apart: 30, of which 12 were waited for; matrix products, arithmetic and copies ran while one was open for 19% of the time, Pallas kernels for 0%

profile of v1, /device:TPU:15, one launch (start us, length us, event | category | flops | bytes accessed | tf_op | source)
XLA Modules:
  0.0 233.2 jit_solution(1055330623601883644)
XLA Ops:
  1.6 1.9 bitcast_select_fusion
  3.5 1.4 pad_maximum_fusion.28
  4.9 3.0 %collective-permute-start.42 = (bf16[290,512]{1,0:T(8,128)(2,1)}, bf16[290,512]{1,0:T(8,128)(2,1)S(1)}, u32[]{:S(2)}, u32[]{:S(2)}) collective-permute-start(bf16[290,512]{1,0:T(8,128)(2,1)} %pad_maximum_fusion.28), channel_id=1, source_target_pairs={{0,2},{1,3},{2,0},{3,1},{4,6},{5,7},{6,4},{7,5},{8,10},{9,11},{10,... | collective-permute-start | bytes 890888 | tf_op jit(solution)/shard_map/ppermute | solution.py:41
  7.9 1.7 dynamic-slice_bitcast_fusion.7
  9.6 3.3 %dynamic-slice_bitcast_fusion.3 = (bf16[512,3,512]{2,0,1:T(8,128)(2,1)S(1)}, bf16[512,3,512]{2,0,1:T(8,128)(2,1)S(1)}, bf16[512,3,512]{2,0,1:T(8,128)(2,1)S(1)}, bf16[512,3,512]{2,0,1:T(8,128)(2,1)S(1)}) fusion(bf16[1,2048,3,512]{3,1,2,0:T(8,128)(2,1)} %param.18, s32[]{:T(128)S(6)} %select_n.96, s32[]{:T(128)S(6)} %select_n.97, s32[]{:T(128)S(6)} %select_n.99, ...), kind=kLoop, calls=%fused_computation.302 | loop fusion | bytes 12582928 | tf_op jit(solution)/shard_map/dynamic_slice | solution.py:216
  12.8 1.4 slice_bitcast_fusion.12
  14.2 1.8 slice_bitcast_fusion.10
  16.0 1.6 pad_maximum_fusion.19
  17.8 3.7 %collective-permute-done.42 = bf16[290,512]{1,0:T(8,128)(2,1)S(1)} collective-permute-done((bf16[290,512]{1,0:T(8,128)(2,1)}, bf16[290,512]{1,0:T(8,128)(2,1)S(1)}, u32[]{:S(2)}, u32[]{:S(2)}) %collective-permute-start.42) | collective-permute-done | bytes 296992 | tf_op jit(solution)/shard_map/ppermute | solution.py:41
  21.6 1.4 collective-permute-start.44
  23.9 3.0 %collective-permute-start.43 = (bf16[256,512]{1,0:T(8,128)(2,1)S(1)}, bf16[256,512]{1,0:T(8,128)(2,1)S(1)}, u32[]{:S(2)}, u32[]{:S(2)}) collective-permute-start(bf16[256,512]{1,0:T(8,128)(2,1)S(1)} %copy-done.29), channel_id=1, source_target_pairs={{0,2},{1,3},{2,0},{3,1},{4,6},{5,7},{6,4},{7,5},{8,10},{9,11},{10,... | collective-permute-start | bytes 786440 | tf_op jit(solution)/shard_map/ppermute | solution.py:41
  26.9 1.5 pad_maximum_fusion.17
  28.4 12.7 %collective-permute-done.43 = bf16[256,512]{1,0:T(8,128)(2,1)S(1)} collective-permute-done((bf16[256,512]{1,0:T(8,128)(2,1)S(1)}, bf16[256,512]{1,0:T(8,128)(2,1)S(1)}, u32[]{:S(2)}, u32[]{:S(2)}) %collective-permute-start.43) | collective-permute-done | bytes 262176 | tf_op jit(solution)/shard_map/ppermute | solution.py:41
  43.8 68.4 %conditional.3 = (bf16[256,512]{1,0:T(8,128)(2,1)}, bf16[32,512]{1,0:T(8,128)(2,1)S(1)}, bf16[256,1024]{1,0:T(8,128)(2,1)}, bf16[256,512]{1,0:T(8,128)(2,1)}, bf...) conditional(s32[]{:T(128)} %convert_element_type.341, (bf16[256,512]{1,0:T(8,128)(2,1)S(1)}, ...), branch_computations={%region_1.7_spmd, %region_7.10_spmd} | conditional | flops 4106386432 | bytes 57627664 | solution.py:268
  43.8 6.1 %collective-permute-start.12 = (bf16[256,1024]{1,0:T(8,128)(2,1)S(1)}, bf16[256,1024]{1,0:T(8,128)(2,1)}, u32[]{:S(2)}, u32[]{:S(2)}) collective-permute-start(bf16[256,1024]{1,0:T(8,128)(2,1)S(1)} %get-tuple-element.145), channel_id=1, source_target_pairs={{0,1},{1,0},{2,3},{3,2},{4,5},{5,4},{6,7},{7,6},{8,9},{9,8},{10,11... | collective-permute-start | bytes 1572872 | tf_op jit(solution)/shard_map/cond/branch_1_fun/ppermute | solution.py:41
  50.0 2.3 convolution_convert_fusion.14
  54.7 1.7 convolution_convert_fusion.11
  56.4 4.7 %collective-permute-done.12 = bf16[256,1024]{1,0:T(8,128)(2,1)} collective-permute-done((bf16[256,1024]{1,0:T(8,128)(2,1)S(1)}, bf16[256,1024]{1,0:T(8,128)(2,1)}, u32[]{:S(2)}, u32[]{:S(2)}) %collective-permute-start.12) | collective-permute-done | bytes 524320 | tf_op jit(solution)/shard_map/cond/branch_1_fun/ppermute | solution.py:41
  61.1 1.1 slice.265
  62.2 3.0 %collective-permute-start.13 = (bf16[256,1024]{1,0:T(8,128)(2,1)S(1)}, bf16[256,1024]{1,0:T(8,128)(2,1)S(1)}, u32[]{:S(2)}, u32[]{:S(2)}) collective-permute-start(bf16[256,1024]{1,0:T(8,128)(2,1)S(1)} %slice.265), channel_id=1, source_target_pairs={{0,1},{1,0},{2,3},{3,2},{4,5},{5,4},{6,7},{7,6},{8,9},{9,8},{10,11... | collective-permute-start | bytes 1572872 | tf_op jit(solution)/shard_map/cond/branch_1_fun/ppermute | solution.py:41
  65.3 10.6 %collective-permute-done.13 = bf16[256,1024]{1,0:T(8,128)(2,1)S(1)} collective-permute-done((bf16[256,1024]{1,0:T(8,128)(2,1)S(1)}, bf16[256,1024]{1,0:T(8,128)(2,1)S(1)}, u32[]{:S(2)}, u32[]{:S(2)}) %collective-permute-start.13) | collective-permute-done | bytes 524320 | tf_op jit(solution)/shard_map/cond/branch_1_fun/ppermute | solution.py:41
  75.9 1.2 convert_add_fusion.1
  77.2 2.2 collective-permute-start.14
  79.4 13.8 %collective-permute-done.14 = bf16[256,512]{1,0:T(8,128)(2,1)S(1)} collective-permute-done((bf16[256,512]{1,0:T(8,128)(2,1)S(1)}, bf16[256,512]{1,0:T(8,128)(2,1)S(1)}, u32[]{:S(2)}, u32[]{:S(2)}) %collective-permute-start.14) | collective-permute-done | bytes 262176 | tf_op jit(solution)/shard_map/cond/branch_1_fun/ppermute | solution.py:41
  93.2 0.8 fusion.44
  94.0 1.6 slice_bitcast_fusion
  95.6 1.3 collective-permute-start.15
  96.9 1.9 collective-permute-start.19
  98.8 0.9 fusion.48
  101.0 1.3 collective-permute-start.18
  102.3 1.2 collective-permute-start.17
  103.5 1.3 collective-permute-start.16
  104.8 0.8 slice.274
  105.6 0.8 fusion.59
  106.4 5.8 %collective-permute-done.19 = bf16[256,512]{1,0:T(8,128)(2,1)} collective-permute-done((bf16[256,512]{1,0:T(8,128)(2,1)}, bf16[256,512]{1,0:T(8,128)(2,1)}, u32[]{:S(2)}, u32[]{:S(2)}) %collective-permute-start.19) | collective-permute-done | bytes 262176 | tf_op jit(solution)/shard_map/cond/branch_1_fun/ppermute | solution.py:41
  112.2 0.8 collective-permute-start.50
  115.0 1.4 collective-permute-start.46
  116.5 1.6 fusion.138
  118.1 1.3 collective-permute-start.45
  120.6 2.2 collective-permute-done.46
  122.8 1.6 collective-permute-done.45
  124.4 105.6 %conditional.5 = (bf16[256,512]{1,0:T(8,128)(2,1)S(1)}, f32[256,512]{1,0:T(8,128)S(1)}, f32[256,1]{0,1:T(1,128)S(1)}, f32[256,1]{0,1:T(1,128)S(1)}, f32[256,512]{1,0:T(8,128)S(1)}) conditional(s32[]{:T(128)} %convert_element_type.340, (bf16[256,1024]{1,0:T(8,128)(2,1)S(1)}, bf16[256,1024]{1,0:T(8,128)(2,1)}, f32[1,2048]{1,0:T(1,128)S(1)}, ...), branch_computations={%region_10.19_spmd, %region_19.25_spmd} | conditional | flops 4127771648 | bytes 92367768
  124.4 2.4 %collective-permute-start.20 = (bf16[32,512]{1,0:T(8,128)(2,1)S(1)}, bf16[32,512]{1,0:T(8,128)(2,1)S(1)}, u32[]{:S(2)}, u32[]{:S(2)}) collective-permute-start(bf16[32,512]{1,0:T(8,128)(2,1)S(1)} %slice.629), channel_id=1, source_target_pairs={{64,66},{65,67},{66,64},{67,65},{68,70},{69,71},{70,68},{71,69},{7... | collective-permute-start | bytes 98312 | tf_op jit(solution)/shard_map/cond/branch_0_fun/ppermute | solution.py:41
  126.9 1.3 fusion.62
  128.2 2.3 collective-permute-done.20
  130.5 12.3 %collective-permute-start.21 = (bf16[32,512]{1,0:T(8,128)(2,1)S(1)}, bf16[32,512]{1,0:T(8,128)(2,1)S(1)}, u32[]{:S(2)}, u32[]{:S(2)}) collective-permute-start(bf16[32,512]{1,0:T(8,128)(2,1)S(1)} %fusion.96), channel_id=1, source_target_pairs={{64,72},{65,73},{66,74},{67,75},{68,76},{69,77},{70,78},{71,79},{8... | collective-permute-start | bytes 98312 | tf_op jit(solution)/shard_map/cond/branch_0_fun/ppermute | solution.py:41
  142.8 1.8 convolution_convert_fusion.19
  145.3 2.6 %convolution_convert_fusion.20 = bf16[256,512]{1,0:T(8,128)(2,1)S(1)} fusion(bf16[2048,512]{1,0:T(8,128)(2,1)} %get-tuple-element.156, f32[2048]{0:T(1024)S(1)} %bitcast.182, f32[256]{0:T(256)S(1)} %add_rsqrt_fusion.1, bf16[256,1024]{1,0:T(8,128)(2,1)} %get-tuple-element.154, bf16[256,1024]{1,0:T(8,128)(2,1)S(1)} %get-tuple-element.153), kind=kOutput, calls=%fused_computation.124 | convolution fusion | flops 540672000 | bytes 3417088 | tf_op jit(solution)/shard_map/cond/branch_0_fun/dot_general | solution.py:128
  148.6 1.1 pad_maximum_fusion.4
  149.8 2.2 collective-permute-start.27
  152.0 1.1 multiply_reduce_fusion.6
  153.1 1.1 subtract_convert_fusion
  156.6 3.7 %collective-permute-done.27 = bf16[256,1024]{1,0:T(8,128)(2,1)S(1)} collective-permute-done((bf16[256,1024]{1,0:T(8,128)(2,1)S(1)}, bf16[256,1024]{1,0:T(8,128)(2,1)S(1)}, u32[]{:S(2)}, u32[]{:S(2)}) %collective-permute-start.27) | collective-permute-done | bytes 524320 | tf_op jit(solution)/shard_map/cond/branch_0_fun/ppermute | solution.py:41
  161.2 1.8 convolution_convert_fusion.17
  163.0 26.5 %collective-permute-start.29 = (bf16[256,512]{1,0:T(8,128)(2,1)}, bf16[256,512]{1,0:T(8,128)(2,1)S(1)}, u32[]{:S(2)}, u32[]{:S(2)}) collective-permute-start(bf16[256,512]{1,0:T(8,128)(2,1)} %get-tuple-element.172), channel_id=1, source_target_pairs={{0,4},{1,5},{2,6},{3,7},{4,8},{5,9},{6,10},{7,11},{8,12},{9,13},{1... | collective-permute-start | bytes 786440 | tf_op jit(solution)/shard_map/cond/branch_0_fun/ppermute | solution.py:41
  190.1 1.1 copy-done.6
  193.8 2.3 fusion.68
  197.7 1.5 fusion.65
  199.3 2.6 %collective-permute-start.30 = (bf16[257,1024]{1,0:T(8,128)(2,1)S(1)}, bf16[257,1024]{1,0:T(8,128)(2,1)S(1)}, u32[]{:S(2)}, u32[]{:S(2)}) collective-permute-start(bf16[257,1024]{1,0:T(8,128)(2,1)S(1)} %pad_maximum_fusion.3), channel_id=1, source_target_pairs={{0,1},{1,0},{2,3},{3,2},{4,5},{5,4},{6,7},{7,6},{8,9},{9,8},{10,11... | collective-permute-start | bytes 1579016 | tf_op jit(solution)/shard_map/cond/branch_0_fun/ppermute | solution.py:41
  202.0 11.0 %collective-permute-done.30 = bf16[257,1024]{1,0:T(8,128)(2,1)S(1)} collective-permute-done((bf16[257,1024]{1,0:T(8,128)(2,1)S(1)}, bf16[257,1024]{1,0:T(8,128)(2,1)S(1)}, u32[]{:S(2)}, u32[]{:S(2)}) %collective-permute-start.30) | collective-permute-done | bytes 526368 | tf_op jit(solution)/shard_map/cond/branch_0_fun/ppermute | solution.py:41
  213.4 3.6 %collective-permute-start.31 = (bf16[257,512]{1,0:T(8,128)(2,1)S(1)}, bf16[257,512]{1,0:T(8,128)(2,1)S(1)}, u32[]{:S(2)}, u32[]{:S(2)}) collective-permute-start(bf16[257,512]{1,0:T(8,128)(2,1)S(1)} %pad_maximum_fusion.6), channel_id=1, source_target_pairs={{0,2},{1,3},{2,0},{3,1},{4,6},{5,7},{6,4},{7,5},{8,10},{9,11},{10,... | collective-permute-start | bytes 789512 | tf_op jit(solution)/shard_map/cond/branch_0_fun/ppermute | solution.py:41
  217.0 12.6 %collective-permute-done.31 = bf16[257,512]{1,0:T(8,128)(2,1)S(1)} collective-permute-done((bf16[257,512]{1,0:T(8,128)(2,1)S(1)}, bf16[257,512]{1,0:T(8,128)(2,1)S(1)}, u32[]{:S(2)}, u32[]{:S(2)}) %collective-permute-start.31) | collective-permute-done | bytes 263200 | tf_op jit(solution)/shard_map/cond/branch_0_fun/ppermute | solution.py:41
  230.1 0.8 collective-permute-start.51
  230.9 1.6 fusion.139
  (161 shorter events, 22.2 us)
Async XLA Ops:
  0.6 1.0 copy-start
  1.6 19.9 %copy-start.13 = (bf16[32,512]{1,0:T(8,128)(2,1)}, bf16[32,512]{1,0:T(8,128)(2,1)S(1)}, u32[]{:S(2)}) copy-start(bf16[32,512]{1,0:T(8,128)(2,1)S(1)} %constant_dynamic-slice_fusion) | copy-start | bytes 98308
  4.9 16.6 %collective-permute-start.42 = (bf16[290,512]{1,0:T(8,128)(2,1)}, bf16[290,512]{1,0:T(8,128)(2,1)S(1)}, u32[]{:S(2)}, u32[]{:S(2)}) collective-permute-start(bf16[290,512]{1,0:T(8,128)(2,1)} %pad_maximum_fusion.28), channel_id=1, source_target_pairs={{0,2},{1,3},{2,0},{3,1},{4,6},{5,7},{6,4},{7,5},{8,10},{9,11},{10,... | collective-permute-start | bytes 890888 | tf_op jit(solution)/shard_map/ppermute | solution.py:41
  16.0 1.6 copy-start.26
  16.0 1.6 copy-start.27
  17.6 3.9 %copy-start.31 = (bf16[1,512]{1,0:T(2,128)(2,1)S(1)}, bf16[1,512]{1,0:T(2,128)(2,1)}, u32[]{:S(2)}) copy-start(bf16[1,512]{1,0:T(2,128)(2,1)} %param.16) | copy-start | bytes 3076
  17.6 5.4 %copy-start.22 = (bf16[512,512]{1,0:T(8,128)(2,1)S(1)}, bf16[512,512]{1,0:T(8,128)(2,1)}, u32[]{:S(2)}) copy-start(bf16[512,512]{1,0:T(8,128)(2,1)} %get-tuple-element.297) | copy-start | bytes 1572868
  17.6 5.4 %copy-start.23 = (bf16[512,512]{1,0:T(8,128)(2,1)S(1)}, bf16[512,512]{1,0:T(8,128)(2,1)}, u32[]{:S(2)}) copy-start(bf16[512,512]{1,0:T(8,128)(2,1)} %get-tuple-element.313) | copy-start | bytes 1572868
  17.6 5.4 %copy-start.24 = (bf16[512,512]{1,0:T(8,128)(2,1)S(1)}, bf16[512,512]{1,0:T(8,128)(2,1)}, u32[]{:S(2)}) copy-start(bf16[512,512]{1,0:T(8,128)(2,1)} %get-tuple-element.303) | copy-start | bytes 1572868
  17.6 5.3 %copy-start.25 = (bf16[512,512]{1,0:T(8,128)(2,1)S(1)}, bf16[512,512]{1,0:T(8,128)(2,1)}, u32[]{:S(2)}) copy-start(bf16[512,512]{1,0:T(8,128)(2,1)} %get-tuple-element.310) | copy-start | bytes 1572868
  17.8 26.0 %copy-start.2 = (bf16[2048,512]{1,0:T(8,128)(2,1)}, bf16[2048,512]{1,0:T(8,128)(2,1)S(1)}, u32[]{:S(2)}) copy-start(bf16[2048,512]{1,0:T(8,128)(2,1)S(1)} %pad_maximum_fusion.20) | copy-start | bytes 6291460
  21.6 19.6 %collective-permute-start.44 = (bf16[290,1024]{1,0:T(8,128)(2,1)S(1)}, bf16[290,1024]{1,0:T(8,128)(2,1)S(1)}, u32[]{:S(2)}, u32[]{:S(2)}) collective-permute-start(bf16[290,1024]{1,0:T(8,128)(2,1)S(1)} %pad_maximum_fusion.26), channel_id=1, source_target_pairs={{0,1},{1,0},{2,3},{3,2},{4,5},{5,4},{6,7},{7,6},{8,9},{9,8},{10,11... | collective-permute-start | bytes 1781768 | tf_op jit(solution)/shard_map/ppermute | solution.py:41
  23.0 1.0 copy-start.29
  23.0 3.9 %copy-start.18 = (bf16[512,512]{1,0:T(8,128)(2,1)S(1)}, bf16[512,512]{1,0:T(8,128)(2,1)}, u32[]{:S(2)}) copy-start(bf16[512,512]{1,0:T(8,128)(2,1)} %get-tuple-element.298) | copy-start | bytes 1572868
  23.0 3.9 %copy-start.19 = (bf16[512,512]{1,0:T(8,128)(2,1)S(1)}, bf16[512,512]{1,0:T(8,128)(2,1)}, u32[]{:S(2)}) copy-start(bf16[512,512]{1,0:T(8,128)(2,1)} %get-tuple-element.312) | copy-start | bytes 1572868
  23.0 3.9 %copy-start.20 = (bf16[512,512]{1,0:T(8,128)(2,1)S(1)}, bf16[512,512]{1,0:T(8,128)(2,1)}, u32[]{:S(2)}) copy-start(bf16[512,512]{1,0:T(8,128)(2,1)} %get-tuple-element.304) | copy-start | bytes 1572868
  23.0 3.9 %copy-start.21 = (bf16[512,512]{1,0:T(8,128)(2,1)S(1)}, bf16[512,512]{1,0:T(8,128)(2,1)}, u32[]{:S(2)}) copy-start(bf16[512,512]{1,0:T(8,128)(2,1)} %get-tuple-element.309) | copy-start | bytes 1572868
  23.9 17.2 %collective-permute-start.43 = (bf16[256,512]{1,0:T(8,128)(2,1)S(1)}, bf16[256,512]{1,0:T(8,128)(2,1)S(1)}, u32[]{:S(2)}, u32[]{:S(2)}) collective-permute-start(bf16[256,512]{1,0:T(8,128)(2,1)S(1)} %copy-done.29), channel_id=1, source_target_pairs={{0,2},{1,3},{2,0},{3,1},{4,6},{5,7},{6,4},{7,5},{8,10},{9,11},{10,... | collective-permute-start | bytes 786440 | tf_op jit(solution)/shard_map/ppermute | solution.py:41
  26.9 14.3 %copy-start.14 = (bf16[32,512]{1,0:T(8,128)(2,1)S(1)}, bf16[32,512]{1,0:T(8,128)(2,1)}, u32[]{:S(2)}) copy-start(bf16[32,512]{1,0:T(8,128)(2,1)} %copy-done.13) | copy-start | bytes 98308
  41.2 2.6 %copy-start.9 = (bf16[256,1024]{1,0:T(8,128)(2,1)}, bf16[256,1024]{1,0:T(8,128)(2,1)S(1)}, u32[]{:S(2)}) copy-start(bf16[256,1024]{1,0:T(8,128)(2,1)S(1)} %pad_maximum_fusion.27) | copy-start | bytes 1572868
  41.5 0.6 copy-start.32
  42.1 1.7 copy-start.5
  42.1 1.7 copy-start.8
  43.8 17.3 %collective-permute-start.12 = (bf16[256,1024]{1,0:T(8,128)(2,1)S(1)}, bf16[256,1024]{1,0:T(8,128)(2,1)}, u32[]{:S(2)}, u32[]{:S(2)}) collective-permute-start(bf16[256,1024]{1,0:T(8,128)(2,1)S(1)} %get-tuple-element.145), channel_id=1, source_target_pairs={{0,1},{1,0},{2,3},{3,2},{4,5},{5,4},{6,7},{7,6},{8,9},{9,8},{10,11... | collective-permute-start | bytes 1572872 | tf_op jit(solution)/shard_map/cond/branch_1_fun/ppermute | solution.py:41
  62.2 13.7 %collective-permute-start.13 = (bf16[256,1024]{1,0:T(8,128)(2,1)S(1)}, bf16[256,1024]{1,0:T(8,128)(2,1)S(1)}, u32[]{:S(2)}, u32[]{:S(2)}) collective-permute-start(bf16[256,1024]{1,0:T(8,128)(2,1)S(1)} %slice.265), channel_id=1, source_target_pairs={{0,1},{1,0},{2,3},{3,2},{4,5},{5,4},{6,7},{7,6},{8,9},{9,8},{10,11... | collective-permute-start | bytes 1572872 | tf_op jit(solution)/shard_map/cond/branch_1_fun/ppermute | solution.py:41
  77.2 16.0 %collective-permute-start.14 = (bf16[256,512]{1,0:T(8,128)(2,1)S(1)}, bf16[256,512]{1,0:T(8,128)(2,1)S(1)}, u32[]{:S(2)}, u32[]{:S(2)}) collective-permute-start(bf16[256,512]{1,0:T(8,128)(2,1)S(1)} %slice.627), channel_id=1, source_target_pairs={{0,2},{1,3},{2,0},{3,1},{4,6},{5,7},{6,4},{7,5},{8,10},{9,11},{10,... | collective-permute-start | bytes 786440 | tf_op jit(solution)/shard_map/cond/branch_1_fun/ppermute | solution.py:41
  95.6 1.3 collective-permute-start.15
  96.9 15.3 %collective-permute-start.19 = (bf16[256,512]{1,0:T(8,128)(2,1)}, bf16[256,512]{1,0:T(8,128)(2,1)}, u32[]{:S(2)}, u32[]{:S(2)}) collective-permute-start(bf16[256,512]{1,0:T(8,128)(2,1)} %get-tuple-element.152), channel_id=1, source_target_pairs={{0,2},{1,3},{2,0},{3,1},{4,6},{5,7},{6,4},{7,5},{8,10},{9,11},{10,... | collective-permute-start | bytes 786440 | tf_op jit(solution)/shard_map/cond/branch_1_fun/ppermute | solution.py:41
  99.7 0.6 copy-start.30
  101.0 4.6 %collective-permute-start.18 = (bf16[32,512]{1,0:T(8,128)(2,1)}, bf16[32,512]{1,0:T(8,128)(2,1)}, u32[]{:S(2)}, u32[]{:S(2)}) collective-permute-start(bf16[32,512]{1,0:T(8,128)(2,1)} %get-tuple-element.253), channel_id=1, source_target_pairs={{120,104},{121,105},{122,106},{123,107},{124,108},{125,109},{126,1... | collective-permute-start | bytes 98312 | tf_op jit(solution)/shard_map/cond/branch_1_fun/ppermute | solution.py:41
  102.3 3.4 %collective-permute-start.17 = (bf16[32,512]{1,0:T(8,128)(2,1)}, bf16[32,512]{1,0:T(8,128)(2,1)}, u32[]{:S(2)}, u32[]{:S(2)}) collective-permute-start(bf16[32,512]{1,0:T(8,128)(2,1)} %get-tuple-element.254), channel_id=1, source_target_pairs={{120,88},{121,89},{122,90},{123,91},{124,92},{125,93},{126,94},{12... | collective-permute-start | bytes 98312 | tf_op jit(solution)/shard_map/cond/branch_1_fun/ppermute | solution.py:41
  103.5 2.1 collective-permute-start.16
  112.2 7.2 %copy-start.15 = (bf16[32,512]{1,0:T(8,128)(2,1)S(1)}, bf16[32,512]{1,0:T(8,128)(2,1)}, u32[]{:S(2)}) copy-start(bf16[32,512]{1,0:T(8,128)(2,1)} %copy-done.13) | copy-start | bytes 98308
  112.2 5.9 %collective-permute-start.50 = (bf16[32,512]{1,0:T(8,128)(2,1)S(1)}, bf16[32,512]{1,0:T(8,128)(2,1)S(1)}, u32[]{:S(2)}, u32[]{:S(2)}) collective-permute-start(bf16[32,512]{1,0:T(8,128)(2,1)S(1)} %get-tuple-element.218), channel_id=1, source_target_pairs={{72,200},{73,201},{74,202},{75,203},{76,204},{77,205},{78,206},{79... | collective-permute-start | bytes 98312 | tf_op jit(solution)/shard_map/ppermute | solution.py:41
  113.0 7.0 %collective-permute-start.49 = (bf16[32,512]{1,0:T(8,128)(2,1)S(1)}, bf16[32,512]{1,0:T(8,128)(2,1)S(1)}, u32[]{:S(2)}, u32[]{:S(2)}) collective-permute-start(bf16[32,512]{1,0:T(8,128)(2,1)S(1)} %get-tuple-element.218), channel_id=1, source_target_pairs={{72,192},{73,193},{74,194},{75,195},{76,196},{77,197},{78,198},{79... | collective-permute-start | bytes 98312 | tf_op jit(solution)/shard_map/ppermute | solution.py:41
  113.7 6.3 %collective-permute-start.48 = (bf16[32,512]{1,0:T(8,128)(2,1)S(1)}, bf16[32,512]{1,0:T(8,128)(2,1)S(1)}, u32[]{:S(2)}, u32[]{:S(2)}) collective-permute-start(bf16[32,512]{1,0:T(8,128)(2,1)S(1)} %get-tuple-element.218), channel_id=1, source_target_pairs={{72,136},{73,137},{74,138},{75,139},{76,140},{77,141},{78,142},{79... | collective-permute-start | bytes 98312 | tf_op jit(solution)/shard_map/ppermute | solution.py:41
  114.3 5.6 %collective-permute-start.47 = (bf16[32,512]{1,0:T(8,128)(2,1)S(1)}, bf16[32,512]{1,0:T(8,128)(2,1)S(1)}, u32[]{:S(2)}, u32[]{:S(2)}) collective-permute-start(bf16[32,512]{1,0:T(8,128)(2,1)S(1)} %get-tuple-element.218), channel_id=1, source_target_pairs={{72,128},{73,129},{74,130},{75,131},{76,132},{77,133},{78,134},{79... | collective-permute-start | bytes 98312 | tf_op jit(solution)/shard_map/ppermute | solution.py:41
  115.0 9.4 %copy-start.10 = (bf16[256,1024]{1,0:T(8,128)(2,1)S(1)}, bf16[256,1024]{1,0:T(8,128)(2,1)}, u32[]{:S(2)}) copy-start(bf16[256,1024]{1,0:T(8,128)(2,1)} %copy-done.9) | copy-start | bytes 1572868
  115.0 7.8 %collective-permute-start.46 = (bf16[32,1024]{1,0:T(8,128)(2,1)S(1)}, bf16[32,1024]{1,0:T(8,128)(2,1)S(1)}, u32[]{:S(2)}, u32[]{:S(2)}) collective-permute-start(bf16[32,1024]{1,0:T(8,128)(2,1)S(1)} %get-tuple-element.216), channel_id=1, source_target_pairs={{192,64},{193,65},{194,66},{195,67},{196,68},{197,69},{198,70},{19... | collective-permute-start | bytes 196616 | tf_op jit(solution)/shard_map/ppermute | solution.py:41
  118.1 6.3 %collective-permute-start.45 = (bf16[32,1024]{1,0:T(8,128)(2,1)S(1)}, bf16[32,1024]{1,0:T(8,128)(2,1)S(1)}, u32[]{:S(2)}, u32[]{:S(2)}) collective-permute-start(bf16[32,1024]{1,0:T(8,128)(2,1)S(1)} %get-tuple-element.216), channel_id=1, source_target_pairs={{128,64},{129,65},{130,66},{131,67},{132,68},{133,69},{134,70},{13... | collective-permute-start | bytes 196616 | tf_op jit(solution)/shard_map/ppermute | solution.py:41
  124.4 106.5 %copy-start.28 = (bf16[1,256,512]{2,1,0:T(8,128)(2,1)S(1)}, bf16[1,256,512]{2,1,0:T(8,128)(2,1)}, u32[]{:S(2)}) copy-start(bf16[1,256,512]{2,1,0:T(8,128)(2,1)} %param.13) | copy-start | bytes 786436
  124.4 20.9 %copy-start.11 = (bf16[256,1024]{1,0:T(8,128)(2,1)}, bf16[256,1024]{1,0:T(8,128)(2,1)S(1)}, u32[]{:S(2)}) copy-start(bf16[256,1024]{1,0:T(8,128)(2,1)S(1)} %get-tuple-element.153) | copy-start | bytes 1572868
  124.4 6.0 %collective-permute-start.20 = (bf16[32,512]{1,0:T(8,128)(2,1)S(1)}, bf16[32,512]{1,0:T(8,128)(2,1)S(1)}, u32[]{:S(2)}, u32[]{:S(2)}) collective-permute-start(bf16[32,512]{1,0:T(8,128)(2,1)S(1)} %slice.629), channel_id=1, source_target_pairs={{64,66},{65,67},{66,64},{67,65},{68,70},{69,71},{70,68},{71,69},{7... | collective-permute-start | bytes 98312 | tf_op jit(solution)/shard_map/cond/branch_0_fun/ppermute | solution.py:41
  130.5 14.1 %collective-permute-start.21 = (bf16[32,512]{1,0:T(8,128)(2,1)S(1)}, bf16[32,512]{1,0:T(8,128)(2,1)S(1)}, u32[]{:S(2)}, u32[]{:S(2)}) collective-permute-start(bf16[32,512]{1,0:T(8,128)(2,1)S(1)} %fusion.96), channel_id=1, source_target_pairs={{64,72},{65,73},{66,74},{67,75},{68,76},{69,77},{70,78},{71,79},{8... | collective-permute-start | bytes 98312 | tf_op jit(solution)/shard_map/cond/branch_0_fun/ppermute | solution.py:41
  144.6 3.3 %collective-permute-start.22 = (bf16[32,512]{1,0:T(8,128)(2,1)S(1)}, bf16[32,512]{1,0:T(8,128)(2,1)S(1)}, u32[]{:S(2)}, u32[]{:S(2)}) collective-permute-start(bf16[32,512]{1,0:T(8,128)(2,1)S(1)} %add_convert_fusion.1), channel_id=1, source_target_pairs={{72,74},{73,75},{74,72},{75,73},{76,78},{77,79},{78,76},{79,77},{8... | collective-permute-start | bytes 98312 | tf_op jit(solution)/shard_map/cond/branch_0_fun/ppermute | solution.py:41
  145.3 3.3 %copy-start.16 = (bf16[256,512]{1,0:T(8,128)(2,1)S(1)}, bf16[256,512]{1,0:T(8,128)(2,1)}, u32[]{:S(2)}) copy-start(bf16[256,512]{1,0:T(8,128)(2,1)} %get-tuple-element.161) | copy-start | bytes 786436
  147.9 1.9 collective-permute-start.23
  148.6 12.6 %copy-start.3 = (bf16[2048,512]{1,0:T(8,128)(2,1)S(1)}, bf16[2048,512]{1,0:T(8,128)(2,1)}, u32[]{:S(2)}) copy-start(bf16[2048,512]{1,0:T(8,128)(2,1)} %get-tuple-element.171) | copy-start | bytes 6291460
  148.6 12.6 %copy-start.12 = (bf16[256,1024]{1,0:T(8,128)(2,1)S(1)}, bf16[256,1024]{1,0:T(8,128)(2,1)}, u32[]{:S(2)}) copy-start(bf16[256,1024]{1,0:T(8,128)(2,1)} %copy-done.11) | copy-start | bytes 1572868
  149.8 10.4 %collective-permute-start.27 = (bf16[256,1024]{1,0:T(8,128)(2,1)S(1)}, bf16[256,1024]{1,0:T(8,128)(2,1)S(1)}, u32[]{:S(2)}, u32[]{:S(2)}) collective-permute-start(bf16[256,1024]{1,0:T(8,128)(2,1)S(1)} %pad_maximum_fusion.4), channel_id=1, source_target_pairs={{0,1},{1,0},{2,3},{3,2},{4,5},{5,4},{6,7},{7,6},{8,9},{9,8},{10,11... | collective-permute-start | bytes 1572872 | tf_op jit(solution)/shard_map/cond/branch_0_fun/ppermute | solution.py:41
  154.2 2.3 collective-permute-start.26
  154.9 1.6 collective-permute-start.25
  155.5 1.0 collective-permute-start.24
  160.2 29.3 %collective-permute-start.28 = (bf16[128,2048]{1,0:T(8,128)(2,1)S(1)}, bf16[128,2048]{1,0:T(8,128)(2,1)S(1)}, u32[]{:S(2)}, u32[]{:S(2)}) collective-permute-start(bf16[128,2048]{1,0:T(8,128)(2,1)S(1)} %pad_maximum_fusion.5), channel_id=1, source_target_pairs={{72,76},{73,77},{74,78},{75,79},{76,72},{77,73},{78,74},{79,75},{8... | collective-permute-start | bytes 1572872 | tf_op jit(solution)/shard_map/cond/branch_0_fun/ppermute | solution.py:41
  163.0 34.7 %collective-permute-start.29 = (bf16[256,512]{1,0:T(8,128)(2,1)}, bf16[256,512]{1,0:T(8,128)(2,1)S(1)}, u32[]{:S(2)}, u32[]{:S(2)}) collective-permute-start(bf16[256,512]{1,0:T(8,128)(2,1)} %get-tuple-element.172), channel_id=1, source_target_pairs={{0,4},{1,5},{2,6},{3,7},{4,8},{5,9},{6,10},{7,11},{8,12},{9,13},{1... | collective-permute-start | bytes 786440 | tf_op jit(solution)/shard_map/cond/branch_0_fun/ppermute | solution.py:41
  189.6 1.6 copy-start.6
  199.3 13.7 %collective-permute-start.30 = (bf16[257,1024]{1,0:T(8,128)(2,1)S(1)}, bf16[257,1024]{1,0:T(8,128)(2,1)S(1)}, u32[]{:S(2)}, u32[]{:S(2)}) collective-permute-start(bf16[257,1024]{1,0:T(8,128)(2,1)S(1)} %pad_maximum_fusion.3), channel_id=1, source_target_pairs={{0,1},{1,0},{2,3},{3,2},{4,5},{5,4},{6,7},{7,6},{8,9},{9,8},{10,11... | collective-permute-start | bytes 1579016 | tf_op jit(solution)/shard_map/cond/branch_0_fun/ppermute | solution.py:41
  213.4 16.2 %collective-permute-start.31 = (bf16[257,512]{1,0:T(8,128)(2,1)S(1)}, bf16[257,512]{1,0:T(8,128)(2,1)S(1)}, u32[]{:S(2)}, u32[]{:S(2)}) collective-permute-start(bf16[257,512]{1,0:T(8,128)(2,1)S(1)} %pad_maximum_fusion.6), channel_id=1, source_target_pairs={{0,2},{1,3},{2,0},{3,1},{4,6},{5,7},{6,4},{7,5},{8,10},{9,11},{10,... | collective-permute-start | bytes 789512 | tf_op jit(solution)/shard_map/cond/branch_0_fun/ppermute | solution.py:41
  230.0 3.2 %copy-start.1 = (bf16[256,512]{1,0:T(8,128)(2,1)S(1)}, bf16[256,512]{1,0:T(8,128)(2,1)}, u32[]{:S(2)}) copy-start(bf16[256,512]{1,0:T(8,128)(2,1)} %param.15) | copy-start | bytes 786436
  230.1 2.4 %collective-permute-start.51 = (bf16[256,512]{1,0:T(8,128)(2,1)S(1)}, bf16[256,512]{1,0:T(8,128)(2,1)S(1)}, u32[]{:S(2)}, u32[]{:S(2)}) collective-permute-start(bf16[256,512]{1,0:T(8,128)(2,1)S(1)} %get-tuple-element.220), channel_id=1, source_target_pairs={{128,132},{129,133},{130,134},{131,135},{132,136},{133,137},{134,1... | collective-permute-start | bytes 786440 | tf_op jit(solution)/shard_map/ppermute | solution.py:41

commit v2 on v1

--- a/solution.py
+++ b/solution.py
@@ -114,6 +114,29 @@
         tail = got[rows:].reshape(-1)
         sums = (sums + tail[:rows] + tail[rows : 2 * rows]).reshape(rows, 1)
     return summed, sums, beside
+
+
+def scatter(total, row_part, who, beside=None):
+    rows, width = total.shape[0], total.shape[1] // NT
+    give3 = total[:, 3 * width :]
+    if row_part is not None:
+        give3 = jnp.concatenate([give3, high_low(row_part, width)], axis=0)
+    give1, got3 = tie(total[:, 2 * width : 3 * width], swap_t(give3, 1, who))
+    got3 = got3.astype(f32)
+    give2 = (total[:, width : 2 * width].astype(f32) + got3[:rows]).astype(bf16)
+    if row_part is not None:
+        tail = got3[rows:].reshape(-1)
+        row_part = row_part + tail[:rows] + tail[rows : 2 * rows]
+        give2 = jnp.concatenate([give2, high_low(row_part, width)], axis=0)
+    if beside is not None:
+        give2, beside = tie(give2, beside)
+    got2 = swap_t(give2, 2, who).astype(f32)
+    got1 = swap_t(give1, 1, who).astype(f32)
+    summed = total[:, :width].astype(f32) + got1 + got2[:rows]
+    if row_part is not None:
+        tail = got2[rows:].reshape(-1)
+        row_part = (row_part + tail[:rows] + tail[rows : 2 * rows]).reshape(rows, 1)
+    return summed, row_part, beside
 
 
 def inverse_rms(values):
@@ -203,11 +226,14 @@
     )
     b_shard = jnp.where(dec, cot_shard, bwd_shard)
     a_far = swap_t(a_shard, 2, everyone)
-    a_pair = jnp.concatenate([a_shard, a_far], axis=1)
+    a_near = swap_t(a_shard, 1, everyone)
+    a_last = swap_t(a_far, 1, everyone)
     b_far = swap_t(after(b_shard, a_far), 2, everyone)
-    a_near = swap_t(a_pair, 1, everyone)
-    b_pair = jnp.concatenate([b_shard, b_far], axis=1)
-    a_all = jnp.concatenate([a_pair, a_near], axis=1)
+    b_own, a_near = tie(b_shard, a_near)
+    b_near = swap_t(b_own, 1, everyone)
+    a_all = jnp.concatenate([a_shard, a_far, a_near, a_last], axis=1)
+    b_three = jnp.concatenate([b_shard, b_far, b_near], axis=1)
+
     small = a_all[rows:].astype(f32)
     saved, gain, final = small[:part], small[part : part + 1], small[part + 1 :]
 
@@ -224,10 +250,10 @@
         return mm(normed, w_q).astype(bf16), mm(source, w_k).astype(bf16), mm(source, w_v).astype(bf16)
 
     def enc_phase1(_):
-        b_near = swap_t(b_pair, 1, encoders)
+        b_last = swap_t(b_far, 1, encoders)
         out = attend_out(*project(a_normed, a_normed), w_o).astype(bf16)
-        out, b_near = tie(out, b_near)
-        summed, _, _ = scatter_far(*scatter_near(out, None, encoders), encoders)
+        out, b_last = tie(out, b_last)
+        summed, _, _ = scatter(out, None, encoders)
         enc_y = (fwd_shard.astype(f32) + summed).astype(bf16)
         blocks = enc_y.reshape(NX, NC, part, width)
         passed, c_shard = tie(swap_core(blocks[:, 0], top_row), cot_shard)
@@ -239,19 +265,19 @@
                 blocks[(NX - 1) ^ k], lambda y, x, z, c, tt: (y, x ^ k, z, c, tt) if top_row(y, z) and x == NX - 1 else None
             )
             top = jnp.where(x_at ^ (NX - 1) == k, sent, top)
-        return enc_y, top, b_near, c_far, out, out[:part, : 2 * width]
+        return enc_y, top, jnp.concatenate([b_last, b_last], axis=1), c_far, out, out[:part, : 2 * width]
 
     def dec_phase1(_):
-        b_near = swap_t(b_pair, 1, decoders)
+        b_last = swap_t(b_far, 1, decoders)
         c_far = swap_t(fwd_shard, 2, decoders)
         q = mm(a_normed, w_q).astype(bf16)
         saved_rows, q = tie(scale_rows(saved, inverse_rms(saved), final), q)
         saved_half = jnp.concatenate([saved_rows] + [swap_x(saved_rows, k, decoders) for k in range(1, NX)], axis=0)
-        saved_half, b_near, c_far = lax.optimization_barrier((saved_half, b_near, c_far))
+        saved_half, b_last, c_far = lax.optimization_barrier((saved_half, b_last, c_far))
         saved_normed = jnp.concatenate([saved_half, swap_core(saved_half, decoders)], axis=0)
         k, v = mm(saved_normed, w_k).astype(bf16), mm(saved_normed, w_v).astype(bf16)
         c_near = swap_t(jnp.concatenate([fwd_shard, c_far], axis=1), 1, decoders)
-        b_full = jnp.concatenate([b_pair, b_near], axis=1)
+        b_full = jnp.concatenate([b_three, b_last], axis=1)
         dq, dk, dv = attend_back(q, k, v, b_full, w_o)
         dc = (mm_t(dk, w_k) + mm_t(dv, w_v)).astype(bf16)
         dn = mm_t(dq, w_q).astype(bf16)
@@ -279,7 +305,7 @@
     top = sum(arrivals)
 
     def enc_phase2(_):
-        b_full = jnp.concatenate([b_pair, near], axis=1)
+        b_full = jnp.concatenate([b_three, near[:, :width]], axis=1)
         first_row = lambda y, z: y == 1
         pair = dc_from2.astype(f32) + dc_from3.astype(f32)
         mine = pair[:, :width] + swap_t(pair[:, width:].astype(bf16), 2, first_row).astype(f32)
@@ -319,8 +345,7 @@
         dq, dk, dv = attend_back(q, k, v, upstream, w_o)
         term = (mm_t(dq, w_q) + mm_t(dk, w_k) + mm_t(dv, w_v)).astype(bf16)
         term, sent = tie(term, sent)
-        near_half = scatter_near(term, jnp.sum(gain * term.astype(f32) * values, axis=-1), encoders)
-        summed, row_sum, _ = scatter_far(*near_half, encoders)
+        summed, row_sum, _ = scatter(term, jnp.sum(gain * term.astype(f32) * values, axis=-1), encoders)
         return sent, summed, row_sum, inverse, upstream[:, :width]
 
     def dec_phase2(_):
@@ -335,8 +360,7 @@
         normed = scale_rows(values, inverse_rms(values), gain)
         out = attend_out(*project(normed, top_full), w_o).astype(bf16)
         dn_sum, row_sum, out = scatter_far(dn_pair, row_part, decoders, out)
-        out_pair, _ = scatter_near(out, None, decoders)
-        summed, _, dn_sum = scatter_far(out_pair, None, decoders, dn_sum)
+        summed, _, dn_sum = scatter(out, None, decoders, dn_sum)
         dec_y = (fwd_shard.astype(f32) + summed).astype(bf16)
         return dec_y, dn_sum, row_sum, a_inverse, cot_shard
 

time: 235 us -> 229 us (0.974)
  the two profiles are of different devices: /device:TPU:15 before, /device:TPU:24 now
where the time goes in v2:
time: 229 us; the launch traced here: 228 us
  starting transfers between devices  88.3 us (39%)
  waiting for transfers between devices  79 us (34%)
  other arithmetic  26.6 us (12%)
  matrix products  17.2 us (8%)
  local copies, waits for them, and re-layouts  14.4 us (6%)
    ppermute x35, starting transfers between devices, move(): return lax.ppermute(value, ('section', 'tensor'), pairs)  88.3 us
    ppermute x35, waiting for transfers between devices, move(): return lax.ppermute(value, ('section', 'tensor'), pairs)  79 us
    dot_general x11, matrix products, mm(): return jnp.dot(a, b, preferred_element_type=f32)  9.38 us
    dot_general x10, matrix products, mm_t(): lax.dot_general(a, b, (((1,), (1,)), ((), ())), preferred_element_type=f32)  7.06 us
    reduce_sum x4, other arithmetic, inverse_rms(): jnp.mean(values * values, axis=-1, keepdims=True) + epsilon  5.19 us
  transfers between devices with their start and end apart: 35, of which 18 were waited for; matrix products, arithmetic and copies ran while one was open for 14% of the time, Pallas kernels for 0%

profile of v2, /device:TPU:24, one launch (start us, length us, event | category | flops | bytes accessed | tf_op | source)
XLA Modules:
  0.0 227.8 jit_solution(2808270379103399029)
XLA Ops:
  2.8 1.5 pad_maximum_fusion.30
  4.2 1.9 collective-permute-start.46
  6.1 3.3 %collective-permute-start.45 = (bf16[290,512]{1,0:T(8,128)(2,1)}, bf16[290,512]{1,0:T(8,128)(2,1)}, u32[]{:S(2)}, u32[]{:S(2)}) collective-permute-start(bf16[290,512]{1,0:T(8,128)(2,1)} %pad_maximum_fusion.30), channel_id=1, source_target_pairs={{0,2},{1,3},{2,0},{3,1},{4,6},{5,7},{6,4},{7,5},{8,10},{9,11},{10,... | collective-permute-start | bytes 890888 | tf_op jit(solution)/shard_map/ppermute | solution.py:41
  9.4 3.2 %dynamic-slice_bitcast_fusion.3 = (bf16[512,3,512]{2,0,1:T(8,128)(2,1)S(1)}, bf16[512,3,512]{2,0,1:T(8,128)(2,1)S(1)}, bf16[512,3,512]{2,0,1:T(8,128)(2,1)S(1)}, bf16[512,3,512]{2,0,1:T(8,128)(2,1)S(1)}) fusion(bf16[1,2048,3,512]{3,1,2,0:T(8,128)(2,1)} %param.18, s32[]{:T(128)S(6)} %select_n.96, s32[]{:T(128)S(6)} %select_n.97, s32[]{:T(128)S(6)} %select_n.99, ...), kind=kLoop, calls=%fused_computation.294 | loop fusion | bytes 12582928 | tf_op jit(solution)/shard_map/dynamic_slice | solution.py:242
  13.2 1.5 pad_maximum_fusion.22
  14.8 1.4 copy-done.15
  16.5 1.5 pad_maximum_fusion.19
  18.0 1.8 collective-permute-done.46
  19.8 3.6 %collective-permute-done.45 = bf16[290,512]{1,0:T(8,128)(2,1)} collective-permute-done((bf16[290,512]{1,0:T(8,128)(2,1)}, bf16[290,512]{1,0:T(8,128)(2,1)}, u32[]{:S(2)}, u32[]{:S(2)}) %collective-permute-start.45) | collective-permute-done | bytes 296992 | tf_op jit(solution)/shard_map/ppermute | solution.py:41
  23.4 2.7 %collective-permute-start.49 = (bf16[256,512]{1,0:T(8,128)(2,1)S(1)}, bf16[256,512]{1,0:T(8,128)(2,1)}, u32[]{:S(2)}, u32[]{:S(2)}) collective-permute-start(bf16[256,512]{1,0:T(8,128)(2,1)S(1)} %get-tuple-element.226), channel_id=1, source_target_pairs={{0,1},{1,0},{2,3},{3,2},{4,5},{5,4},{6,7},{7,6},{8,9},{9,8},{10,11... | collective-permute-start | bytes 786440 | tf_op jit(solution)/shard_map/ppermute | solution.py:41
  26.1 1.7 pad_maximum_fusion.21
  27.8 6.7 %collective-permute-done.48 = bf16[256,512]{1,0:T(8,128)(2,1)} collective-permute-done((bf16[256,512]{1,0:T(8,128)(2,1)S(1)}, bf16[256,512]{1,0:T(8,128)(2,1)}, u32[]{:S(2)}, u32[]{:S(2)}) %collective-permute-start.48) | collective-permute-done | bytes 262176 | tf_op jit(solution)/shard_map/ppermute | solution.py:41
  34.5 2.0 collective-permute-done.49
  37.6 3.4 %collective-permute-done.47 = bf16[290,512]{1,0:T(8,128)(2,1)} collective-permute-done((bf16[290,512]{1,0:T(8,128)(2,1)}, bf16[290,512]{1,0:T(8,128)(2,1)}, u32[]{:S(2)}, u32[]{:S(2)}) %collective-permute-start.47) | collective-permute-done | bytes 296992 | tf_op jit(solution)/shard_map/ppermute | solution.py:41
  43.4 1.3 multiply_reduce_fusion.9
  45.3 1.3 multiply_convert_fusion.6
  46.7 71.0 %conditional.3 = (bf16[256,512]{1,0:T(8,128)(2,1)}, bf16[32,512]{1,0:T(8,128)(2,1)}, bf16[256,1024]{1,0:T(8,128)(2,1)}, bf16[256,512]{1,0:T(8,128)(2,1)}, bf16[2...) conditional(s32[]{:T(128)} %convert_element_type.364, (bf16[256,512]{1,0:T(8,128)(2,1)S(1)}, ...), branch_computations={%region_1.7_spmd, %region_7.10_spmd} | conditional | flops 4106386432 | bytes 56579088 | solution.py:294
  48.9 2.3 %convolution_convert_fusion.4 = bf16[256,512]{1,0:T(8,128)(2,1)S(1)} fusion(bf16[256,2048]{1,0:T(8,128)(2,1)S(1)} %get-tuple-element.128, bf16[2048,512]{1,0:T(8,128)(2,1)} %get-tuple-element.129), kind=kOutput, calls=%fused_computation.6 | convolution fusion | flops 537001984 | bytes 3407872 | tf_op jit(solution)/shard_map/cond/branch_0_fun/dot_general | solution.py:151
  51.2 3.4 %collective-permute-start = (bf16[32,2048]{1,0:T(8,128)(2,1)S(1)}, bf16[32,2048]{1,0:T(8,128)(2,1)S(1)}, u32[]{:S(2)}, u32[]{:S(2)}) collective-permute-start(bf16[32,2048]{1,0:T(8,128)(2,1)S(1)} %multiply_convert_fusion.2), channel_id=1, source_target_pairs={{128,144},{129,145},{130,146},{131,147},{132,148},{133,149},{134,1... | collective-permute-start | bytes 393224 | tf_op jit(solution)/shard_map/cond/branch_0_fun/ppermute | solution.py:41
  54.6 4.6 %collective-permute-start.1 = (bf16[32,2048]{1,0:T(8,128)(2,1)S(1)}, bf16[32,2048]{1,0:T(8,128)(2,1)S(1)}, u32[]{:S(2)}, u32[]{:S(2)}) collective-permute-start(bf16[32,2048]{1,0:T(8,128)(2,1)S(1)} %multiply_convert_fusion.2), channel_id=1, source_target_pairs={{128,160},{129,161},{130,162},{131,163},{132,164},{133,165},{134,1... | collective-permute-start | bytes 393224 | tf_op jit(solution)/shard_map/cond/branch_0_fun/ppermute | solution.py:41
  59.2 2.4 %collective-permute-start.2 = (bf16[32,2048]{1,0:T(8,128)(2,1)S(1)}, bf16[32,2048]{1,0:T(8,128)(2,1)S(1)}, u32[]{:S(2)}, u32[]{:S(2)}) collective-permute-start(bf16[32,2048]{1,0:T(8,128)(2,1)S(1)} %multiply_convert_fusion.2), channel_id=1, source_target_pairs={{128,176},{129,177},{130,178},{131,179},{132,180},{133,181},{134,1... | collective-permute-start | bytes 393224 | tf_op jit(solution)/shard_map/cond/branch_0_fun/ppermute | solution.py:41
  61.6 4.9 %collective-permute-start.4 = (bf16[256,512]{1,0:T(8,128)(2,1)S(1)}, bf16[256,512]{1,0:T(8,128)(2,1)}, u32[]{:S(2)}, u32[]{:S(2)}) collective-permute-start(bf16[256,512]{1,0:T(8,128)(2,1)S(1)} %get-tuple-element.334), channel_id=1, source_target_pairs={{128,130},{129,131},{130,128},{131,129},{132,134},{133,135},{134,1... | collective-permute-start | bytes 786440 | tf_op jit(solution)/shard_map/cond/branch_0_fun/ppermute | solution.py:41
  66.6 3.6 %collective-permute-start.3 = (bf16[256,512]{1,0:T(8,128)(2,1)}, bf16[256,512]{1,0:T(8,128)(2,1)S(1)}, u32[]{:S(2)}, u32[]{:S(2)}) collective-permute-start(bf16[256,512]{1,0:T(8,128)(2,1)} %get-tuple-element.132), channel_id=1, source_target_pairs={{128,129},{129,128},{130,131},{131,130},{132,133},{133,132},{134,1... | collective-permute-start | bytes 786440 | tf_op jit(solution)/shard_map/cond/branch_0_fun/ppermute | solution.py:41
  70.3 6.0 %collective-permute-done.4 = bf16[256,512]{1,0:T(8,128)(2,1)} collective-permute-done((bf16[256,512]{1,0:T(8,128)(2,1)S(1)}, bf16[256,512]{1,0:T(8,128)(2,1)}, u32[]{:S(2)}, u32[]{:S(2)}) %collective-permute-start.4) | collective-permute-done | bytes 262176 | tf_op jit(solution)/shard_map/cond/branch_0_fun/ppermute | solution.py:41
  76.2 2.3 %collective-permute-done.3 = bf16[256,512]{1,0:T(8,128)(2,1)S(1)} collective-permute-done((bf16[256,512]{1,0:T(8,128)(2,1)}, bf16[256,512]{1,0:T(8,128)(2,1)S(1)}, u32[]{:S(2)}, u32[]{:S(2)}) %collective-permute-start.3) | collective-permute-done | bytes 262176 | tf_op jit(solution)/shard_map/cond/branch_0_fun/ppermute | solution.py:41
  78.5 1.9 collective-permute-start.5
  87.2 2.0 collective-permute-start.6
  91.6 1.9 collective-permute-start.10
  94.0 2.2 collective-permute-start.7
  96.2 5.9 %collective-permute-start.8 = (bf16[32,2048]{1,0:T(8,128)(2,1)S(1)}, bf16[32,2048]{1,0:T(8,128)(2,1)S(1)}, u32[]{:S(2)}, u32[]{:S(2)}) collective-permute-start(bf16[32,2048]{1,0:T(8,128)(2,1)S(1)} %get-tuple-element.257), channel_id=1, source_target_pairs={{128,160},{129,161},{130,162},{131,163},{132,164},{133,165},{134,1... | collective-permute-start | bytes 393224 | tf_op jit(solution)/shard_map/cond/branch_0_fun/ppermute | solution.py:41
  102.1 2.4 %collective-permute-start.9 = (bf16[32,2048]{1,0:T(8,128)(2,1)S(1)}, bf16[32,2048]{1,0:T(8,128)(2,1)S(1)}, u32[]{:S(2)}, u32[]{:S(2)}) collective-permute-start(bf16[32,2048]{1,0:T(8,128)(2,1)S(1)} %get-tuple-element.256), channel_id=1, source_target_pairs={{128,176},{129,177},{130,178},{131,179},{132,180},{133,181},{134,1... | collective-permute-start | bytes 393224 | tf_op jit(solution)/shard_map/cond/branch_0_fun/ppermute | solution.py:41
  104.7 2.0 collective-permute-done.8
  106.7 3.7 %collective-permute-done.9 = bf16[32,2048]{1,0:T(8,128)(2,1)S(1)} collective-permute-done((bf16[32,2048]{1,0:T(8,128)(2,1)S(1)}, bf16[32,2048]{1,0:T(8,128)(2,1)S(1)}, u32[]{:S(2)}, u32[]{:S(2)}) %collective-permute-start.9) | collective-permute-done | bytes 131104 | tf_op jit(solution)/shard_map/cond/branch_0_fun/ppermute | solution.py:41
  110.5 3.7 %collective-permute-start.11 = (bf16[32,1024]{1,0:T(8,128)(2,1)S(1)}, bf16[32,1024]{1,0:T(8,128)(2,1)S(1)}, u32[]{:S(2)}, u32[]{:S(2)}) collective-permute-start(bf16[32,1024]{1,0:T(8,128)(2,1)S(1)} %slice.614), channel_id=1, source_target_pairs={{128,129},{129,128},{130,131},{131,130},{132,133},{133,132},{134,1... | collective-permute-start | bytes 196616 | tf_op jit(solution)/shard_map/cond/branch_0_fun/ppermute | solution.py:41
  114.2 3.3 %convolution_convert_fusion = bf16[256,2048]{1,0:T(8,128)(2,1)} fusion(bf16[2048,512]{1,0:T(8,128)(2,1)} %get-tuple-element.129, bf16[256,256]{1,0:T(8,128)(2,1)S(1)} %convolution_convert_fusion.5, bf16[256,256]{1,0:T(8,128)(2,1)S(1)} %convolution_convert_fusion.6), kind=kOutput, calls=%fused_computation.2 | convolution fusion | flops 537919488 | bytes 3407872 | tf_op jit(solution)/shard_map/cond/branch_0_fun/dot_general | solution.py:155
  117.7 1.3 collective-permute-start.52
  119.7 1.3 collective-permute-start.54
  122.3 1.3 collective-permute-start.51
  123.6 2.7 %fusion.132 = f32[256,2048]{1,0:T(8,128)} fusion(bf16[290,512]{1,0:T(8,128)(2,1)} %collective-permute-done.47, bf16[290,512]{1,0:T(8,128)(2,1)} %copy-done.9, bf16[290,512]{1,0:T(8,128)(2,1)} %collective-permute-done.45, bf16[1,512]{1,0:T(2,128)(2,1)S(1)} %broadcast_in_dim.6, bf16[1,512]{1,0:T(2,128)(2,1)} %param.16, ...), kind=kLoop, calls=%fused_computation.296 | loop fusion | flops 7340032 | bytes 3284992 | tf_op jit(solution)/shard_map/convert_element_type | solution.py:246
  126.4 1.3 slice.447
  127.7 4.9 %collective-permute-done.54 = bf16[32,512]{1,0:T(8,128)(2,1)S(1)} collective-permute-done((bf16[32,512]{1,0:T(8,128)(2,1)}, bf16[32,512]{1,0:T(8,128)(2,1)S(1)}, u32[]{:S(2)}, u32[]{:S(2)}) %collective-permute-start.54) | collective-permute-done | bytes 32800 | tf_op jit(solution)/shard_map/ppermute | solution.py:41
  133.1 76.3 %conditional.5 = (bf16[256,512]{1,0:T(8,128)(2,1)S(1)}, f32[256,512]{1,0:T(8,128)S(1)}, f32[256,1]{0,1:T(1,128)S(1)}, f32[256,1]{0,1:T(1,128)S(1)}, f32[256,512]{1,0:T(8,128)S(1)}) conditional(s32[]{:T(128)} %convert_element_type.363, (bf16[256,1024]{1,0:T(8,128)(2,1)}, bf16[256,1536]{1,0:T(8,128)(2,1)S(1)}, f32[1,2048]{1,0:T(1,128)S(1)}, ...), branch_computations={%region_10.19_spmd, %region_19.25_spmd} | conditional | flops 4127370752 | bytes 89471992
  133.9 3.6 %collective-permute-start.34 = (bf16[32,512]{1,0:T(8,128)(2,1)S(1)}, bf16[32,512]{1,0:T(8,128)(2,1)S(1)}, u32[]{:S(2)}, u32[]{:S(2)}) collective-permute-start(bf16[32,512]{1,0:T(8,128)(2,1)S(1)} %add_add_fusion.1), channel_id=1, source_target_pairs={{128,130},{129,131},{130,128},{131,129},{132,134},{133,135},{134,1... | collective-permute-start | bytes 98312 | tf_op jit(solution)/shard_map/cond/branch_1_fun/ppermute | solution.py:41
  137.5 2.7 %fusion.105 = (f32[256]{0:T(256)S(1)}, f32[256]{0:T(256)S(1)}) fusion(bf16[256,1024]{1,0:T(8,128)(2,1)} %get-tuple-element.192, bf16[256,512]{1,0:T(8,128)(2,1)} %get-tuple-element.191, bf16[256,512]{1,0:T(8,128)(2,1)S(1)} %get-tuple-element.182, f32[256,2048]{1,0:T(8,128)} %get-tuple-element.190, bf16[256,2048]{1,0:T(8,128)(2,1)} %get-tuple-element.188, ...), kind=kLoop, calls=%fused_computation.218 | loop fusion | flops 6290944 | bytes 4204544 | tf_op jit(solution)/shard_map/cond/branch_1_fun/reduce_sum | solution.py:143
  140.2 2.6 %convolution_convert_fusion.30 = bf16[256,512]{1,0:T(8,128)(2,1)S(1)} fusion(bf16[2048,512]{1,0:T(8,128)(2,1)} %get-tuple-element.193, f32[256]{0:T(256)S(1)} %add_rsqrt_fusion.4, f32[2048]{0:T(1024)S(1)} %bitcast.186, bf16[256,1024]{1,0:T(8,128)(2,1)} %get-tuple-element.192, bf16[256,512]{1,0:T(8,128)(2,1)} %get-tuple-element.191, ...), kind=kOutput, calls=%fused_computation.224 | convolution fusion | flops 541720576 | bytes 3417088 | tf_op jit(solution)/shard_map/cond/branch_1_fun/dot_general | solution.py:151
  142.8 3.0 %collective-permute-start.35 = (bf16[32,1024]{1,0:T(8,128)(2,1)S(1)}, bf16[32,1024]{1,0:T(8,128)(2,1)S(1)}, u32[]{:S(2)}, u32[]{:S(2)}) collective-permute-start(bf16[32,1024]{1,0:T(8,128)(2,1)S(1)} %pad_maximum_fusion.17), channel_id=1, source_target_pairs={{128,129},{129,128},{130,131},{131,130},{132,133},{133,132},{134,1... | collective-permute-start | bytes 196616 | tf_op jit(solution)/shard_map/cond/branch_1_fun/ppermute | solution.py:41
  145.8 3.1 %collective-permute-done.35 = bf16[32,1024]{1,0:T(8,128)(2,1)S(1)} collective-permute-done((bf16[32,1024]{1,0:T(8,128)(2,1)S(1)}, bf16[32,1024]{1,0:T(8,128)(2,1)S(1)}, u32[]{:S(2)}, u32[]{:S(2)}) %collective-permute-start.35) | collective-permute-done | bytes 65568 | tf_op jit(solution)/shard_map/cond/branch_1_fun/ppermute | solution.py:41
  149.2 1.9 collective-permute-start.37
  151.2 3.8 %collective-permute-start.38 = (bf16[32,2048]{1,0:T(8,128)(2,1)S(1)}, bf16[32,2048]{1,0:T(8,128)(2,1)S(1)}, u32[]{:S(2)}, u32[]{:S(2)}) collective-permute-start(bf16[32,2048]{1,0:T(8,128)(2,1)S(1)} %get-tuple-element.250), channel_id=1, source_target_pairs={{128,160},{129,161},{130,162},{131,163},{132,164},{133,165},{134,1... | collective-permute-start | bytes 393224 | tf_op jit(solution)/shard_map/cond/branch_1_fun/ppermute | solution.py:41
  155.0 4.7 %collective-permute-start.39 = (bf16[32,2048]{1,0:T(8,128)(2,1)S(1)}, bf16[32,2048]{1,0:T(8,128)(2,1)S(1)}, u32[]{:S(2)}, u32[]{:S(2)}) collective-permute-start(bf16[32,2048]{1,0:T(8,128)(2,1)S(1)} %get-tuple-element.250), channel_id=1, source_target_pairs={{128,176},{129,177},{130,178},{131,179},{132,180},{133,181},{134,1... | collective-permute-start | bytes 393224 | tf_op jit(solution)/shard_map/cond/branch_1_fun/ppermute | solution.py:41
  160.8 3.0 %collective-permute-start.36 = (bf16[257,1024]{1,0:T(8,128)(2,1)S(1)}, bf16[257,1024]{1,0:T(8,128)(2,1)S(1)}, u32[]{:S(2)}, u32[]{:S(2)}) collective-permute-start(bf16[257,1024]{1,0:T(8,128)(2,1)S(1)} %pad_maximum_fusion.13), channel_id=1, source_target_pairs={{128,129},{129,128},{130,131},{131,130},{132,133},{133,132},{134,1... | collective-permute-start | bytes 1579016 | tf_op jit(solution)/shard_map/cond/branch_1_fun/ppermute | solution.py:41
  163.9 2.2 collective-permute-start.40
  166.2 5.9 %collective-permute-done.36 = bf16[257,1024]{1,0:T(8,128)(2,1)S(1)} collective-permute-done((bf16[257,1024]{1,0:T(8,128)(2,1)S(1)}, bf16[257,1024]{1,0:T(8,128)(2,1)S(1)}, u32[]{:S(2)}, u32[]{:S(2)}) %collective-permute-start.36) | collective-permute-done | bytes 526368 | tf_op jit(solution)/shard_map/cond/branch_1_fun/ppermute | solution.py:41
  178.3 3.1 %collective-permute-start.41 = (bf16[256,512]{1,0:T(8,128)(2,1)S(1)}, bf16[256,512]{1,0:T(8,128)(2,1)S(1)}, u32[]{:S(2)}, u32[]{:S(2)}) collective-permute-start(bf16[256,512]{1,0:T(8,128)(2,1)S(1)} %get-tuple-element.292), channel_id=1, source_target_pairs={{128,129},{129,128},{130,131},{131,130},{132,133},{133,132},{134,1... | collective-permute-start | bytes 786440 | tf_op jit(solution)/shard_map/cond/branch_1_fun/ppermute | solution.py:41
  181.5 3.0 %collective-permute-start.43 = (bf16[257,512]{1,0:T(8,128)(2,1)S(1)}, bf16[257,512]{1,0:T(8,128)(2,1)S(1)}, u32[]{:S(2)}, u32[]{:S(2)}) collective-permute-start(bf16[257,512]{1,0:T(8,128)(2,1)S(1)} %pad_maximum_fusion.16), channel_id=1, source_target_pairs={{128,130},{129,131},{130,128},{131,129},{132,134},{133,135},{134,1... | collective-permute-start | bytes 789512 | tf_op jit(solution)/shard_map/cond/branch_1_fun/ppermute | solution.py:41
  184.5 9.1 %collective-permute-done.41 = bf16[256,512]{1,0:T(8,128)(2,1)S(1)} collective-permute-done((bf16[256,512]{1,0:T(8,128)(2,1)S(1)}, bf16[256,512]{1,0:T(8,128)(2,1)S(1)}, u32[]{:S(2)}, u32[]{:S(2)}) %collective-permute-start.41) | collective-permute-done | bytes 262176 | tf_op jit(solution)/shard_map/cond/branch_1_fun/ppermute | solution.py:41
  193.6 1.9 collective-permute-start.42
  195.6 1.3 collective-permute-done.43
  197.0 3.3 %collective-permute-start.44 = (bf16[256,512]{1,0:T(8,128)(2,1)S(1)}, bf16[256,512]{1,0:T(8,128)(2,1)S(1)}, u32[]{:S(2)}, u32[]{:S(2)}) collective-permute-start(bf16[256,512]{1,0:T(8,128)(2,1)S(1)} %add_convert_fusion.5), channel_id=1, source_target_pairs={{128,130},{129,131},{130,128},{131,129},{132,134},{133,135},{134,1... | collective-permute-start | bytes 786440 | tf_op jit(solution)/shard_map/cond/branch_1_fun/ppermute | solution.py:41
  200.5 1.6 collective-permute-done.42
  202.1 6.9 %collective-permute-done.44 = bf16[256,512]{1,0:T(8,128)(2,1)S(1)} collective-permute-done((bf16[256,512]{1,0:T(8,128)(2,1)S(1)}, bf16[256,512]{1,0:T(8,128)(2,1)S(1)}, u32[]{:S(2)}, u32[]{:S(2)}) %collective-permute-start.44) | collective-permute-done | bytes 262176 | tf_op jit(solution)/shard_map/cond/branch_1_fun/ppermute | solution.py:41
  209.5 2.1 collective-permute-start.56
  211.5 1.9 fusion.133
  213.4 13.6 %collective-permute-done.56 = bf16[256,512]{1,0:T(8,128)(2,1)S(1)} collective-permute-done((bf16[256,512]{1,0:T(8,128)(2,1)S(1)}, bf16[256,512]{1,0:T(8,128)(2,1)S(1)}, u32[]{:S(2)}, u32[]{:S(2)}) %collective-permute-start.56) | collective-permute-done | bytes 262176 | tf_op jit(solution)/shard_map/ppermute | solution.py:41
  (148 shorter events, 31.1 us)
Async XLA Ops:
  0.6 1.0 copy-start
  2.7 20.7 %copy-start.17 = (bf16[256,512]{1,0:T(8,128)(2,1)}, bf16[256,512]{1,0:T(8,128)(2,1)S(1)}, u32[]{:S(2)}) copy-start(bf16[256,512]{1,0:T(8,128)(2,1)S(1)} %get-tuple-element.226) | copy-start | bytes 786436
  4.2 15.5 %collective-permute-start.46 = (bf16[290,512]{1,0:T(8,128)(2,1)}, bf16[290,512]{1,0:T(8,128)(2,1)S(1)}, u32[]{:S(2)}, u32[]{:S(2)}) collective-permute-start(bf16[290,512]{1,0:T(8,128)(2,1)} %pad_maximum_fusion.30), channel_id=1, source_target_pairs={{0,1},{1,0},{2,3},{3,2},{4,5},{5,4},{6,7},{7,6},{8,9},{9,8},{10,11... | collective-permute-start | bytes 890888 | tf_op jit(solution)/shard_map/ppermute | solution.py:41
  6.1 17.3 %collective-permute-start.45 = (bf16[290,512]{1,0:T(8,128)(2,1)}, bf16[290,512]{1,0:T(8,128)(2,1)}, u32[]{:S(2)}, u32[]{:S(2)}) collective-permute-start(bf16[290,512]{1,0:T(8,128)(2,1)} %pad_maximum_fusion.30), channel_id=1, source_target_pairs={{0,2},{1,3},{2,0},{3,1},{4,6},{5,7},{6,4},{7,5},{8,10},{9,11},{10,... | collective-permute-start | bytes 890888 | tf_op jit(solution)/shard_map/ppermute | solution.py:41
  14.7 1.6 copy-start.15
  19.8 8.0 %copy-start.9 = (bf16[290,512]{1,0:T(8,128)(2,1)}, bf16[290,512]{1,0:T(8,128)(2,1)S(1)}, u32[]{:S(2)}) copy-start(bf16[290,512]{1,0:T(8,128)(2,1)S(1)} %collective-permute-done.46) | copy-start | bytes 890884
  23.4 11.1 %collective-permute-start.48 = (bf16[256,512]{1,0:T(8,128)(2,1)S(1)}, bf16[256,512]{1,0:T(8,128)(2,1)}, u32[]{:S(2)}, u32[]{:S(2)}) collective-permute-start(bf16[256,512]{1,0:T(8,128)(2,1)S(1)} %get-tuple-element.226), channel_id=1, source_target_pairs={{0,2},{1,3},{2,0},{3,1},{4,6},{5,7},{6,4},{7,5},{8,10},{9,11},{10,... | collective-permute-start | bytes 786440 | tf_op jit(solution)/shard_map/ppermute | solution.py:41
  23.4 13.1 %collective-permute-start.49 = (bf16[256,512]{1,0:T(8,128)(2,1)S(1)}, bf16[256,512]{1,0:T(8,128)(2,1)}, u32[]{:S(2)}, u32[]{:S(2)}) collective-permute-start(bf16[256,512]{1,0:T(8,128)(2,1)S(1)} %get-tuple-element.226), channel_id=1, source_target_pairs={{0,1},{1,0},{2,3},{3,2},{4,5},{5,4},{6,7},{7,6},{8,9},{9,8},{10,11... | collective-permute-start | bytes 786440 | tf_op jit(solution)/shard_map/ppermute | solution.py:41
  26.1 14.8 %collective-permute-start.47 = (bf16[290,512]{1,0:T(8,128)(2,1)}, bf16[290,512]{1,0:T(8,128)(2,1)}, u32[]{:S(2)}, u32[]{:S(2)}) collective-permute-start(bf16[290,512]{1,0:T(8,128)(2,1)} %collective-permute-done.45), channel_id=1, source_target_pairs={{0,1},{1,0},{2,3},{3,2},{4,5},{5,4},{6,7},{7,6},{8,9},{9,8},{10,11... | collective-permute-start | bytes 890888 | tf_op jit(solution)/shard_map/ppermute | solution.py:41
  26.1 10.4 %copy-start.18 = (bf16[256,512]{1,0:T(8,128)(2,1)S(1)}, bf16[256,512]{1,0:T(8,128)(2,1)}, u32[]{:S(2)}) copy-start(bf16[256,512]{1,0:T(8,128)(2,1)} %copy-done.17) | copy-start | bytes 786436
  26.1 14.8 %copy-start.23 = (bf16[1,512]{1,0:T(2,128)(2,1)S(1)}, bf16[1,512]{1,0:T(2,128)(2,1)}, u32[]{:S(2)}) copy-start(bf16[1,512]{1,0:T(2,128)(2,1)} %param.16) | copy-start | bytes 3076
  27.8 15.6 %copy-start.10 = (bf16[290,512]{1,0:T(8,128)(2,1)S(1)}, bf16[290,512]{1,0:T(8,128)(2,1)}, u32[]{:S(2)}) copy-start(bf16[290,512]{1,0:T(8,128)(2,1)} %copy-done.9) | copy-start | bytes 890884
  41.0 5.7 %copy-start.5 = (bf16[512,2048]{1,0:T(8,128)(2,1)S(1)}, bf16[512,2048]{1,0:T(8,128)(2,1)}, u32[]{:S(2)}) copy-start(bf16[512,2048]{1,0:T(8,128)(2,1)} %pad_maximum_fusion.21) | copy-start | bytes 6291460
  42.0 0.7 copy-start.16
  42.0 4.7 %copy-start.2 = (bf16[2048,512]{1,0:T(8,128)(2,1)S(1)}, bf16[2048,512]{1,0:T(8,128)(2,1)}, u32[]{:S(2)}) copy-start(bf16[2048,512]{1,0:T(8,128)(2,1)} %pad_maximum_fusion.22) | copy-start | bytes 6291460
  42.0 4.7 %copy-start.8 = (bf16[1,256,512]{2,1,0:T(8,128)(2,1)S(1)}, bf16[1,256,512]{2,1,0:T(8,128)(2,1)}, u32[]{:S(2)}) copy-start(bf16[1,256,512]{2,1,0:T(8,128)(2,1)} %param.12) | copy-start | bytes 786436
  44.7 0.6 copy-start.24
  51.2 19.0 %collective-permute-start = (bf16[32,2048]{1,0:T(8,128)(2,1)S(1)}, bf16[32,2048]{1,0:T(8,128)(2,1)S(1)}, u32[]{:S(2)}, u32[]{:S(2)}) collective-permute-start(bf16[32,2048]{1,0:T(8,128)(2,1)S(1)} %multiply_convert_fusion.2), channel_id=1, source_target_pairs={{128,144},{129,145},{130,146},{131,147},{132,148},{133,149},{134,1... | collective-permute-start | bytes 393224 | tf_op jit(solution)/shard_map/cond/branch_0_fun/ppermute | solution.py:41
  54.6 15.6 %collective-permute-start.1 = (bf16[32,2048]{1,0:T(8,128)(2,1)S(1)}, bf16[32,2048]{1,0:T(8,128)(2,1)S(1)}, u32[]{:S(2)}, u32[]{:S(2)}) collective-permute-start(bf16[32,2048]{1,0:T(8,128)(2,1)S(1)} %multiply_convert_fusion.2), channel_id=1, source_target_pairs={{128,160},{129,161},{130,162},{131,163},{132,164},{133,165},{134,1... | collective-permute-start | bytes 393224 | tf_op jit(solution)/shard_map/cond/branch_0_fun/ppermute | solution.py:41
  59.2 11.0 %collective-permute-start.2 = (bf16[32,2048]{1,0:T(8,128)(2,1)S(1)}, bf16[32,2048]{1,0:T(8,128)(2,1)S(1)}, u32[]{:S(2)}, u32[]{:S(2)}) collective-permute-start(bf16[32,2048]{1,0:T(8,128)(2,1)S(1)} %multiply_convert_fusion.2), channel_id=1, source_target_pairs={{128,176},{129,177},{130,178},{131,179},{132,180},{133,181},{134,1... | collective-permute-start | bytes 393224 | tf_op jit(solution)/shard_map/cond/branch_0_fun/ppermute | solution.py:41
  61.6 14.6 %collective-permute-start.4 = (bf16[256,512]{1,0:T(8,128)(2,1)S(1)}, bf16[256,512]{1,0:T(8,128)(2,1)}, u32[]{:S(2)}, u32[]{:S(2)}) collective-permute-start(bf16[256,512]{1,0:T(8,128)(2,1)S(1)} %get-tuple-element.334), channel_id=1, source_target_pairs={{128,130},{129,131},{130,128},{131,129},{132,134},{133,135},{134,1... | collective-permute-start | bytes 786440 | tf_op jit(solution)/shard_map/cond/branch_0_fun/ppermute | solution.py:41
  66.6 12.0 %collective-permute-start.3 = (bf16[256,512]{1,0:T(8,128)(2,1)}, bf16[256,512]{1,0:T(8,128)(2,1)S(1)}, u32[]{:S(2)}, u32[]{:S(2)}) collective-permute-start(bf16[256,512]{1,0:T(8,128)(2,1)} %get-tuple-element.132), channel_id=1, source_target_pairs={{128,129},{129,128},{130,131},{131,130},{132,133},{133,132},{134,1... | collective-permute-start | bytes 786440 | tf_op jit(solution)/shard_map/cond/branch_0_fun/ppermute | solution.py:41
  78.5 3.8 %collective-permute-start.5 = (bf16[128,2048]{1,0:T(8,128)(2,1)S(1)}, bf16[128,2048]{1,0:T(8,128)(2,1)S(1)}, u32[]{:S(2)}, u32[]{:S(2)}) collective-permute-start(bf16[128,2048]{1,0:T(8,128)(2,1)S(1)} %pad_maximum_fusion), channel_id=1, source_target_pairs={{128,132},{129,133},{130,134},{131,135},{132,128},{133,129},{134,1... | collective-permute-start | bytes 1572872 | tf_op jit(solution)/shard_map/cond/branch_0_fun/ppermute | solution.py:41
  87.2 6.6 %collective-permute-start.6 = (bf16[128,2048]{1,0:T(8,128)(2,1)S(1)}, bf16[128,2048]{1,0:T(8,128)(2,1)S(1)}, u32[]{:S(2)}, u32[]{:S(2)}) collective-permute-start(bf16[128,2048]{1,0:T(8,128)(2,1)S(1)} %slice.379), channel_id=1, source_target_pairs={{128,132},{129,133},{130,134},{131,135},{132,128},{133,129},{134,1... | collective-permute-start | bytes 1572872 | tf_op jit(solution)/shard_map/cond/branch_0_fun/ppermute | solution.py:41
  91.6 18.8 %collective-permute-start.10 = (bf16[256,1024]{1,0:T(8,128)(2,1)S(1)}, bf16[256,1024]{1,0:T(8,128)(2,1)}, u32[]{:S(2)}, u32[]{:S(2)}) collective-permute-start(bf16[256,1024]{1,0:T(8,128)(2,1)S(1)} %pad_maximum_fusion.1), channel_id=1, source_target_pairs={{128,129},{129,128},{130,131},{131,130},{132,133},{133,132},{134,1... | collective-permute-start | bytes 1572872 | tf_op jit(solution)/shard_map/cond/branch_0_fun/ppermute | solution.py:41
  94.0 10.7 %collective-permute-start.7 = (bf16[32,2048]{1,0:T(8,128)(2,1)S(1)}, bf16[32,2048]{1,0:T(8,128)(2,1)S(1)}, u32[]{:S(2)}, u32[]{:S(2)}) collective-permute-start(bf16[32,2048]{1,0:T(8,128)(2,1)S(1)} %get-tuple-element.255), channel_id=1, source_target_pairs={{128,144},{129,145},{130,146},{131,147},{132,148},{133,149},{134,1... | collective-permute-start | bytes 393224 | tf_op jit(solution)/shard_map/cond/branch_0_fun/ppermute | solution.py:41
  96.2 10.5 %collective-permute-start.8 = (bf16[32,2048]{1,0:T(8,128)(2,1)S(1)}, bf16[32,2048]{1,0:T(8,128)(2,1)S(1)}, u32[]{:S(2)}, u32[]{:S(2)}) collective-permute-start(bf16[32,2048]{1,0:T(8,128)(2,1)S(1)} %get-tuple-element.257), channel_id=1, source_target_pairs={{128,160},{129,161},{130,162},{131,163},{132,164},{133,165},{134,1... | collective-permute-start | bytes 393224 | tf_op jit(solution)/shard_map/cond/branch_0_fun/ppermute | solution.py:41
  102.1 8.3 %collective-permute-start.9 = (bf16[32,2048]{1,0:T(8,128)(2,1)S(1)}, bf16[32,2048]{1,0:T(8,128)(2,1)S(1)}, u32[]{:S(2)}, u32[]{:S(2)}) collective-permute-start(bf16[32,2048]{1,0:T(8,128)(2,1)S(1)} %get-tuple-element.256), channel_id=1, source_target_pairs={{128,176},{129,177},{130,178},{131,179},{132,180},{133,181},{134,1... | collective-permute-start | bytes 393224 | tf_op jit(solution)/shard_map/cond/branch_0_fun/ppermute | solution.py:41
  110.5 7.0 %collective-permute-start.11 = (bf16[32,1024]{1,0:T(8,128)(2,1)S(1)}, bf16[32,1024]{1,0:T(8,128)(2,1)S(1)}, u32[]{:S(2)}, u32[]{:S(2)}) collective-permute-start(bf16[32,1024]{1,0:T(8,128)(2,1)S(1)} %slice.614), channel_id=1, source_target_pairs={{128,129},{129,128},{130,131},{131,130},{132,133},{133,132},{134,1... | collective-permute-start | bytes 196616 | tf_op jit(solution)/shard_map/cond/branch_0_fun/ppermute | solution.py:41
  117.7 3.9 %copy-start.22 = (bf16[32,1024]{1,0:T(8,128)(2,1)}, bf16[32,1024]{1,0:T(8,128)(2,1)S(1)}, u32[]{:S(2)}) copy-start(bf16[32,1024]{1,0:T(8,128)(2,1)S(1)} %get-tuple-element.229) | copy-start | bytes 196612
  117.7 4.6 %collective-permute-start.52 = (bf16[32,512]{1,0:T(8,128)(2,1)}, bf16[32,512]{1,0:T(8,128)(2,1)}, u32[]{:S(2)}, u32[]{:S(2)}) collective-permute-start(bf16[32,512]{1,0:T(8,128)(2,1)} %get-tuple-element.231), channel_id=1, source_target_pairs={{72,128},{73,129},{74,130},{75,131},{76,132},{77,133},{78,134},{79... | collective-permute-start | bytes 98312 | tf_op jit(solution)/shard_map/ppermute | solution.py:41
  119.0 8.7 %collective-permute-start.53 = (bf16[32,512]{1,0:T(8,128)(2,1)}, bf16[32,512]{1,0:T(8,128)(2,1)S(1)}, u32[]{:S(2)}, u32[]{:S(2)}) collective-permute-start(bf16[32,512]{1,0:T(8,128)(2,1)} %get-tuple-element.231), channel_id=1, source_target_pairs={{72,136},{73,137},{74,138},{75,139},{76,140},{77,141},{78,142},{79... | collective-permute-start | bytes 98312 | tf_op jit(solution)/shard_map/ppermute | solution.py:41
  119.7 12.9 %collective-permute-start.54 = (bf16[32,512]{1,0:T(8,128)(2,1)}, bf16[32,512]{1,0:T(8,128)(2,1)S(1)}, u32[]{:S(2)}, u32[]{:S(2)}) collective-permute-start(bf16[32,512]{1,0:T(8,128)(2,1)} %get-tuple-element.231), channel_id=1, source_target_pairs={{72,192},{73,193},{74,194},{75,195},{76,196},{77,197},{78,198},{79... | collective-permute-start | bytes 98312 | tf_op jit(solution)/shard_map/ppermute | solution.py:41
  121.0 11.6 %collective-permute-start.55 = (bf16[32,512]{1,0:T(8,128)(2,1)}, bf16[32,512]{1,0:T(8,128)(2,1)S(1)}, u32[]{:S(2)}, u32[]{:S(2)}) collective-permute-start(bf16[32,512]{1,0:T(8,128)(2,1)} %get-tuple-element.231), channel_id=1, source_target_pairs={{72,200},{73,201},{74,202},{75,203},{76,204},{77,205},{78,206},{79... | collective-permute-start | bytes 98312 | tf_op jit(solution)/shard_map/ppermute | solution.py:41
  121.6 11.5 %collective-permute-start.50 = (bf16[32,1024]{1,0:T(8,128)(2,1)}, bf16[32,1024]{1,0:T(8,128)(2,1)S(1)}, u32[]{:S(2)}, u32[]{:S(2)}) collective-permute-start(bf16[32,1024]{1,0:T(8,128)(2,1)} %copy-done.22), channel_id=1, source_target_pairs={{128,64},{129,65},{130,66},{131,67},{132,68},{133,69},{134,70},{13... | collective-permute-start | bytes 196616 | tf_op jit(solution)/shard_map/ppermute | solution.py:41
  122.3 10.8 %collective-permute-start.51 = (bf16[32,1024]{1,0:T(8,128)(2,1)}, bf16[32,1024]{1,0:T(8,128)(2,1)S(1)}, u32[]{:S(2)}, u32[]{:S(2)}) collective-permute-start(bf16[32,1024]{1,0:T(8,128)(2,1)} %copy-done.22), channel_id=1, source_target_pairs={{192,64},{193,65},{194,66},{195,67},{196,68},{197,69},{198,70},{19... | collective-permute-start | bytes 196616 | tf_op jit(solution)/shard_map/ppermute | solution.py:41
  133.9 8.9 %collective-permute-start.34 = (bf16[32,512]{1,0:T(8,128)(2,1)S(1)}, bf16[32,512]{1,0:T(8,128)(2,1)S(1)}, u32[]{:S(2)}, u32[]{:S(2)}) collective-permute-start(bf16[32,512]{1,0:T(8,128)(2,1)S(1)} %add_add_fusion.1), channel_id=1, source_target_pairs={{128,130},{129,131},{130,128},{131,129},{132,134},{133,135},{134,1... | collective-permute-start | bytes 98312 | tf_op jit(solution)/shard_map/cond/branch_1_fun/ppermute | solution.py:41
  142.8 6.2 %collective-permute-start.35 = (bf16[32,1024]{1,0:T(8,128)(2,1)S(1)}, bf16[32,1024]{1,0:T(8,128)(2,1)S(1)}, u32[]{:S(2)}, u32[]{:S(2)}) collective-permute-start(bf16[32,1024]{1,0:T(8,128)(2,1)S(1)} %pad_maximum_fusion.17), channel_id=1, source_target_pairs={{128,129},{129,128},{130,131},{131,130},{132,133},{133,132},{134,1... | collective-permute-start | bytes 196616 | tf_op jit(solution)/shard_map/cond/branch_1_fun/ppermute | solution.py:41
  149.2 14.6 %collective-permute-start.37 = (bf16[32,2048]{1,0:T(8,128)(2,1)S(1)}, bf16[32,2048]{1,0:T(8,128)(2,1)S(1)}, u32[]{:S(2)}, u32[]{:S(2)}) collective-permute-start(bf16[32,2048]{1,0:T(8,128)(2,1)S(1)} %get-tuple-element.250), channel_id=1, source_target_pairs={{128,144},{129,145},{130,146},{131,147},{132,148},{133,149},{134,1... | collective-permute-start | bytes 393224 | tf_op jit(solution)/shard_map/cond/branch_1_fun/ppermute | solution.py:41
  151.2 12.7 %collective-permute-start.38 = (bf16[32,2048]{1,0:T(8,128)(2,1)S(1)}, bf16[32,2048]{1,0:T(8,128)(2,1)S(1)}, u32[]{:S(2)}, u32[]{:S(2)}) collective-permute-start(bf16[32,2048]{1,0:T(8,128)(2,1)S(1)} %get-tuple-element.250), channel_id=1, source_target_pairs={{128,160},{129,161},{130,162},{131,163},{132,164},{133,165},{134,1... | collective-permute-start | bytes 393224 | tf_op jit(solution)/shard_map/cond/branch_1_fun/ppermute | solution.py:41
  155.0 8.9 %collective-permute-start.39 = (bf16[32,2048]{1,0:T(8,128)(2,1)S(1)}, bf16[32,2048]{1,0:T(8,128)(2,1)S(1)}, u32[]{:S(2)}, u32[]{:S(2)}) collective-permute-start(bf16[32,2048]{1,0:T(8,128)(2,1)S(1)} %get-tuple-element.250), channel_id=1, source_target_pairs={{128,176},{129,177},{130,178},{131,179},{132,180},{133,181},{134,1... | collective-permute-start | bytes 393224 | tf_op jit(solution)/shard_map/cond/branch_1_fun/ppermute | solution.py:41
  160.8 11.3 %collective-permute-start.36 = (bf16[257,1024]{1,0:T(8,128)(2,1)S(1)}, bf16[257,1024]{1,0:T(8,128)(2,1)S(1)}, u32[]{:S(2)}, u32[]{:S(2)}) collective-permute-start(bf16[257,1024]{1,0:T(8,128)(2,1)S(1)} %pad_maximum_fusion.13), channel_id=1, source_target_pairs={{128,129},{129,128},{130,131},{131,130},{132,133},{133,132},{134,1... | collective-permute-start | bytes 1579016 | tf_op jit(solution)/shard_map/cond/branch_1_fun/ppermute | solution.py:41
  163.9 9.6 %collective-permute-start.40 = (bf16[128,2048]{1,0:T(8,128)(2,1)S(1)}, bf16[128,2048]{1,0:T(8,128)(2,1)S(1)}, u32[]{:S(2)}, u32[]{:S(2)}) collective-permute-start(bf16[128,2048]{1,0:T(8,128)(2,1)S(1)} %pad_maximum_fusion.14), channel_id=1, source_target_pairs={{128,132},{129,133},{130,134},{131,135},{132,128},{133,129},{134,1... | collective-permute-start | bytes 1572872 | tf_op jit(solution)/shard_map/cond/branch_1_fun/ppermute | solution.py:41
  173.6 1.6 copy-start.4
  175.9 1.6 copy-start.7
  178.3 22.1 %copy-start.25 = (f32[256]{0:T(256)S(1)}, f32[256]{0:T(256)}, u32[]{:S(2)}) copy-start(f32[256]{0:T(256)} %get-tuple-element.205) | copy-start | bytes 3076
  178.3 22.1 %copy-start.26 = (f32[256,1]{0,1:T(1,128)S(1)}, f32[256,1]{0,1:T(1,128)}, u32[]{:S(2)}) copy-start(f32[256,1]{0,1:T(1,128)} %get-tuple-element.206) | copy-start | bytes 3076
  178.3 22.1 %copy-start.12 = (bf16[256,512]{1,0:T(8,128)(2,1)S(1)}, bf16[256,512]{1,0:T(8,128)(2,1)}, u32[]{:S(2)}) copy-start(bf16[256,512]{1,0:T(8,128)(2,1)} %get-tuple-element.207) | copy-start | bytes 786436
  178.3 15.2 %collective-permute-start.41 = (bf16[256,512]{1,0:T(8,128)(2,1)S(1)}, bf16[256,512]{1,0:T(8,128)(2,1)S(1)}, u32[]{:S(2)}, u32[]{:S(2)}) collective-permute-start(bf16[256,512]{1,0:T(8,128)(2,1)S(1)} %get-tuple-element.292), channel_id=1, source_target_pairs={{128,129},{129,128},{130,131},{131,130},{132,133},{133,132},{134,1... | collective-permute-start | bytes 786440 | tf_op jit(solution)/shard_map/cond/branch_1_fun/ppermute | solution.py:41
  181.5 15.4 %collective-permute-start.43 = (bf16[257,512]{1,0:T(8,128)(2,1)S(1)}, bf16[257,512]{1,0:T(8,128)(2,1)S(1)}, u32[]{:S(2)}, u32[]{:S(2)}) collective-permute-start(bf16[257,512]{1,0:T(8,128)(2,1)S(1)} %pad_maximum_fusion.16), channel_id=1, source_target_pairs={{128,130},{129,131},{130,128},{131,129},{132,134},{133,135},{134,1... | collective-permute-start | bytes 789512 | tf_op jit(solution)/shard_map/cond/branch_1_fun/ppermute | solution.py:41
  193.6 8.5 %collective-permute-start.42 = (bf16[256,512]{1,0:T(8,128)(2,1)S(1)}, bf16[256,512]{1,0:T(8,128)(2,1)S(1)}, u32[]{:S(2)}, u32[]{:S(2)}) collective-permute-start(bf16[256,512]{1,0:T(8,128)(2,1)S(1)} %get-tuple-element.200), channel_id=1, source_target_pairs={{128,129},{129,128},{130,131},{131,130},{132,133},{133,132},{134,1... | collective-permute-start | bytes 786440 | tf_op jit(solution)/shard_map/cond/branch_1_fun/ppermute | solution.py:41
  197.0 12.0 %collective-permute-start.44 = (bf16[256,512]{1,0:T(8,128)(2,1)S(1)}, bf16[256,512]{1,0:T(8,128)(2,1)S(1)}, u32[]{:S(2)}, u32[]{:S(2)}) collective-permute-start(bf16[256,512]{1,0:T(8,128)(2,1)S(1)} %add_convert_fusion.5), channel_id=1, source_target_pairs={{128,130},{129,131},{130,128},{131,129},{132,134},{133,135},{134,1... | collective-permute-start | bytes 786440 | tf_op jit(solution)/shard_map/cond/branch_1_fun/ppermute | solution.py:41
  209.4 18.3 %copy-start.1 = (bf16[256,512]{1,0:T(8,128)(2,1)S(1)}, bf16[256,512]{1,0:T(8,128)(2,1)}, u32[]{:S(2)}) copy-start(bf16[256,512]{1,0:T(8,128)(2,1)} %param.15) | copy-start | bytes 786436
  209.5 17.5 %collective-permute-start.56 = (bf16[256,512]{1,0:T(8,128)(2,1)S(1)}, bf16[256,512]{1,0:T(8,128)(2,1)S(1)}, u32[]{:S(2)}, u32[]{:S(2)}) collective-permute-start(bf16[256,512]{1,0:T(8,128)(2,1)S(1)} %get-tuple-element.233), channel_id=1, source_target_pairs={{128,132},{129,133},{130,134},{131,135},{132,136},{133,137},{134,1... | collective-permute-start | bytes 786440 | tf_op jit(solution)/shard_map/ppermute | solution.py:41

commit v3 on v2

--- a/solution.py
+++ b/solution.py
@@ -269,14 +269,14 @@
 
     def dec_phase1(_):
         b_last = swap_t(b_far, 1, decoders)
-        c_far = swap_t(fwd_shard, 2, decoders)
         q = mm(a_normed, w_q).astype(bf16)
         saved_rows, q = tie(scale_rows(saved, inverse_rms(saved), final), q)
         saved_half = jnp.concatenate([saved_rows] + [swap_x(saved_rows, k, decoders) for k in range(1, NX)], axis=0)
-        saved_half, b_last, c_far = lax.optimization_barrier((saved_half, b_last, c_far))
+        saved_half, b_last = tie(saved_half, b_last)
         saved_normed = jnp.concatenate([saved_half, swap_core(saved_half, decoders)], axis=0)
         k, v = mm(saved_normed, w_k).astype(bf16), mm(saved_normed, w_v).astype(bf16)
-        c_near = swap_t(jnp.concatenate([fwd_shard, c_far], axis=1), 1, decoders)
+        c_shard, b_last = tie(fwd_shard, b_last)
+        c_far, c_near = swap_t(c_shard, 2, decoders), swap_t(c_shard, 1, decoders)
         b_full = jnp.concatenate([b_three, b_last], axis=1)
         dq, dk, dv = attend_back(q, k, v, b_full, w_o)
         dc = (mm_t(dk, w_k) + mm_t(dv, w_v)).astype(bf16)
@@ -286,10 +286,10 @@
         total = acc[:part]
         for k in range(1, NX):
             total = total + swap_x(acc16[k * part : (k + 1) * part], k, decoders).astype(f32)
-        total, c_near = tie(total, c_near)
+        total, c_far, c_near = lax.optimization_barrier((total, c_far, c_near))
         total = total[:, : 2 * width] + swap_t(total[:, 2 * width :].astype(bf16), 1, decoders).astype(f32)
         total = total.astype(bf16)
-        return fwd_shard, fwd_shard[:part], c_near, c_far, dn, total
+        return fwd_shard, fwd_shard[:part], jnp.concatenate([c_near, c_near], axis=1), c_far, dn, total
 
     enc_y, top, near, c_far, dn, total = lax.cond(~dec, enc_phase1, dec_phase1, 0)
 
@@ -317,7 +317,7 @@
         pair = jnp.concatenate([mine, swap_t(mine, 2, top_row)], axis=1)
         u = jnp.concatenate([pair, swap_t(pair, 1, top_row)], axis=1)
         c_pair = jnp.concatenate([cot_shard, c_far], axis=1)
-        c_pair, u, y_out = lax.optimization_barrier((c_pair, u, enc_y))
+        c_pair, u = tie(c_pair, u)
         c_near = swap_t(c_pair, 1, encoders)
         u = final * u.astype(f32)
         r = inverse_rms(saved)
@@ -336,7 +336,7 @@
             k = xi ^ (NX - 1)
             pieces += [swapped[k * part : (k + 1) * part], slots[k * part : (k + 1) * part]]
         returned_full = jnp.concatenate(pieces, axis=0)
-        sent = move(y_out, following(False))
+        sent = move(enc_y, following(False))
         values = b_full.astype(f32)
         inverse = inverse_rms(values)
         normed = scale_rows(values, inverse, gain)
@@ -349,11 +349,12 @@
         return sent, summed, row_sum, inverse, upstream[:, :width]
 
     def dec_phase2(_):
-        c_full = jnp.concatenate([fwd_shard, c_far, near], axis=1)
         all_top = jnp.concatenate([top, swap_t(top, 2, decoders)], axis=1)
         all_top = jnp.concatenate([all_top, swap_t(all_top, 1, decoders)], axis=1).astype(f32)
         row_part = jnp.sum(gain * dn.astype(f32) * a_values, axis=-1)
-        dn_tied, all_top = tie(dn, all_top)
+        dn_tied, all_top, c_last = lax.optimization_barrier((dn, all_top, c_far))
+        c_last = swap_t(c_last, 1, decoders)
+        c_full = jnp.concatenate([fwd_shard, c_far, near[:, :width], c_last], axis=1)
         dn_pair, row_part = scatter_near(dn_tied, row_part, decoders)
         top_full = gather_rows(scale_rows(all_top, inverse_rms(all_top), final), decoders)
         values = c_full.astype(f32)

time: 229 us -> 225 us (0.983)
  matrix products: 17.2 us -> 13.1 us
  waiting for transfers between devices: 79 us -> 75.5 us
    ppermute x35 -> x36, waiting for transfers between devices: 79 us -> 75.5 us  [move(): return lax.ppermute(value, ('section', 'tensor'), pairs)]
    dot_general x11, matrix products: 9.38 us -> 6.9 us  [mm(): return jnp.dot(a, b, preferred_element_type=f32)]
    ppermute x35 -> x36, starting transfers between devices: 88.3 us -> 89.5 us  [move(): return lax.ppermute(value, ('section', 'tensor'), pairs)]
  transfers between devices with their start and end apart: 35 -> 36, of which waited for: 18 -> 19; matrix products, arithmetic and copies ran while one was open for 14% -> 14% of each run, Pallas kernels for 0% -> 0%
where the time goes in v3:
time: 225 us; the launch traced here: 224 us
  starting transfers between devices  89.5 us (40%)
  waiting for transfers between devices  75.5 us (34%)
  other arithmetic  28.1 us (12%)
  local copies, waits for them, and re-layouts  15.3 us (7%)
  matrix products  13.1 us (6%)
    ppermute x36, starting transfers between devices, move(): return lax.ppermute(value, ('section', 'tensor'), pairs)  89.5 us
    ppermute x36, waiting for transfers between devices, move(): return lax.ppermute(value, ('section', 'tensor'), pairs)  75.5 us
    dot_general x11, matrix products, mm(): return jnp.dot(a, b, preferred_element_type=f32)  6.9 us
    dot_general x10, matrix products, mm_t(): lax.dot_general(a, b, (((1,), (1,)), ((), ())), preferred_element_type=f32)  5.47 us
  transfers between devices with their start and end apart: 36, of which 19 were waited for; matrix products, arithmetic and copies ran while one was open for 14% of the time, Pallas kernels for 0%

profile of v3, /device:TPU:24, one launch (start us, length us, event | category | flops | bytes accessed | tf_op | source)
XLA Modules:
  0.0 223.5 jit_solution(4191855542699522007)
XLA Ops:
  2.8 1.4 pad_maximum_fusion.30
  4.2 1.9 collective-permute-start.47
  6.1 3.3 %collective-permute-start.46 = (bf16[290,512]{1,0:T(8,128)(2,1)}, bf16[290,512]{1,0:T(8,128)(2,1)}, u32[]{:S(2)}, u32[]{:S(2)}) collective-permute-start(bf16[290,512]{1,0:T(8,128)(2,1)} %pad_maximum_fusion.30), channel_id=1, source_target_pairs={{0,2},{1,3},{2,0},{3,1},{4,6},{5,7},{6,4},{7,5},{8,10},{9,11},{10,... | collective-permute-start | bytes 890888 | tf_op jit(solution)/shard_map/ppermute | solution.py:41
  9.4 3.2 %dynamic-slice_bitcast_fusion.3 = (bf16[512,3,512]{2,0,1:T(8,128)(2,1)S(1)}, bf16[512,3,512]{2,0,1:T(8,128)(2,1)S(1)}, bf16[512,3,512]{2,0,1:T(8,128)(2,1)S(1)}, bf16[512,3,512]{2,0,1:T(8,128)(2,1)S(1)}) fusion(bf16[1,2048,3,512]{3,1,2,0:T(8,128)(2,1)} %param.18, s32[]{:T(128)S(6)} %select_n.96, s32[]{:T(128)S(6)} %select_n.97, s32[]{:T(128)S(6)} %select_n.99, ...), kind=kLoop, calls=%fused_computation.294 | loop fusion | bytes 12582928 | tf_op jit(solution)/shard_map/dynamic_slice | solution.py:242
  13.1 1.5 pad_maximum_fusion.22
  14.8 1.4 copy-done.19
  16.5 1.5 pad_maximum_fusion.19
  18.0 1.8 collective-permute-done.47
  19.7 3.6 %collective-permute-done.46 = bf16[290,512]{1,0:T(8,128)(2,1)} collective-permute-done((bf16[290,512]{1,0:T(8,128)(2,1)}, bf16[290,512]{1,0:T(8,128)(2,1)}, u32[]{:S(2)}, u32[]{:S(2)}) %collective-permute-start.46) | collective-permute-done | bytes 296992 | tf_op jit(solution)/shard_map/ppermute | solution.py:41
  23.4 2.7 %collective-permute-start.50 = (bf16[256,512]{1,0:T(8,128)(2,1)S(1)}, bf16[256,512]{1,0:T(8,128)(2,1)}, u32[]{:S(2)}, u32[]{:S(2)}) collective-permute-start(bf16[256,512]{1,0:T(8,128)(2,1)S(1)} %get-tuple-element.228), channel_id=1, source_target_pairs={{0,1},{1,0},{2,3},{3,2},{4,5},{5,4},{6,7},{7,6},{8,9},{9,8},{10,11... | collective-permute-start | bytes 786440 | tf_op jit(solution)/shard_map/ppermute | solution.py:41
  26.1 1.7 pad_maximum_fusion.21
  27.8 6.7 %collective-permute-done.49 = bf16[256,512]{1,0:T(8,128)(2,1)} collective-permute-done((bf16[256,512]{1,0:T(8,128)(2,1)S(1)}, bf16[256,512]{1,0:T(8,128)(2,1)}, u32[]{:S(2)}, u32[]{:S(2)}) %collective-permute-start.49) | collective-permute-done | bytes 262176 | tf_op jit(solution)/shard_map/ppermute | solution.py:41
  34.5 2.0 collective-permute-done.50
  37.7 3.2 %collective-permute-done.48 = bf16[290,512]{1,0:T(8,128)(2,1)} collective-permute-done((bf16[290,512]{1,0:T(8,128)(2,1)}, bf16[290,512]{1,0:T(8,128)(2,1)}, u32[]{:S(2)}, u32[]{:S(2)}) %collective-permute-start.48) | collective-permute-done | bytes 296992 | tf_op jit(solution)/shard_map/ppermute | solution.py:41
  43.4 1.3 multiply_reduce_fusion.9
  45.3 1.3 multiply_convert_fusion.6
  46.7 65.8 %conditional.3 = (bf16[256,512]{1,0:T(8,128)(2,1)}, bf16[32,512]{1,0:T(8,128)(2,1)}, bf16[256,1024]{1,0:T(8,128)(2,1)}, bf16[256,512]{1,0:T(8,128)(2,1)}, bf16[2...) conditional(s32[]{:T(128)} %convert_element_type.364, (bf16[256,512]{1,0:T(8,128)(2,1)S(1)}, ...), branch_computations={%region_1.7_spmd, %region_7.10_spmd} | conditional | flops 4106386432 | bytes 55268368 | solution.py:294
  49.5 3.4 %collective-permute-start = (bf16[32,2048]{1,0:T(8,128)(2,1)S(1)}, bf16[32,2048]{1,0:T(8,128)(2,1)S(1)}, u32[]{:S(2)}, u32[]{:S(2)}) collective-permute-start(bf16[32,2048]{1,0:T(8,128)(2,1)S(1)} %multiply_convert_fusion.2), channel_id=1, source_target_pairs={{128,144},{129,145},{130,146},{131,147},{132,148},{133,149},{134,1... | collective-permute-start | bytes 393224 | tf_op jit(solution)/shard_map/cond/branch_0_fun/ppermute | solution.py:41
  53.0 4.6 %collective-permute-start.1 = (bf16[32,2048]{1,0:T(8,128)(2,1)S(1)}, bf16[32,2048]{1,0:T(8,128)(2,1)S(1)}, u32[]{:S(2)}, u32[]{:S(2)}) collective-permute-start(bf16[32,2048]{1,0:T(8,128)(2,1)S(1)} %multiply_convert_fusion.2), channel_id=1, source_target_pairs={{128,160},{129,161},{130,162},{131,163},{132,164},{133,165},{134,1... | collective-permute-start | bytes 393224 | tf_op jit(solution)/shard_map/cond/branch_0_fun/ppermute | solution.py:41
  57.6 2.4 %collective-permute-start.2 = (bf16[32,2048]{1,0:T(8,128)(2,1)S(1)}, bf16[32,2048]{1,0:T(8,128)(2,1)S(1)}, u32[]{:S(2)}, u32[]{:S(2)}) collective-permute-start(bf16[32,2048]{1,0:T(8,128)(2,1)S(1)} %multiply_convert_fusion.2), channel_id=1, source_target_pairs={{128,176},{129,177},{130,178},{131,179},{132,180},{133,181},{134,1... | collective-permute-start | bytes 393224 | tf_op jit(solution)/shard_map/cond/branch_0_fun/ppermute | solution.py:41
  60.0 3.2 %collective-permute-start.3 = (bf16[256,512]{1,0:T(8,128)(2,1)}, bf16[256,512]{1,0:T(8,128)(2,1)S(1)}, u32[]{:S(2)}, u32[]{:S(2)}) collective-permute-start(bf16[256,512]{1,0:T(8,128)(2,1)} %get-tuple-element.132), channel_id=1, source_target_pairs={{128,129},{129,128},{130,131},{131,130},{132,133},{133,132},{134,1... | collective-permute-start | bytes 786440 | tf_op jit(solution)/shard_map/cond/branch_0_fun/ppermute | solution.py:41
  63.2 2.5 %collective-permute-done.2 = bf16[32,2048]{1,0:T(8,128)(2,1)S(1)} collective-permute-done((bf16[32,2048]{1,0:T(8,128)(2,1)S(1)}, bf16[32,2048]{1,0:T(8,128)(2,1)S(1)}, u32[]{:S(2)}, u32[]{:S(2)}) %collective-permute-start.2) | collective-permute-done | bytes 131104 | tf_op jit(solution)/shard_map/cond/branch_0_fun/ppermute | solution.py:41
  65.7 2.7 %collective-permute-done.3 = bf16[256,512]{1,0:T(8,128)(2,1)S(1)} collective-permute-done((bf16[256,512]{1,0:T(8,128)(2,1)}, bf16[256,512]{1,0:T(8,128)(2,1)S(1)}, u32[]{:S(2)}, u32[]{:S(2)}) %collective-permute-start.3) | collective-permute-done | bytes 262176 | tf_op jit(solution)/shard_map/cond/branch_0_fun/ppermute | solution.py:41
  68.5 1.9 collective-permute-start.4
  77.2 2.0 collective-permute-start.5
  80.6 3.2 %collective-permute-start.10 = (bf16[256,512]{1,0:T(8,128)(2,1)S(1)}, bf16[256,512]{1,0:T(8,128)(2,1)S(1)}, u32[]{:S(2)}, u32[]{:S(2)}) collective-permute-start(bf16[256,512]{1,0:T(8,128)(2,1)S(1)} %get-tuple-element.140), channel_id=1, source_target_pairs={{128,129},{129,128},{130,131},{131,130},{132,133},{133,132},{134,1... | collective-permute-start | bytes 786440 | tf_op jit(solution)/shard_map/cond/branch_0_fun/ppermute | solution.py:41
  83.8 5.4 %collective-permute-start.9 = (bf16[256,512]{1,0:T(8,128)(2,1)S(1)}, bf16[256,512]{1,0:T(8,128)(2,1)}, u32[]{:S(2)}, u32[]{:S(2)}) collective-permute-start(bf16[256,512]{1,0:T(8,128)(2,1)S(1)} %get-tuple-element.140), channel_id=1, source_target_pairs={{128,130},{129,131},{130,128},{131,129},{132,134},{133,135},{134,1... | collective-permute-start | bytes 786440 | tf_op jit(solution)/shard_map/cond/branch_0_fun/ppermute | solution.py:41
  89.8 2.2 collective-permute-start.6
  92.0 5.9 %collective-permute-start.7 = (bf16[32,2048]{1,0:T(8,128)(2,1)S(1)}, bf16[32,2048]{1,0:T(8,128)(2,1)S(1)}, u32[]{:S(2)}, u32[]{:S(2)}) collective-permute-start(bf16[32,2048]{1,0:T(8,128)(2,1)S(1)} %get-tuple-element.259), channel_id=1, source_target_pairs={{128,160},{129,161},{130,162},{131,163},{132,164},{133,165},{134,1... | collective-permute-start | bytes 393224 | tf_op jit(solution)/shard_map/cond/branch_0_fun/ppermute | solution.py:41
  97.9 2.4 %collective-permute-start.8 = (bf16[32,2048]{1,0:T(8,128)(2,1)S(1)}, bf16[32,2048]{1,0:T(8,128)(2,1)S(1)}, u32[]{:S(2)}, u32[]{:S(2)}) collective-permute-start(bf16[32,2048]{1,0:T(8,128)(2,1)S(1)} %get-tuple-element.258), channel_id=1, source_target_pairs={{128,176},{129,177},{130,178},{131,179},{132,180},{133,181},{134,1... | collective-permute-start | bytes 393224 | tf_op jit(solution)/shard_map/cond/branch_0_fun/ppermute | solution.py:41
  100.3 1.7 convolution_convert_fusion
  102.0 4.0 %collective-permute-done.8 = bf16[32,2048]{1,0:T(8,128)(2,1)S(1)} collective-permute-done((bf16[32,2048]{1,0:T(8,128)(2,1)S(1)}, bf16[32,2048]{1,0:T(8,128)(2,1)S(1)}, u32[]{:S(2)}, u32[]{:S(2)}) %collective-permute-start.8) | collective-permute-done | bytes 131104 | tf_op jit(solution)/shard_map/cond/branch_0_fun/ppermute | solution.py:41
  106.0 2.2 collective-permute-start.11
  109.1 3.1 %collective-permute-done.11 = bf16[32,1024]{1,0:T(8,128)(2,1)S(1)} collective-permute-done((bf16[32,1024]{1,0:T(8,128)(2,1)S(1)}, bf16[32,1024]{1,0:T(8,128)(2,1)S(1)}, u32[]{:S(2)}, u32[]{:S(2)}) %collective-permute-start.11) | collective-permute-done | bytes 65568 | tf_op jit(solution)/shard_map/cond/branch_0_fun/ppermute | solution.py:41
  114.5 1.3 collective-permute-start.55
  117.2 1.3 collective-permute-start.52
  118.5 2.7 %fusion.132 = f32[256,2048]{1,0:T(8,128)} fusion(bf16[290,512]{1,0:T(8,128)(2,1)} %collective-permute-done.48, bf16[290,512]{1,0:T(8,128)(2,1)} %copy-done.13, bf16[290,512]{1,0:T(8,128)(2,1)} %collective-permute-done.46, bf16[1,512]{1,0:T(2,128)(2,1)S(1)} %broadcast_in_dim.6, bf16[1,512]{1,0:T(2,128)(2,1)} %param.16, ...), kind=kLoop, calls=%fused_computation.296 | loop fusion | flops 7340032 | bytes 3284992 | tf_op jit(solution)/shard_map/convert_element_type | solution.py:246
  121.2 1.3 slice.450
  122.5 4.9 %collective-permute-done.55 = bf16[32,512]{1,0:T(8,128)(2,1)S(1)} collective-permute-done((bf16[32,512]{1,0:T(8,128)(2,1)}, bf16[32,512]{1,0:T(8,128)(2,1)S(1)}, u32[]{:S(2)}, u32[]{:S(2)}) %collective-permute-start.55) | collective-permute-done | bytes 32800 | tf_op jit(solution)/shard_map/ppermute | solution.py:41
  127.9 77.1 %conditional.5 = (bf16[256,512]{1,0:T(8,128)(2,1)}, f32[256,512]{1,0:T(8,128)S(1)}, f32[256,1]{0,1:T(1,128)S(1)}, f32[256,1]{0,1:T(1,128)S(1)}, f32[256,512]{1,0:T(8,128)S(1)}) conditional(s32[]{:T(128)} %convert_element_type.363, (bf16[256,1024]{1,0:T(8,128)(2,1)}, bf16[256,1536]{1,0:T(8,128)(2,1)S(1)}, f32[1,2048]{1,0:T(1,128)S(1)}, ...), branch_computations={%region_10.19_spmd, %region_19.25_spmd} | conditional | flops 4127370752 | bytes 106249272
  128.7 1.9 collective-permute-start.34
  130.7 2.2 multiply_reduce_fusion.7
  132.9 2.7 %collective-permute-done.34 = bf16[32,512]{1,0:T(8,128)(2,1)S(1)} collective-permute-done((bf16[32,512]{1,0:T(8,128)(2,1)S(1)}, bf16[32,512]{1,0:T(8,128)(2,1)S(1)}, u32[]{:S(2)}, u32[]{:S(2)}) %collective-permute-start.34) | collective-permute-done | bytes 32800 | tf_op jit(solution)/shard_map/cond/branch_1_fun/ppermute | solution.py:41
  135.6 2.0 collective-permute-start.35
  137.7 4.1 %collective-permute-done.35 = bf16[32,1024]{1,0:T(8,128)(2,1)S(1)} collective-permute-done((bf16[32,1024]{1,0:T(8,128)(2,1)S(1)}, bf16[32,1024]{1,0:T(8,128)(2,1)S(1)}, u32[]{:S(2)}, u32[]{:S(2)}) %collective-permute-start.35) | collective-permute-done | bytes 65568 | tf_op jit(solution)/shard_map/cond/branch_1_fun/ppermute | solution.py:41
  142.1 1.9 collective-permute-start.38
  144.0 3.9 %collective-permute-start.39 = (bf16[32,2048]{1,0:T(8,128)(2,1)S(1)}, bf16[32,2048]{1,0:T(8,128)(2,1)S(1)}, u32[]{:S(2)}, u32[]{:S(2)}) collective-permute-start(bf16[32,2048]{1,0:T(8,128)(2,1)S(1)} %get-tuple-element.252), channel_id=1, source_target_pairs={{128,160},{129,161},{130,162},{131,163},{132,164},{133,165},{134,1... | collective-permute-start | bytes 393224 | tf_op jit(solution)/shard_map/cond/branch_1_fun/ppermute | solution.py:41
  147.9 4.6 %collective-permute-start.40 = (bf16[32,2048]{1,0:T(8,128)(2,1)S(1)}, bf16[32,2048]{1,0:T(8,128)(2,1)S(1)}, u32[]{:S(2)}, u32[]{:S(2)}) collective-permute-start(bf16[32,2048]{1,0:T(8,128)(2,1)S(1)} %get-tuple-element.252), channel_id=1, source_target_pairs={{128,176},{129,177},{130,178},{131,179},{132,180},{133,181},{134,1... | collective-permute-start | bytes 393224 | tf_op jit(solution)/shard_map/cond/branch_1_fun/ppermute | solution.py:41
  153.5 2.1 collective-permute-start.37
  156.7 3.8 %collective-permute-start.36 = (bf16[257,1024]{1,0:T(8,128)(2,1)S(1)}, bf16[257,1024]{1,0:T(8,128)(2,1)S(1)}, u32[]{:S(2)}, u32[]{:S(2)}) collective-permute-start(bf16[257,1024]{1,0:T(8,128)(2,1)S(1)} %pad_maximum_fusion.13), channel_id=1, source_target_pairs={{128,129},{129,128},{130,131},{131,130},{132,133},{133,132},{134,1... | collective-permute-start | bytes 1579016 | tf_op jit(solution)/shard_map/cond/branch_1_fun/ppermute | solution.py:41
  160.6 2.2 collective-permute-start.41
  164.1 1.7 convolution_convert_fusion.30
  165.8 2.7 %collective-permute-done.36 = bf16[257,1024]{1,0:T(8,128)(2,1)S(1)} collective-permute-done((bf16[257,1024]{1,0:T(8,128)(2,1)S(1)}, bf16[257,1024]{1,0:T(8,128)(2,1)S(1)}, u32[]{:S(2)}, u32[]{:S(2)}) %collective-permute-start.36) | collective-permute-done | bytes 526368 | tf_op jit(solution)/shard_map/cond/branch_1_fun/ppermute | solution.py:41
  174.8 3.5 %collective-permute-start.42 = (bf16[256,512]{1,0:T(8,128)(2,1)S(1)}, bf16[256,512]{1,0:T(8,128)(2,1)S(1)}, u32[]{:S(2)}, u32[]{:S(2)}) collective-permute-start(bf16[256,512]{1,0:T(8,128)(2,1)S(1)} %get-tuple-element.294), channel_id=1, source_target_pairs={{128,129},{129,128},{130,131},{131,130},{132,133},{133,132},{134,1... | collective-permute-start | bytes 786440 | tf_op jit(solution)/shard_map/cond/branch_1_fun/ppermute | solution.py:41
  178.3 2.8 %collective-permute-start.44 = (bf16[257,512]{1,0:T(8,128)(2,1)S(1)}, bf16[257,512]{1,0:T(8,128)(2,1)S(1)}, u32[]{:S(2)}, u32[]{:S(2)}) collective-permute-start(bf16[257,512]{1,0:T(8,128)(2,1)S(1)} %pad_maximum_fusion.15), channel_id=1, source_target_pairs={{128,130},{129,131},{130,128},{131,129},{132,134},{133,135},{134,1... | collective-permute-start | bytes 789512 | tf_op jit(solution)/shard_map/cond/branch_1_fun/ppermute | solution.py:41
  181.1 7.5 %collective-permute-done.42 = bf16[256,512]{1,0:T(8,128)(2,1)S(1)} collective-permute-done((bf16[256,512]{1,0:T(8,128)(2,1)S(1)}, bf16[256,512]{1,0:T(8,128)(2,1)S(1)}, u32[]{:S(2)}, u32[]{:S(2)}) %collective-permute-start.42) | collective-permute-done | bytes 262176 | tf_op jit(solution)/shard_map/cond/branch_1_fun/ppermute | solution.py:41
  188.6 1.9 collective-permute-start.43
  190.6 1.4 collective-permute-done.44
  192.2 4.2 %collective-permute-start.45 = (bf16[256,512]{1,0:T(8,128)(2,1)S(1)}, bf16[256,512]{1,0:T(8,128)(2,1)S(1)}, u32[]{:S(2)}, u32[]{:S(2)}) collective-permute-start(bf16[256,512]{1,0:T(8,128)(2,1)S(1)} %add_convert_fusion.5), channel_id=1, source_target_pairs={{128,130},{129,131},{130,128},{131,129},{132,134},{133,135},{134,1... | collective-permute-start | bytes 786440 | tf_op jit(solution)/shard_map/cond/branch_1_fun/ppermute | solution.py:41
  196.5 1.9 collective-permute-done.43
  198.4 5.7 %collective-permute-done.45 = bf16[256,512]{1,0:T(8,128)(2,1)S(1)} collective-permute-done((bf16[256,512]{1,0:T(8,128)(2,1)S(1)}, bf16[256,512]{1,0:T(8,128)(2,1)S(1)}, u32[]{:S(2)}, u32[]{:S(2)}) %collective-permute-start.45) | collective-permute-done | bytes 262176 | tf_op jit(solution)/shard_map/cond/branch_1_fun/ppermute | solution.py:41
  205.0 2.1 collective-permute-start.57
  207.1 1.9 fusion.133
  208.9 13.8 %collective-permute-done.57 = bf16[256,512]{1,0:T(8,128)(2,1)S(1)} collective-permute-done((bf16[256,512]{1,0:T(8,128)(2,1)}, bf16[256,512]{1,0:T(8,128)(2,1)S(1)}, u32[]{:S(2)}, u32[]{:S(2)}) %collective-permute-start.57) | collective-permute-done | bytes 262176 | tf_op jit(solution)/shard_map/ppermute | solution.py:41
  (156 shorter events, 36.1 us)
Async XLA Ops:
  0.6 1.0 copy-start
  2.7 20.6 %copy-start.21 = (bf16[256,512]{1,0:T(8,128)(2,1)}, bf16[256,512]{1,0:T(8,128)(2,1)S(1)}, u32[]{:S(2)}) copy-start(bf16[256,512]{1,0:T(8,128)(2,1)S(1)} %get-tuple-element.228) | copy-start | bytes 786436
  4.2 15.5 %collective-permute-start.47 = (bf16[290,512]{1,0:T(8,128)(2,1)}, bf16[290,512]{1,0:T(8,128)(2,1)S(1)}, u32[]{:S(2)}, u32[]{:S(2)}) collective-permute-start(bf16[290,512]{1,0:T(8,128)(2,1)} %pad_maximum_fusion.30), channel_id=1, source_target_pairs={{0,1},{1,0},{2,3},{3,2},{4,5},{5,4},{6,7},{7,6},{8,9},{9,8},{10,11... | collective-permute-start | bytes 890888 | tf_op jit(solution)/shard_map/ppermute | solution.py:41
  6.1 17.3 %collective-permute-start.46 = (bf16[290,512]{1,0:T(8,128)(2,1)}, bf16[290,512]{1,0:T(8,128)(2,1)}, u32[]{:S(2)}, u32[]{:S(2)}) collective-permute-start(bf16[290,512]{1,0:T(8,128)(2,1)} %pad_maximum_fusion.30), channel_id=1, source_target_pairs={{0,2},{1,3},{2,0},{3,1},{4,6},{5,7},{6,4},{7,5},{8,10},{9,11},{10,... | collective-permute-start | bytes 890888 | tf_op jit(solution)/shard_map/ppermute | solution.py:41
  14.6 1.6 copy-start.19
  19.7 8.0 %copy-start.13 = (bf16[290,512]{1,0:T(8,128)(2,1)}, bf16[290,512]{1,0:T(8,128)(2,1)S(1)}, u32[]{:S(2)}) copy-start(bf16[290,512]{1,0:T(8,128)(2,1)S(1)} %collective-permute-done.47) | copy-start | bytes 890884
  23.4 11.1 %collective-permute-start.49 = (bf16[256,512]{1,0:T(8,128)(2,1)S(1)}, bf16[256,512]{1,0:T(8,128)(2,1)}, u32[]{:S(2)}, u32[]{:S(2)}) collective-permute-start(bf16[256,512]{1,0:T(8,128)(2,1)S(1)} %get-tuple-element.228), channel_id=1, source_target_pairs={{0,2},{1,3},{2,0},{3,1},{4,6},{5,7},{6,4},{7,5},{8,10},{9,11},{10,... | collective-permute-start | bytes 786440 | tf_op jit(solution)/shard_map/ppermute | solution.py:41
  23.4 13.1 %collective-permute-start.50 = (bf16[256,512]{1,0:T(8,128)(2,1)S(1)}, bf16[256,512]{1,0:T(8,128)(2,1)}, u32[]{:S(2)}, u32[]{:S(2)}) collective-permute-start(bf16[256,512]{1,0:T(8,128)(2,1)S(1)} %get-tuple-element.228), channel_id=1, source_target_pairs={{0,1},{1,0},{2,3},{3,2},{4,5},{5,4},{6,7},{7,6},{8,9},{9,8},{10,11... | collective-permute-start | bytes 786440 | tf_op jit(solution)/shard_map/ppermute | solution.py:41
  26.1 14.8 %collective-permute-start.48 = (bf16[290,512]{1,0:T(8,128)(2,1)}, bf16[290,512]{1,0:T(8,128)(2,1)}, u32[]{:S(2)}, u32[]{:S(2)}) collective-permute-start(bf16[290,512]{1,0:T(8,128)(2,1)} %collective-permute-done.46), channel_id=1, source_target_pairs={{0,1},{1,0},{2,3},{3,2},{4,5},{5,4},{6,7},{7,6},{8,9},{9,8},{10,11... | collective-permute-start | bytes 890888 | tf_op jit(solution)/shard_map/ppermute | solution.py:41
  26.1 10.4 %copy-start.22 = (bf16[256,512]{1,0:T(8,128)(2,1)S(1)}, bf16[256,512]{1,0:T(8,128)(2,1)}, u32[]{:S(2)}) copy-start(bf16[256,512]{1,0:T(8,128)(2,1)} %copy-done.21) | copy-start | bytes 786436
  26.1 14.8 %copy-start.27 = (bf16[1,512]{1,0:T(2,128)(2,1)S(1)}, bf16[1,512]{1,0:T(2,128)(2,1)}, u32[]{:S(2)}) copy-start(bf16[1,512]{1,0:T(2,128)(2,1)} %param.16) | copy-start | bytes 3076
  27.8 15.6 %copy-start.14 = (bf16[290,512]{1,0:T(8,128)(2,1)S(1)}, bf16[290,512]{1,0:T(8,128)(2,1)}, u32[]{:S(2)}) copy-start(bf16[290,512]{1,0:T(8,128)(2,1)} %copy-done.13) | copy-start | bytes 890884
  36.5 10.1 %copy-start.9 = (bf16[512,2048]{1,0:T(8,128)(2,1)S(1)}, bf16[512,2048]{1,0:T(8,128)(2,1)}, u32[]{:S(2)}) copy-start(bf16[512,2048]{1,0:T(8,128)(2,1)} %pad_maximum_fusion.21) | copy-start | bytes 6291460
  40.9 5.7 %copy-start.5 = (bf16[2048,512]{1,0:T(8,128)(2,1)S(1)}, bf16[2048,512]{1,0:T(8,128)(2,1)}, u32[]{:S(2)}) copy-start(bf16[2048,512]{1,0:T(8,128)(2,1)} %pad_maximum_fusion.19) | copy-start | bytes 6291460
  41.9 0.7 copy-start.20
  41.9 4.7 %copy-start.2 = (bf16[2048,512]{1,0:T(8,128)(2,1)S(1)}, bf16[2048,512]{1,0:T(8,128)(2,1)}, u32[]{:S(2)}) copy-start(bf16[2048,512]{1,0:T(8,128)(2,1)} %pad_maximum_fusion.22) | copy-start | bytes 6291460
  42.0 4.7 %copy-start.12 = (bf16[1,256,512]{2,1,0:T(8,128)(2,1)S(1)}, bf16[1,256,512]{2,1,0:T(8,128)(2,1)}, u32[]{:S(2)}) copy-start(bf16[1,256,512]{2,1,0:T(8,128)(2,1)} %param.12) | copy-start | bytes 786436
  44.7 0.6 copy-start.28
  49.5 13.6 %collective-permute-start = (bf16[32,2048]{1,0:T(8,128)(2,1)S(1)}, bf16[32,2048]{1,0:T(8,128)(2,1)S(1)}, u32[]{:S(2)}, u32[]{:S(2)}) collective-permute-start(bf16[32,2048]{1,0:T(8,128)(2,1)S(1)} %multiply_convert_fusion.2), channel_id=1, source_target_pairs={{128,144},{129,145},{130,146},{131,147},{132,148},{133,149},{134,1... | collective-permute-start | bytes 393224 | tf_op jit(solution)/shard_map/cond/branch_0_fun/ppermute | solution.py:41
  53.0 10.2 %collective-permute-start.1 = (bf16[32,2048]{1,0:T(8,128)(2,1)S(1)}, bf16[32,2048]{1,0:T(8,128)(2,1)S(1)}, u32[]{:S(2)}, u32[]{:S(2)}) collective-permute-start(bf16[32,2048]{1,0:T(8,128)(2,1)S(1)} %multiply_convert_fusion.2), channel_id=1, source_target_pairs={{128,160},{129,161},{130,162},{131,163},{132,164},{133,165},{134,1... | collective-permute-start | bytes 393224 | tf_op jit(solution)/shard_map/cond/branch_0_fun/ppermute | solution.py:41
  57.6 8.1 %collective-permute-start.2 = (bf16[32,2048]{1,0:T(8,128)(2,1)S(1)}, bf16[32,2048]{1,0:T(8,128)(2,1)S(1)}, u32[]{:S(2)}, u32[]{:S(2)}) collective-permute-start(bf16[32,2048]{1,0:T(8,128)(2,1)S(1)} %multiply_convert_fusion.2), channel_id=1, source_target_pairs={{128,176},{129,177},{130,178},{131,179},{132,180},{133,181},{134,1... | collective-permute-start | bytes 393224 | tf_op jit(solution)/shard_map/cond/branch_0_fun/ppermute | solution.py:41
  60.0 8.5 %collective-permute-start.3 = (bf16[256,512]{1,0:T(8,128)(2,1)}, bf16[256,512]{1,0:T(8,128)(2,1)S(1)}, u32[]{:S(2)}, u32[]{:S(2)}) collective-permute-start(bf16[256,512]{1,0:T(8,128)(2,1)} %get-tuple-element.132), channel_id=1, source_target_pairs={{128,129},{129,128},{130,131},{131,130},{132,133},{133,132},{134,1... | collective-permute-start | bytes 786440 | tf_op jit(solution)/shard_map/cond/branch_0_fun/ppermute | solution.py:41
  68.5 3.8 %collective-permute-start.4 = (bf16[128,2048]{1,0:T(8,128)(2,1)S(1)}, bf16[128,2048]{1,0:T(8,128)(2,1)S(1)}, u32[]{:S(2)}, u32[]{:S(2)}) collective-permute-start(bf16[128,2048]{1,0:T(8,128)(2,1)S(1)} %pad_maximum_fusion), channel_id=1, source_target_pairs={{128,132},{129,133},{130,134},{131,135},{132,128},{133,129},{134,1... | collective-permute-start | bytes 1572872 | tf_op jit(solution)/shard_map/cond/branch_0_fun/ppermute | solution.py:41
  77.2 12.4 %collective-permute-start.5 = (bf16[128,2048]{1,0:T(8,128)(2,1)S(1)}, bf16[128,2048]{1,0:T(8,128)(2,1)S(1)}, u32[]{:S(2)}, u32[]{:S(2)}) collective-permute-start(bf16[128,2048]{1,0:T(8,128)(2,1)S(1)} %slice.382), channel_id=1, source_target_pairs={{128,132},{129,133},{130,134},{131,135},{132,128},{133,129},{134,1... | collective-permute-start | bytes 1572872 | tf_op jit(solution)/shard_map/cond/branch_0_fun/ppermute | solution.py:41
  80.6 25.4 %collective-permute-start.10 = (bf16[256,512]{1,0:T(8,128)(2,1)S(1)}, bf16[256,512]{1,0:T(8,128)(2,1)S(1)}, u32[]{:S(2)}, u32[]{:S(2)}) collective-permute-start(bf16[256,512]{1,0:T(8,128)(2,1)S(1)} %get-tuple-element.140), channel_id=1, source_target_pairs={{128,129},{129,128},{130,131},{131,130},{132,133},{133,132},{134,1... | collective-permute-start | bytes 786440 | tf_op jit(solution)/shard_map/cond/branch_0_fun/ppermute | solution.py:41
  83.8 22.3 %collective-permute-start.9 = (bf16[256,512]{1,0:T(8,128)(2,1)S(1)}, bf16[256,512]{1,0:T(8,128)(2,1)}, u32[]{:S(2)}, u32[]{:S(2)}) collective-permute-start(bf16[256,512]{1,0:T(8,128)(2,1)S(1)} %get-tuple-element.140), channel_id=1, source_target_pairs={{128,130},{129,131},{130,128},{131,129},{132,134},{133,135},{134,1... | collective-permute-start | bytes 786440 | tf_op jit(solution)/shard_map/cond/branch_0_fun/ppermute | solution.py:41
  89.8 12.2 %collective-permute-start.6 = (bf16[32,2048]{1,0:T(8,128)(2,1)S(1)}, bf16[32,2048]{1,0:T(8,128)(2,1)S(1)}, u32[]{:S(2)}, u32[]{:S(2)}) collective-permute-start(bf16[32,2048]{1,0:T(8,128)(2,1)S(1)} %get-tuple-element.257), channel_id=1, source_target_pairs={{128,144},{129,145},{130,146},{131,147},{132,148},{133,149},{134,1... | collective-permute-start | bytes 393224 | tf_op jit(solution)/shard_map/cond/branch_0_fun/ppermute | solution.py:41
  92.0 10.0 %collective-permute-start.7 = (bf16[32,2048]{1,0:T(8,128)(2,1)S(1)}, bf16[32,2048]{1,0:T(8,128)(2,1)S(1)}, u32[]{:S(2)}, u32[]{:S(2)}) collective-permute-start(bf16[32,2048]{1,0:T(8,128)(2,1)S(1)} %get-tuple-element.259), channel_id=1, source_target_pairs={{128,160},{129,161},{130,162},{131,163},{132,164},{133,165},{134,1... | collective-permute-start | bytes 393224 | tf_op jit(solution)/shard_map/cond/branch_0_fun/ppermute | solution.py:41
  97.9 8.1 %collective-permute-start.8 = (bf16[32,2048]{1,0:T(8,128)(2,1)S(1)}, bf16[32,2048]{1,0:T(8,128)(2,1)S(1)}, u32[]{:S(2)}, u32[]{:S(2)}) collective-permute-start(bf16[32,2048]{1,0:T(8,128)(2,1)S(1)} %get-tuple-element.258), channel_id=1, source_target_pairs={{128,176},{129,177},{130,178},{131,179},{132,180},{133,181},{134,1... | collective-permute-start | bytes 393224 | tf_op jit(solution)/shard_map/cond/branch_0_fun/ppermute | solution.py:41
  106.0 6.2 %collective-permute-start.11 = (bf16[32,1024]{1,0:T(8,128)(2,1)S(1)}, bf16[32,1024]{1,0:T(8,128)(2,1)S(1)}, u32[]{:S(2)}, u32[]{:S(2)}) collective-permute-start(bf16[32,1024]{1,0:T(8,128)(2,1)S(1)} %slice.617), channel_id=1, source_target_pairs={{128,129},{129,128},{130,131},{131,130},{132,133},{133,132},{134,1... | collective-permute-start | bytes 196616 | tf_op jit(solution)/shard_map/cond/branch_0_fun/ppermute | solution.py:41
  112.4 4.0 %copy-start.26 = (bf16[32,1024]{1,0:T(8,128)(2,1)}, bf16[32,1024]{1,0:T(8,128)(2,1)S(1)}, u32[]{:S(2)}) copy-start(bf16[32,1024]{1,0:T(8,128)(2,1)S(1)} %get-tuple-element.231) | copy-start | bytes 196612
  112.5 4.7 %collective-permute-start.53 = (bf16[32,512]{1,0:T(8,128)(2,1)}, bf16[32,512]{1,0:T(8,128)(2,1)}, u32[]{:S(2)}, u32[]{:S(2)}) collective-permute-start(bf16[32,512]{1,0:T(8,128)(2,1)} %get-tuple-element.233), channel_id=1, source_target_pairs={{72,128},{73,129},{74,130},{75,131},{76,132},{77,133},{78,134},{79... | collective-permute-start | bytes 98312 | tf_op jit(solution)/shard_map/ppermute | solution.py:41
  113.7 14.2 %copy-start.6 = (bf16[2048,512]{1,0:T(8,128)(2,1)S(1)}, bf16[2048,512]{1,0:T(8,128)(2,1)}, u32[]{:S(2)}) copy-start(bf16[2048,512]{1,0:T(8,128)(2,1)} %pad_maximum_fusion.19) | copy-start | bytes 6291460
  113.7 8.8 %collective-permute-start.54 = (bf16[32,512]{1,0:T(8,128)(2,1)}, bf16[32,512]{1,0:T(8,128)(2,1)S(1)}, u32[]{:S(2)}, u32[]{:S(2)}) collective-permute-start(bf16[32,512]{1,0:T(8,128)(2,1)} %get-tuple-element.233), channel_id=1, source_target_pairs={{72,136},{73,137},{74,138},{75,139},{76,140},{77,141},{78,142},{79... | collective-permute-start | bytes 98312 | tf_op jit(solution)/shard_map/ppermute | solution.py:41
  114.5 12.9 %collective-permute-start.55 = (bf16[32,512]{1,0:T(8,128)(2,1)}, bf16[32,512]{1,0:T(8,128)(2,1)S(1)}, u32[]{:S(2)}, u32[]{:S(2)}) collective-permute-start(bf16[32,512]{1,0:T(8,128)(2,1)} %get-tuple-element.233), channel_id=1, source_target_pairs={{72,192},{73,193},{74,194},{75,195},{76,196},{77,197},{78,198},{79... | collective-permute-start | bytes 98312 | tf_op jit(solution)/shard_map/ppermute | solution.py:41
  115.8 11.6 %collective-permute-start.56 = (bf16[32,512]{1,0:T(8,128)(2,1)}, bf16[32,512]{1,0:T(8,128)(2,1)S(1)}, u32[]{:S(2)}, u32[]{:S(2)}) collective-permute-start(bf16[32,512]{1,0:T(8,128)(2,1)} %get-tuple-element.233), channel_id=1, source_target_pairs={{72,200},{73,201},{74,202},{75,203},{76,204},{77,205},{78,206},{79... | collective-permute-start | bytes 98312 | tf_op jit(solution)/shard_map/ppermute | solution.py:41
  116.5 11.4 %collective-permute-start.51 = (bf16[32,1024]{1,0:T(8,128)(2,1)}, bf16[32,1024]{1,0:T(8,128)(2,1)S(1)}, u32[]{:S(2)}, u32[]{:S(2)}) collective-permute-start(bf16[32,1024]{1,0:T(8,128)(2,1)} %copy-done.26), channel_id=1, source_target_pairs={{128,64},{129,65},{130,66},{131,67},{132,68},{133,69},{134,70},{13... | collective-permute-start | bytes 196616 | tf_op jit(solution)/shard_map/ppermute | solution.py:41
  117.2 10.8 %collective-permute-start.52 = (bf16[32,1024]{1,0:T(8,128)(2,1)}, bf16[32,1024]{1,0:T(8,128)(2,1)S(1)}, u32[]{:S(2)}, u32[]{:S(2)}) collective-permute-start(bf16[32,1024]{1,0:T(8,128)(2,1)} %copy-done.26), channel_id=1, source_target_pairs={{192,64},{193,65},{194,66},{195,67},{196,68},{197,69},{198,70},{19... | collective-permute-start | bytes 196616 | tf_op jit(solution)/shard_map/ppermute | solution.py:41
  128.7 6.9 %collective-permute-start.34 = (bf16[32,512]{1,0:T(8,128)(2,1)S(1)}, bf16[32,512]{1,0:T(8,128)(2,1)S(1)}, u32[]{:S(2)}, u32[]{:S(2)}) collective-permute-start(bf16[32,512]{1,0:T(8,128)(2,1)S(1)} %add_add_fusion.1), channel_id=1, source_target_pairs={{128,130},{129,131},{130,128},{131,129},{132,134},{133,135},{134,1... | collective-permute-start | bytes 98312 | tf_op jit(solution)/shard_map/cond/branch_1_fun/ppermute | solution.py:41
  135.6 6.1 %collective-permute-start.35 = (bf16[32,1024]{1,0:T(8,128)(2,1)S(1)}, bf16[32,1024]{1,0:T(8,128)(2,1)S(1)}, u32[]{:S(2)}, u32[]{:S(2)}) collective-permute-start(bf16[32,1024]{1,0:T(8,128)(2,1)S(1)} %pad_maximum_fusion.17), channel_id=1, source_target_pairs={{128,129},{129,128},{130,131},{131,130},{132,133},{133,132},{134,1... | collective-permute-start | bytes 196616 | tf_op jit(solution)/shard_map/cond/branch_1_fun/ppermute | solution.py:41
  142.1 18.4 %collective-permute-start.38 = (bf16[32,2048]{1,0:T(8,128)(2,1)S(1)}, bf16[32,2048]{1,0:T(8,128)(2,1)S(1)}, u32[]{:S(2)}, u32[]{:S(2)}) collective-permute-start(bf16[32,2048]{1,0:T(8,128)(2,1)S(1)} %get-tuple-element.252), channel_id=1, source_target_pairs={{128,144},{129,145},{130,146},{131,147},{132,148},{133,149},{134,1... | collective-permute-start | bytes 393224 | tf_op jit(solution)/shard_map/cond/branch_1_fun/ppermute | solution.py:41
  144.0 16.5 %collective-permute-start.39 = (bf16[32,2048]{1,0:T(8,128)(2,1)S(1)}, bf16[32,2048]{1,0:T(8,128)(2,1)S(1)}, u32[]{:S(2)}, u32[]{:S(2)}) collective-permute-start(bf16[32,2048]{1,0:T(8,128)(2,1)S(1)} %get-tuple-element.252), channel_id=1, source_target_pairs={{128,160},{129,161},{130,162},{131,163},{132,164},{133,165},{134,1... | collective-permute-start | bytes 393224 | tf_op jit(solution)/shard_map/cond/branch_1_fun/ppermute | solution.py:41
  147.9 12.6 %collective-permute-start.40 = (bf16[32,2048]{1,0:T(8,128)(2,1)S(1)}, bf16[32,2048]{1,0:T(8,128)(2,1)S(1)}, u32[]{:S(2)}, u32[]{:S(2)}) collective-permute-start(bf16[32,2048]{1,0:T(8,128)(2,1)S(1)} %get-tuple-element.252), channel_id=1, source_target_pairs={{128,176},{129,177},{130,178},{131,179},{132,180},{133,181},{134,1... | collective-permute-start | bytes 393224 | tf_op jit(solution)/shard_map/cond/branch_1_fun/ppermute | solution.py:41
  153.5 9.3 %collective-permute-start.37 = (bf16[256,512]{1,0:T(8,128)(2,1)}, bf16[256,512]{1,0:T(8,128)(2,1)S(1)}, u32[]{:S(2)}, u32[]{:S(2)}) collective-permute-start(bf16[256,512]{1,0:T(8,128)(2,1)} %get-tuple-element.194), channel_id=1, source_target_pairs={{128,129},{129,128},{130,131},{131,130},{132,133},{133,132},{134,1... | collective-permute-start | bytes 786440 | tf_op jit(solution)/shard_map/cond/branch_1_fun/ppermute | solution.py:41
  156.7 11.8 %collective-permute-start.36 = (bf16[257,1024]{1,0:T(8,128)(2,1)S(1)}, bf16[257,1024]{1,0:T(8,128)(2,1)S(1)}, u32[]{:S(2)}, u32[]{:S(2)}) collective-permute-start(bf16[257,1024]{1,0:T(8,128)(2,1)S(1)} %pad_maximum_fusion.13), channel_id=1, source_target_pairs={{128,129},{129,128},{130,131},{131,130},{132,133},{133,132},{134,1... | collective-permute-start | bytes 1579016 | tf_op jit(solution)/shard_map/cond/branch_1_fun/ppermute | solution.py:41
  160.6 9.4 %collective-permute-start.41 = (bf16[128,2048]{1,0:T(8,128)(2,1)S(1)}, bf16[128,2048]{1,0:T(8,128)(2,1)S(1)}, u32[]{:S(2)}, u32[]{:S(2)}) collective-permute-start(bf16[128,2048]{1,0:T(8,128)(2,1)S(1)} %pad_maximum_fusion.14), channel_id=1, source_target_pairs={{128,132},{129,133},{130,134},{131,135},{132,128},{133,129},{134,1... | collective-permute-start | bytes 1572872 | tf_op jit(solution)/shard_map/cond/branch_1_fun/ppermute | solution.py:41
  170.1 1.6 copy-start.4
  172.4 1.6 copy-start.11
  174.7 21.6 %copy-start.29 = (f32[256]{0:T(256)S(1)}, f32[256]{0:T(256)}, u32[]{:S(2)}) copy-start(f32[256]{0:T(256)} %get-tuple-element.207) | copy-start | bytes 3076
  174.7 21.6 %copy-start.30 = (f32[256,1]{0,1:T(1,128)S(1)}, f32[256,1]{0,1:T(1,128)}, u32[]{:S(2)}) copy-start(f32[256,1]{0,1:T(1,128)} %get-tuple-element.208) | copy-start | bytes 3076
  174.7 21.7 %copy-start.16 = (bf16[256,512]{1,0:T(8,128)(2,1)S(1)}, bf16[256,512]{1,0:T(8,128)(2,1)}, u32[]{:S(2)}) copy-start(bf16[256,512]{1,0:T(8,128)(2,1)} %get-tuple-element.209) | copy-start | bytes 786436
  174.8 13.8 %collective-permute-start.42 = (bf16[256,512]{1,0:T(8,128)(2,1)S(1)}, bf16[256,512]{1,0:T(8,128)(2,1)S(1)}, u32[]{:S(2)}, u32[]{:S(2)}) collective-permute-start(bf16[256,512]{1,0:T(8,128)(2,1)S(1)} %get-tuple-element.294), channel_id=1, source_target_pairs={{128,129},{129,128},{130,131},{131,130},{132,133},{133,132},{134,1... | collective-permute-start | bytes 786440 | tf_op jit(solution)/shard_map/cond/branch_1_fun/ppermute | solution.py:41
  178.3 13.7 %collective-permute-start.44 = (bf16[257,512]{1,0:T(8,128)(2,1)S(1)}, bf16[257,512]{1,0:T(8,128)(2,1)S(1)}, u32[]{:S(2)}, u32[]{:S(2)}) collective-permute-start(bf16[257,512]{1,0:T(8,128)(2,1)S(1)} %pad_maximum_fusion.15), channel_id=1, source_target_pairs={{128,130},{129,131},{130,128},{131,129},{132,134},{133,135},{134,1... | collective-permute-start | bytes 789512 | tf_op jit(solution)/shard_map/cond/branch_1_fun/ppermute | solution.py:41
  188.6 9.9 %collective-permute-start.43 = (bf16[256,512]{1,0:T(8,128)(2,1)S(1)}, bf16[256,512]{1,0:T(8,128)(2,1)S(1)}, u32[]{:S(2)}, u32[]{:S(2)}) collective-permute-start(bf16[256,512]{1,0:T(8,128)(2,1)S(1)} %get-tuple-element.202), channel_id=1, source_target_pairs={{128,129},{129,128},{130,131},{131,130},{132,133},{133,132},{134,1... | collective-permute-start | bytes 786440 | tf_op jit(solution)/shard_map/cond/branch_1_fun/ppermute | solution.py:41
  192.2 12.0 %collective-permute-start.45 = (bf16[256,512]{1,0:T(8,128)(2,1)S(1)}, bf16[256,512]{1,0:T(8,128)(2,1)S(1)}, u32[]{:S(2)}, u32[]{:S(2)}) collective-permute-start(bf16[256,512]{1,0:T(8,128)(2,1)S(1)} %add_convert_fusion.5), channel_id=1, source_target_pairs={{128,130},{129,131},{130,128},{131,129},{132,134},{133,135},{134,1... | collective-permute-start | bytes 786440 | tf_op jit(solution)/shard_map/cond/branch_1_fun/ppermute | solution.py:41
  205.0 18.5 %copy-start.1 = (bf16[256,512]{1,0:T(8,128)(2,1)S(1)}, bf16[256,512]{1,0:T(8,128)(2,1)}, u32[]{:S(2)}) copy-start(bf16[256,512]{1,0:T(8,128)(2,1)} %param.15) | copy-start | bytes 786436
  205.0 17.8 %collective-permute-start.57 = (bf16[256,512]{1,0:T(8,128)(2,1)}, bf16[256,512]{1,0:T(8,128)(2,1)S(1)}, u32[]{:S(2)}, u32[]{:S(2)}) collective-permute-start(bf16[256,512]{1,0:T(8,128)(2,1)} %get-tuple-element.235), channel_id=1, source_target_pairs={{128,132},{129,133},{130,134},{131,135},{132,136},{133,137},{134,1... | collective-permute-start | bytes 786440 | tf_op jit(solution)/shard_map/ppermute | solution.py:41

commit v4 on v3

--- a/solution.py
+++ b/solution.py
@@ -243,22 +243,22 @@
     w_q, w_k, w_v = (jnp.concatenate([w[:, i] for w in turned], axis=0) for i in range(3))
     w_o = jnp.concatenate([lax.dynamic_slice_in_dim(w_out[0], o * width, width, 1) for o in order], axis=1)
 
-    a_values = a_all[:rows].astype(f32)
-    a_inverse = inverse_rms(a_values)
-    a_normed = scale_rows(a_values, a_inverse, gain)
+    def normed_a():
+        values = a_all[:rows].astype(f32)
+        return scale_rows(values, inverse_rms(values), gain)
     def project(normed, source):
         return mm(normed, w_q).astype(bf16), mm(source, w_k).astype(bf16), mm(source, w_v).astype(bf16)
 
     def enc_phase1(_):
         b_last = swap_t(b_far, 1, encoders)
+        c_far = swap_t(cot_shard, 2, encoders)
+        a_normed = normed_a()
         out = attend_out(*project(a_normed, a_normed), w_o).astype(bf16)
         out, b_last = tie(out, b_last)
-        summed, _, _ = scatter(out, None, encoders)
+        summed, _, c_far = scatter(out, None, encoders, c_far)
         enc_y = (fwd_shard.astype(f32) + summed).astype(bf16)
         blocks = enc_y.reshape(NX, NC, part, width)
-        passed, c_shard = tie(swap_core(blocks[:, 0], top_row), cot_shard)
-        blocks = jnp.where(core == 1, blocks[:, 1], passed)
-        c_far = swap_t(c_shard, 2, encoders)
+        blocks = jnp.where(core == 1, blocks[:, 1], swap_core(blocks[:, 0], top_row))
         top = blocks[NX - 1]
         for k in range(1, NX):
             sent = move(
@@ -269,12 +269,11 @@
 
     def dec_phase1(_):
         b_last = swap_t(b_far, 1, decoders)
-        q = mm(a_normed, w_q).astype(bf16)
-        saved_rows, q = tie(scale_rows(saved, inverse_rms(saved), final), q)
+        saved_rows = scale_rows(saved, inverse_rms(saved), final)
         saved_half = jnp.concatenate([saved_rows] + [swap_x(saved_rows, k, decoders) for k in range(1, NX)], axis=0)
         saved_half, b_last = tie(saved_half, b_last)
         saved_normed = jnp.concatenate([saved_half, swap_core(saved_half, decoders)], axis=0)
-        k, v = mm(saved_normed, w_k).astype(bf16), mm(saved_normed, w_v).astype(bf16)
+        q, k, v = project(normed_a(), saved_normed)
         c_shard, b_last = tie(fwd_shard, b_last)
         c_far, c_near = swap_t(c_shard, 2, decoders), swap_t(c_shard, 1, decoders)
         b_full = jnp.concatenate([b_three, b_last], axis=1)
@@ -351,6 +350,8 @@
     def dec_phase2(_):
         all_top = jnp.concatenate([top, swap_t(top, 2, decoders)], axis=1)
         all_top = jnp.concatenate([all_top, swap_t(all_top, 1, decoders)], axis=1).astype(f32)
+        a_values = a_all[:rows].astype(f32)
+        a_inverse = inverse_rms(a_values)
         row_part = jnp.sum(gain * dn.astype(f32) * a_values, axis=-1)
         dn_tied, all_top, c_last = lax.optimization_barrier((dn, all_top, c_far))
         c_last = swap_t(c_last, 1, decoders)

time: 225 us -> 224 us (level)
    convert_element_type x1 -> x0, other arithmetic: 2.74 us -> none  [body(): a_values = a_all[:rows].astype(f32)]
    concatenate x0 -> x1, other arithmetic: none -> 2.32 us  [body(): a_all = jnp.concatenate([a_shard, a_far, a_near, a_last], axis=1)]
    convert_element_type x2 -> x1, other arithmetic: 2.39 us -> 0.1 us  [scale_rows(): return (values * inverse * gain_row).astype(bf16)]
    reduce_sum x4 -> x5, other arithmetic: 3.77 us -> 5.12 us  [inverse_rms(): jnp.mean(values * values, axis=-1, keepdims=True) + epsilon]
  transfers between devices with their start and end apart: 36 -> 36, of which waited for: 19 -> 17; matrix products, arithmetic and copies ran while one was open for 14% -> 15% of each run, Pallas kernels for 0% -> 0%
where the time goes in v4:
time: 224 us; the launch traced here: 222 us
  starting transfers between devices  90.1 us (40%)
  waiting for transfers between devices  75 us (33%)
  other arithmetic  26.4 us (12%)
  matrix products  14.6 us (7%)
  local copies, waits for them, and re-layouts  14.1 us (6%)
    ppermute x36, starting transfers between devices, move(): return lax.ppermute(value, ('section', 'tensor'), pairs)  90.1 us
    ppermute x36, waiting for transfers between devices, move(): return lax.ppermute(value, ('section', 'tensor'), pairs)  75 us
    dot_general x11, matrix products, mm(): return jnp.dot(a, b, preferred_element_type=f32)  8.27 us
    dot_general x10, matrix products, mm_t(): lax.dot_general(a, b, (((1,), (1,)), ((), ())), preferred_element_type=f32)  5.57 us
    reduce_sum x5, other arithmetic, inverse_rms(): jnp.mean(values * values, axis=-1, keepdims=True) + epsilon  5.12 us
  transfers between devices with their start and end apart: 36, of which 17 were waited for; matrix products, arithmetic and copies ran while one was open for 15% of the time, Pallas kernels for 0%

profile of v4, /device:TPU:24, one launch (start us, length us, event | category | flops | bytes accessed | tf_op | source)
XLA Modules:
  0.0 222.1 jit_solution(15431319341280328651)
XLA Ops:
  2.7 1.4 pad_maximum_fusion.25
  4.2 1.9 collective-permute-start.47
  6.1 3.3 %collective-permute-start.46 = (bf16[290,512]{1,0:T(8,128)(2,1)}, bf16[290,512]{1,0:T(8,128)(2,1)}, u32[]{:S(2)}, u32[]{:S(2)}) collective-permute-start(bf16[290,512]{1,0:T(8,128)(2,1)} %pad_maximum_fusion.25), channel_id=1, source_target_pairs={{0,2},{1,3},{2,0},{3,1},{4,6},{5,7},{6,4},{7,5},{8,10},{9,11},{10,... | collective-permute-start | bytes 890888 | tf_op jit(solution)/shard_map/ppermute | solution.py:41
  9.4 3.2 %dynamic-slice_bitcast_fusion.3 = (bf16[512,3,512]{2,0,1:T(8,128)(2,1)S(1)}, bf16[512,3,512]{2,0,1:T(8,128)(2,1)S(1)}, bf16[512,3,512]{2,0,1:T(8,128)(2,1)S(1)}, bf16[512,3,512]{2,0,1:T(8,128)(2,1)S(1)}) fusion(bf16[1,2048,3,512]{3,1,2,0:T(8,128)(2,1)} %param.18, s32[]{:T(128)S(6)} %select_n.96, s32[]{:T(128)S(6)} %select_n.97, s32[]{:T(128)S(6)} %select_n.99, ...), kind=kLoop, calls=%fused_computation.310 | loop fusion | bytes 12582928 | tf_op jit(solution)/shard_map/dynamic_slice | solution.py:242
  13.0 1.5 pad_maximum_fusion.22
  14.7 1.4 copy-done.18
  16.4 1.5 pad_maximum_fusion.19
  17.8 2.0 collective-permute-done.47
  19.8 3.5 %collective-permute-done.46 = bf16[290,512]{1,0:T(8,128)(2,1)} collective-permute-done((bf16[290,512]{1,0:T(8,128)(2,1)}, bf16[290,512]{1,0:T(8,128)(2,1)}, u32[]{:S(2)}, u32[]{:S(2)}) %collective-permute-start.46) | collective-permute-done | bytes 296992 | tf_op jit(solution)/shard_map/ppermute | solution.py:41
  23.3 2.7 %collective-permute-start.50 = (bf16[256,512]{1,0:T(8,128)(2,1)S(1)}, bf16[256,512]{1,0:T(8,128)(2,1)}, u32[]{:S(2)}, u32[]{:S(2)}) collective-permute-start(bf16[256,512]{1,0:T(8,128)(2,1)S(1)} %get-tuple-element.226), channel_id=1, source_target_pairs={{0,1},{1,0},{2,3},{3,2},{4,5},{5,4},{6,7},{7,6},{8,9},{9,8},{10,11... | collective-permute-start | bytes 786440 | tf_op jit(solution)/shard_map/ppermute | solution.py:41
  26.1 1.7 pad_maximum_fusion.21
  27.7 6.6 %collective-permute-done.49 = bf16[256,512]{1,0:T(8,128)(2,1)S(1)} collective-permute-done((bf16[256,512]{1,0:T(8,128)(2,1)S(1)}, bf16[256,512]{1,0:T(8,128)(2,1)S(1)}, u32[]{:S(2)}, u32[]{:S(2)}) %collective-permute-start.49) | collective-permute-done | bytes 262176 | tf_op jit(solution)/shard_map/ppermute | solution.py:41
  35.1 1.4 collective-permute-done.50
  37.7 3.2 %collective-permute-done.48 = bf16[290,512]{1,0:T(8,128)(2,1)} collective-permute-done((bf16[290,512]{1,0:T(8,128)(2,1)}, bf16[290,512]{1,0:T(8,128)(2,1)}, u32[]{:S(2)}, u32[]{:S(2)}) %collective-permute-start.48) | collective-permute-done | bytes 296992 | tf_op jit(solution)/shard_map/ppermute | solution.py:41
  40.9 2.3 %pad_maximum_fusion.23 = bf16[290,2048]{1,0:T(8,128)(2,1)} fusion(bf16[290,512]{1,0:T(8,128)(2,1)} %collective-permute-done.48, bf16[290,512]{1,0:T(8,128)(2,1)} %collective-permute-done.47, bf16[290,512]{1,0:T(8,128)(2,1)} %collective-permute-done.46, bf16[1,512]{1,0:T(2,128)(2,1)S(1)} %broadcast_in_dim.6, bf16[1,512]{1,0:T(2,128)(2,1)S(1)} %copy-done.26, ...), kind=kLoop, calls=%fused_computation.311 | loop fusion | flops 8314880 | bytes 2375680 | tf_op jit(solution)/shard_map/concatenate | solution.py:234
  44.9 64.3 %conditional.4 = (bf16[256,512]{1,0:T(8,128)(2,1)}, bf16[32,512]{1,0:T(8,128)(2,1)}, bf16[256,1024]{1,0:T(8,128)(2,1)}, bf16[256,512]{1,0:T(8,128)(2,1)}, bf16[2...) conditional(s32[]{:T(128)} %convert_element_type.372, (bf16[256,512]{1,0:T(8,128)(2,1)S(1)}, ...), branch_computations={%region_0.7_spmd, %region_7.11_spmd} | conditional | flops 4110056704 | bytes 64717868 | solution.py:293
  45.1 3.4 %collective-permute-start = (bf16[32,2048]{1,0:T(8,128)(2,1)S(1)}, bf16[32,2048]{1,0:T(8,128)(2,1)S(1)}, u32[]{:S(2)}, u32[]{:S(2)}) collective-permute-start(bf16[32,2048]{1,0:T(8,128)(2,1)S(1)} %multiply_convert_fusion.2), channel_id=1, source_target_pairs={{128,144},{129,145},{130,146},{131,147},{132,148},{133,149},{134,1... | collective-permute-start | bytes 393224 | tf_op jit(solution)/shard_map/cond/branch_0_fun/ppermute | solution.py:41
  48.5 4.6 %collective-permute-start.1 = (bf16[32,2048]{1,0:T(8,128)(2,1)S(1)}, bf16[32,2048]{1,0:T(8,128)(2,1)S(1)}, u32[]{:S(2)}, u32[]{:S(2)}) collective-permute-start(bf16[32,2048]{1,0:T(8,128)(2,1)S(1)} %multiply_convert_fusion.2), channel_id=1, source_target_pairs={{128,160},{129,161},{130,162},{131,163},{132,164},{133,165},{134,1... | collective-permute-start | bytes 393224 | tf_op jit(solution)/shard_map/cond/branch_0_fun/ppermute | solution.py:41
  53.2 2.4 %collective-permute-start.2 = (bf16[32,2048]{1,0:T(8,128)(2,1)S(1)}, bf16[32,2048]{1,0:T(8,128)(2,1)S(1)}, u32[]{:S(2)}, u32[]{:S(2)}) collective-permute-start(bf16[32,2048]{1,0:T(8,128)(2,1)S(1)} %multiply_convert_fusion.2), channel_id=1, source_target_pairs={{128,176},{129,177},{130,178},{131,179},{132,180},{133,181},{134,1... | collective-permute-start | bytes 393224 | tf_op jit(solution)/shard_map/cond/branch_0_fun/ppermute | solution.py:41
  55.6 3.2 %collective-permute-start.3 = (bf16[256,512]{1,0:T(8,128)(2,1)S(1)}, bf16[256,512]{1,0:T(8,128)(2,1)S(1)}, u32[]{:S(2)}, u32[]{:S(2)}) collective-permute-start(bf16[256,512]{1,0:T(8,128)(2,1)S(1)} %get-tuple-element.131), channel_id=1, source_target_pairs={{128,129},{129,128},{130,131},{131,130},{132,133},{133,132},{134,1... | collective-permute-start | bytes 786440 | tf_op jit(solution)/shard_map/cond/branch_0_fun/ppermute | solution.py:41
  58.8 1.5 fusion.1
  61.3 2.5 %collective-permute-done.3 = bf16[256,512]{1,0:T(8,128)(2,1)S(1)} collective-permute-done((bf16[256,512]{1,0:T(8,128)(2,1)S(1)}, bf16[256,512]{1,0:T(8,128)(2,1)S(1)}, u32[]{:S(2)}, u32[]{:S(2)}) %collective-permute-start.3) | collective-permute-done | bytes 262176 | tf_op jit(solution)/shard_map/cond/branch_0_fun/ppermute | solution.py:41
  63.8 1.9 collective-permute-start.4
  65.8 2.1 convolution_convert_fusion.4
  73.7 2.4 %collective-permute-start.5 = (bf16[128,2048]{1,0:T(8,128)(2,1)S(1)}, bf16[128,2048]{1,0:T(8,128)(2,1)S(1)}, u32[]{:S(2)}, u32[]{:S(2)}) collective-permute-start(bf16[128,2048]{1,0:T(8,128)(2,1)S(1)} %slice.389), channel_id=1, source_target_pairs={{128,132},{129,133},{130,134},{131,135},{132,128},{133,129},{134,1... | collective-permute-start | bytes 1572872 | tf_op jit(solution)/shard_map/cond/branch_0_fun/ppermute | solution.py:41
  77.4 3.2 %collective-permute-start.10 = (bf16[256,512]{1,0:T(8,128)(2,1)S(1)}, bf16[256,512]{1,0:T(8,128)(2,1)S(1)}, u32[]{:S(2)}, u32[]{:S(2)}) collective-permute-start(bf16[256,512]{1,0:T(8,128)(2,1)S(1)} %get-tuple-element.139), channel_id=1, source_target_pairs={{128,129},{129,128},{130,131},{131,130},{132,133},{133,132},{134,1... | collective-permute-start | bytes 786440 | tf_op jit(solution)/shard_map/cond/branch_0_fun/ppermute | solution.py:41
  80.6 5.4 %collective-permute-start.9 = (bf16[256,512]{1,0:T(8,128)(2,1)S(1)}, bf16[256,512]{1,0:T(8,128)(2,1)}, u32[]{:S(2)}, u32[]{:S(2)}) collective-permute-start(bf16[256,512]{1,0:T(8,128)(2,1)S(1)} %get-tuple-element.139), channel_id=1, source_target_pairs={{128,130},{129,131},{130,128},{131,129},{132,134},{133,135},{134,1... | collective-permute-start | bytes 786440 | tf_op jit(solution)/shard_map/cond/branch_0_fun/ppermute | solution.py:41
  86.6 2.2 collective-permute-start.6
  88.8 5.9 %collective-permute-start.7 = (bf16[32,2048]{1,0:T(8,128)(2,1)S(1)}, bf16[32,2048]{1,0:T(8,128)(2,1)S(1)}, u32[]{:S(2)}, u32[]{:S(2)}) collective-permute-start(bf16[32,2048]{1,0:T(8,128)(2,1)S(1)} %get-tuple-element.254), channel_id=1, source_target_pairs={{128,160},{129,161},{130,162},{131,163},{132,164},{133,165},{134,1... | collective-permute-start | bytes 393224 | tf_op jit(solution)/shard_map/cond/branch_0_fun/ppermute | solution.py:41
  94.6 2.4 %collective-permute-start.8 = (bf16[32,2048]{1,0:T(8,128)(2,1)S(1)}, bf16[32,2048]{1,0:T(8,128)(2,1)S(1)}, u32[]{:S(2)}, u32[]{:S(2)}) collective-permute-start(bf16[32,2048]{1,0:T(8,128)(2,1)S(1)} %get-tuple-element.253), channel_id=1, source_target_pairs={{128,176},{129,177},{130,178},{131,179},{132,180},{133,181},{134,1... | collective-permute-start | bytes 393224 | tf_op jit(solution)/shard_map/cond/branch_0_fun/ppermute | solution.py:41
  97.0 1.8 convolution_convert_fusion
  98.8 3.9 %collective-permute-done.8 = bf16[32,2048]{1,0:T(8,128)(2,1)S(1)} collective-permute-done((bf16[32,2048]{1,0:T(8,128)(2,1)S(1)}, bf16[32,2048]{1,0:T(8,128)(2,1)S(1)}, u32[]{:S(2)}, u32[]{:S(2)}) %collective-permute-start.8) | collective-permute-done | bytes 131104 | tf_op jit(solution)/shard_map/cond/branch_0_fun/ppermute | solution.py:41
  102.8 2.2 %collective-permute-start.11 = (bf16[32,1024]{1,0:T(8,128)(2,1)S(1)}, bf16[32,1024]{1,0:T(8,128)(2,1)S(1)}, u32[]{:S(2)}, u32[]{:S(2)}) collective-permute-start(bf16[32,1024]{1,0:T(8,128)(2,1)S(1)} %slice.638), channel_id=1, source_target_pairs={{128,129},{129,128},{130,131},{131,130},{132,133},{133,132},{134,1... | collective-permute-start | bytes 196616 | tf_op jit(solution)/shard_map/cond/branch_0_fun/ppermute | solution.py:41
  105.9 3.1 %collective-permute-done.11 = bf16[32,1024]{1,0:T(8,128)(2,1)S(1)} collective-permute-done((bf16[32,1024]{1,0:T(8,128)(2,1)S(1)}, bf16[32,1024]{1,0:T(8,128)(2,1)S(1)}, u32[]{:S(2)}, u32[]{:S(2)}) %collective-permute-start.11) | collective-permute-done | bytes 65568 | tf_op jit(solution)/shard_map/cond/branch_0_fun/ppermute | solution.py:41
  110.6 1.9 collective-permute-start.52
  113.2 1.3 collective-permute-start.55
  114.5 1.3 collective-permute-start.56
  115.8 1.3 slice.458
  117.1 12.3 %collective-permute-done.55 = bf16[32,512]{1,0:T(8,128)(2,1)} collective-permute-done((bf16[32,512]{1,0:T(8,128)(2,1)}, bf16[32,512]{1,0:T(8,128)(2,1)}, u32[]{:S(2)}, u32[]{:S(2)}) %collective-permute-start.55) | collective-permute-done | bytes 32800 | tf_op jit(solution)/shard_map/ppermute | solution.py:41
  129.4 77.0 %conditional.5 = (bf16[256,512]{1,0:T(8,128)(2,1)}, f32[256,512]{1,0:T(8,128)S(1)}, f32[256,1]{0,1:T(1,128)S(1)}, f32[256,1]{0,1:T(1,128)}, f32[256,512]{1,0:T(8,128)S(1)}, /*index=5*/f32[256,1]{0,1:T(1,128)S(1)}) conditional(s32[]{:T(128)} %convert_element_type.371, (bf16[256,1024]{1,0:T(8,128)(2,1)}, bf16[256,1536]{1,0:T(8,128)(2,1)S(1)}, ...), branch_computations={%region_11.20_spmd, %region_20.27_spmd} | conditional | flops 4127371008 | bytes 97863712
  130.2 1.9 collective-permute-start.34
  132.2 2.1 fusion.119
  134.3 2.9 %collective-permute-done.34 = bf16[32,512]{1,0:T(8,128)(2,1)S(1)} collective-permute-done((bf16[32,512]{1,0:T(8,128)(2,1)S(1)}, bf16[32,512]{1,0:T(8,128)(2,1)S(1)}, u32[]{:S(2)}, u32[]{:S(2)}) %collective-permute-start.34) | collective-permute-done | bytes 32800 | tf_op jit(solution)/shard_map/cond/branch_1_fun/ppermute | solution.py:41
  137.1 2.2 %collective-permute-start.35 = (bf16[32,1024]{1,0:T(8,128)(2,1)S(1)}, bf16[32,1024]{1,0:T(8,128)(2,1)S(1)}, u32[]{:S(2)}, u32[]{:S(2)}) collective-permute-start(bf16[32,1024]{1,0:T(8,128)(2,1)S(1)} %pad_maximum_fusion.17), channel_id=1, source_target_pairs={{128,129},{129,128},{130,131},{131,130},{132,133},{133,132},{134,1... | collective-permute-start | bytes 196616 | tf_op jit(solution)/shard_map/cond/branch_1_fun/ppermute | solution.py:41
  139.4 3.9 %collective-permute-done.35 = bf16[32,1024]{1,0:T(8,128)(2,1)S(1)} collective-permute-done((bf16[32,1024]{1,0:T(8,128)(2,1)S(1)}, bf16[32,1024]{1,0:T(8,128)(2,1)S(1)}, u32[]{:S(2)}, u32[]{:S(2)}) %collective-permute-start.35) | collective-permute-done | bytes 65568 | tf_op jit(solution)/shard_map/cond/branch_1_fun/ppermute | solution.py:41
  143.6 1.9 collective-permute-start.38
  145.5 3.8 %collective-permute-start.39 = (bf16[32,2048]{1,0:T(8,128)(2,1)S(1)}, bf16[32,2048]{1,0:T(8,128)(2,1)S(1)}, u32[]{:S(2)}, u32[]{:S(2)}) collective-permute-start(bf16[32,2048]{1,0:T(8,128)(2,1)S(1)} %get-tuple-element.247), channel_id=1, source_target_pairs={{128,160},{129,161},{130,162},{131,163},{132,164},{133,165},{134,1... | collective-permute-start | bytes 393224 | tf_op jit(solution)/shard_map/cond/branch_1_fun/ppermute | solution.py:41
  149.2 4.8 %collective-permute-start.40 = (bf16[32,2048]{1,0:T(8,128)(2,1)S(1)}, bf16[32,2048]{1,0:T(8,128)(2,1)S(1)}, u32[]{:S(2)}, u32[]{:S(2)}) collective-permute-start(bf16[32,2048]{1,0:T(8,128)(2,1)S(1)} %get-tuple-element.247), channel_id=1, source_target_pairs={{128,176},{129,177},{130,178},{131,179},{132,180},{133,181},{134,1... | collective-permute-start | bytes 393224 | tf_op jit(solution)/shard_map/cond/branch_1_fun/ppermute | solution.py:41
  155.0 2.2 %collective-permute-start.37 = (bf16[256,512]{1,0:T(8,128)(2,1)}, bf16[256,512]{1,0:T(8,128)(2,1)S(1)}, u32[]{:S(2)}, u32[]{:S(2)}) collective-permute-start(bf16[256,512]{1,0:T(8,128)(2,1)} %get-tuple-element.194), channel_id=1, source_target_pairs={{128,129},{129,128},{130,131},{131,130},{132,133},{133,132},{134,1... | collective-permute-start | bytes 786440 | tf_op jit(solution)/shard_map/cond/branch_1_fun/ppermute | solution.py:41
  158.4 3.7 %collective-permute-start.36 = (bf16[257,1024]{1,0:T(8,128)(2,1)S(1)}, bf16[257,1024]{1,0:T(8,128)(2,1)S(1)}, u32[]{:S(2)}, u32[]{:S(2)}) collective-permute-start(bf16[257,1024]{1,0:T(8,128)(2,1)S(1)} %pad_maximum_fusion.13), channel_id=1, source_target_pairs={{128,129},{129,128},{130,131},{131,130},{132,133},{133,132},{134,1... | collective-permute-start | bytes 1579016 | tf_op jit(solution)/shard_map/cond/branch_1_fun/ppermute | solution.py:41
  162.2 2.2 collective-permute-start.41
  164.5 1.2 fusion.120
  165.7 1.7 convolution_convert_fusion.30
  167.4 2.3 %collective-permute-done.36 = bf16[257,1024]{1,0:T(8,128)(2,1)S(1)} collective-permute-done((bf16[257,1024]{1,0:T(8,128)(2,1)S(1)}, bf16[257,1024]{1,0:T(8,128)(2,1)S(1)}, u32[]{:S(2)}, u32[]{:S(2)}) %collective-permute-start.36) | collective-permute-done | bytes 526368 | tf_op jit(solution)/shard_map/cond/branch_1_fun/ppermute | solution.py:41
  176.0 3.7 %collective-permute-start.42 = (bf16[256,512]{1,0:T(8,128)(2,1)S(1)}, bf16[256,512]{1,0:T(8,128)(2,1)S(1)}, u32[]{:S(2)}, u32[]{:S(2)}) collective-permute-start(bf16[256,512]{1,0:T(8,128)(2,1)S(1)} %get-tuple-element.289), channel_id=1, source_target_pairs={{128,129},{129,128},{130,131},{131,130},{132,133},{133,132},{134,1... | collective-permute-start | bytes 786440 | tf_op jit(solution)/shard_map/cond/branch_1_fun/ppermute | solution.py:41
  179.7 2.4 %collective-permute-start.44 = (bf16[257,512]{1,0:T(8,128)(2,1)S(1)}, bf16[257,512]{1,0:T(8,128)(2,1)S(1)}, u32[]{:S(2)}, u32[]{:S(2)}) collective-permute-start(bf16[257,512]{1,0:T(8,128)(2,1)S(1)} %pad_maximum_fusion.15), channel_id=1, source_target_pairs={{128,130},{129,131},{130,128},{131,129},{132,134},{133,135},{134,1... | collective-permute-start | bytes 789512 | tf_op jit(solution)/shard_map/cond/branch_1_fun/ppermute | solution.py:41
  182.1 6.1 %collective-permute-done.42 = bf16[256,512]{1,0:T(8,128)(2,1)S(1)} collective-permute-done((bf16[256,512]{1,0:T(8,128)(2,1)S(1)}, bf16[256,512]{1,0:T(8,128)(2,1)S(1)}, u32[]{:S(2)}, u32[]{:S(2)}) %collective-permute-start.42) | collective-permute-done | bytes 262176 | tf_op jit(solution)/shard_map/cond/branch_1_fun/ppermute | solution.py:41
  188.3 2.6 %collective-permute-start.43 = (bf16[256,512]{1,0:T(8,128)(2,1)S(1)}, bf16[256,512]{1,0:T(8,128)(2,1)S(1)}, u32[]{:S(2)}, u32[]{:S(2)}) collective-permute-start(bf16[256,512]{1,0:T(8,128)(2,1)S(1)} %get-tuple-element.202), channel_id=1, source_target_pairs={{128,129},{129,128},{130,131},{131,130},{132,133},{133,132},{134,1... | collective-permute-start | bytes 786440 | tf_op jit(solution)/shard_map/cond/branch_1_fun/ppermute | solution.py:41
  190.9 2.4 %collective-permute-done.44 = bf16[257,512]{1,0:T(8,128)(2,1)S(1)} collective-permute-done((bf16[257,512]{1,0:T(8,128)(2,1)S(1)}, bf16[257,512]{1,0:T(8,128)(2,1)S(1)}, u32[]{:S(2)}, u32[]{:S(2)}) %collective-permute-start.44) | collective-permute-done | bytes 263200 | tf_op jit(solution)/shard_map/cond/branch_1_fun/ppermute | solution.py:41
  193.4 3.1 %collective-permute-start.45 = (bf16[256,512]{1,0:T(8,128)(2,1)S(1)}, bf16[256,512]{1,0:T(8,128)(2,1)S(1)}, u32[]{:S(2)}, u32[]{:S(2)}) collective-permute-start(bf16[256,512]{1,0:T(8,128)(2,1)S(1)} %add_convert_fusion.5), channel_id=1, source_target_pairs={{128,130},{129,131},{130,128},{131,129},{132,134},{133,135},{134,1... | collective-permute-start | bytes 786440 | tf_op jit(solution)/shard_map/cond/branch_1_fun/ppermute | solution.py:41
  198.0 7.6 %collective-permute-done.45 = bf16[256,512]{1,0:T(8,128)(2,1)S(1)} collective-permute-done((bf16[256,512]{1,0:T(8,128)(2,1)S(1)}, bf16[256,512]{1,0:T(8,128)(2,1)S(1)}, u32[]{:S(2)}, u32[]{:S(2)}) %collective-permute-start.45) | collective-permute-done | bytes 262176 | tf_op jit(solution)/shard_map/cond/branch_1_fun/ppermute | solution.py:41
  206.4 2.0 collective-permute-start.57
  209.1 1.9 fusion.147
  211.0 10.4 %collective-permute-done.57 = bf16[256,512]{1,0:T(8,128)(2,1)S(1)} collective-permute-done((bf16[256,512]{1,0:T(8,128)(2,1)}, bf16[256,512]{1,0:T(8,128)(2,1)S(1)}, u32[]{:S(2)}, u32[]{:S(2)}) %collective-permute-start.57) | collective-permute-done | bytes 262176 | tf_op jit(solution)/shard_map/ppermute | solution.py:41
  (147 shorter events, 31.4 us)
Async XLA Ops:
  0.6 1.0 copy-start
  4.2 15.6 %collective-permute-start.47 = (bf16[290,512]{1,0:T(8,128)(2,1)}, bf16[290,512]{1,0:T(8,128)(2,1)}, u32[]{:S(2)}, u32[]{:S(2)}) collective-permute-start(bf16[290,512]{1,0:T(8,128)(2,1)} %pad_maximum_fusion.25), channel_id=1, source_target_pairs={{0,1},{1,0},{2,3},{3,2},{4,5},{5,4},{6,7},{7,6},{8,9},{9,8},{10,11... | collective-permute-start | bytes 890888 | tf_op jit(solution)/shard_map/ppermute | solution.py:41
  6.1 17.3 %collective-permute-start.46 = (bf16[290,512]{1,0:T(8,128)(2,1)}, bf16[290,512]{1,0:T(8,128)(2,1)}, u32[]{:S(2)}, u32[]{:S(2)}) collective-permute-start(bf16[290,512]{1,0:T(8,128)(2,1)} %pad_maximum_fusion.25), channel_id=1, source_target_pairs={{0,2},{1,3},{2,0},{3,1},{4,6},{5,7},{6,4},{7,5},{8,10},{9,11},{10,... | collective-permute-start | bytes 890888 | tf_op jit(solution)/shard_map/ppermute | solution.py:41
  14.5 1.6 copy-start.18
  23.3 11.0 %collective-permute-start.49 = (bf16[256,512]{1,0:T(8,128)(2,1)S(1)}, bf16[256,512]{1,0:T(8,128)(2,1)S(1)}, u32[]{:S(2)}, u32[]{:S(2)}) collective-permute-start(bf16[256,512]{1,0:T(8,128)(2,1)S(1)} %get-tuple-element.226), channel_id=1, source_target_pairs={{0,2},{1,3},{2,0},{3,1},{4,6},{5,7},{6,4},{7,5},{8,10},{9,11},{10,... | collective-permute-start | bytes 786440 | tf_op jit(solution)/shard_map/ppermute | solution.py:41
  23.3 13.1 %collective-permute-start.50 = (bf16[256,512]{1,0:T(8,128)(2,1)S(1)}, bf16[256,512]{1,0:T(8,128)(2,1)}, u32[]{:S(2)}, u32[]{:S(2)}) collective-permute-start(bf16[256,512]{1,0:T(8,128)(2,1)S(1)} %get-tuple-element.226), channel_id=1, source_target_pairs={{0,1},{1,0},{2,3},{3,2},{4,5},{5,4},{6,7},{7,6},{8,9},{9,8},{10,11... | collective-permute-start | bytes 786440 | tf_op jit(solution)/shard_map/ppermute | solution.py:41
  26.0 14.8 %collective-permute-start.48 = (bf16[290,512]{1,0:T(8,128)(2,1)}, bf16[290,512]{1,0:T(8,128)(2,1)}, u32[]{:S(2)}, u32[]{:S(2)}) collective-permute-start(bf16[290,512]{1,0:T(8,128)(2,1)} %collective-permute-done.46), channel_id=1, source_target_pairs={{0,1},{1,0},{2,3},{3,2},{4,5},{5,4},{6,7},{7,6},{8,9},{9,8},{10,11... | collective-permute-start | bytes 890888 | tf_op jit(solution)/shard_map/ppermute | solution.py:41
  26.1 14.8 %copy-start.26 = (bf16[1,512]{1,0:T(2,128)(2,1)S(1)}, bf16[1,512]{1,0:T(2,128)(2,1)}, u32[]{:S(2)}) copy-start(bf16[1,512]{1,0:T(2,128)(2,1)} %param.16) | copy-start | bytes 3076
  34.4 0.7 copy-start.23
  36.5 7.8 %copy-start.5 = (bf16[2048,512]{1,0:T(8,128)(2,1)S(1)}, bf16[2048,512]{1,0:T(8,128)(2,1)}, u32[]{:S(2)}) copy-start(bf16[2048,512]{1,0:T(8,128)(2,1)} %pad_maximum_fusion.19) | copy-start | bytes 6291460
  37.7 6.5 %copy-start.2 = (bf16[2048,512]{1,0:T(8,128)(2,1)S(1)}, bf16[2048,512]{1,0:T(8,128)(2,1)}, u32[]{:S(2)}) copy-start(bf16[2048,512]{1,0:T(8,128)(2,1)} %pad_maximum_fusion.22) | copy-start | bytes 6291460
  37.7 6.5 %copy-start.12 = (bf16[1,256,512]{2,1,0:T(8,128)(2,1)S(1)}, bf16[1,256,512]{2,1,0:T(8,128)(2,1)}, u32[]{:S(2)}) copy-start(bf16[1,256,512]{2,1,0:T(8,128)(2,1)} %param.12) | copy-start | bytes 786436
  37.7 6.5 %copy-start.13 = (bf16[1,256,512]{2,1,0:T(8,128)(2,1)S(1)}, bf16[1,256,512]{2,1,0:T(8,128)(2,1)}, u32[]{:S(2)}) copy-start(bf16[1,256,512]{2,1,0:T(8,128)(2,1)} %param.14) | copy-start | bytes 786436
  37.7 6.5 %copy-start.24 = (bf16[256,512]{1,0:T(8,128)(2,1)S(1)}, bf16[256,512]{1,0:T(8,128)(2,1)}, u32[]{:S(2)}) copy-start(bf16[256,512]{1,0:T(8,128)(2,1)} %copy-done.23) | copy-start | bytes 786436
  44.2 0.7 copy-start.19
  45.1 15.2 %collective-permute-start = (bf16[32,2048]{1,0:T(8,128)(2,1)S(1)}, bf16[32,2048]{1,0:T(8,128)(2,1)S(1)}, u32[]{:S(2)}, u32[]{:S(2)}) collective-permute-start(bf16[32,2048]{1,0:T(8,128)(2,1)S(1)} %multiply_convert_fusion.2), channel_id=1, source_target_pairs={{128,144},{129,145},{130,146},{131,147},{132,148},{133,149},{134,1... | collective-permute-start | bytes 393224 | tf_op jit(solution)/shard_map/cond/branch_0_fun/ppermute | solution.py:41
  48.5 11.8 %collective-permute-start.1 = (bf16[32,2048]{1,0:T(8,128)(2,1)S(1)}, bf16[32,2048]{1,0:T(8,128)(2,1)S(1)}, u32[]{:S(2)}, u32[]{:S(2)}) collective-permute-start(bf16[32,2048]{1,0:T(8,128)(2,1)S(1)} %multiply_convert_fusion.2), channel_id=1, source_target_pairs={{128,160},{129,161},{130,162},{131,163},{132,164},{133,165},{134,1... | collective-permute-start | bytes 393224 | tf_op jit(solution)/shard_map/cond/branch_0_fun/ppermute | solution.py:41
  53.2 8.1 %collective-permute-start.2 = (bf16[32,2048]{1,0:T(8,128)(2,1)S(1)}, bf16[32,2048]{1,0:T(8,128)(2,1)S(1)}, u32[]{:S(2)}, u32[]{:S(2)}) collective-permute-start(bf16[32,2048]{1,0:T(8,128)(2,1)S(1)} %multiply_convert_fusion.2), channel_id=1, source_target_pairs={{128,176},{129,177},{130,178},{131,179},{132,180},{133,181},{134,1... | collective-permute-start | bytes 393224 | tf_op jit(solution)/shard_map/cond/branch_0_fun/ppermute | solution.py:41
  55.6 8.3 %collective-permute-start.3 = (bf16[256,512]{1,0:T(8,128)(2,1)S(1)}, bf16[256,512]{1,0:T(8,128)(2,1)S(1)}, u32[]{:S(2)}, u32[]{:S(2)}) collective-permute-start(bf16[256,512]{1,0:T(8,128)(2,1)S(1)} %get-tuple-element.131), channel_id=1, source_target_pairs={{128,129},{129,128},{130,131},{131,130},{132,133},{133,132},{134,1... | collective-permute-start | bytes 786440 | tf_op jit(solution)/shard_map/cond/branch_0_fun/ppermute | solution.py:41
  63.8 4.9 %collective-permute-start.4 = (bf16[128,2048]{1,0:T(8,128)(2,1)S(1)}, bf16[128,2048]{1,0:T(8,128)(2,1)S(1)}, u32[]{:S(2)}, u32[]{:S(2)}) collective-permute-start(bf16[128,2048]{1,0:T(8,128)(2,1)S(1)} %pad_maximum_fusion), channel_id=1, source_target_pairs={{128,132},{129,133},{130,134},{131,135},{132,128},{133,129},{134,1... | collective-permute-start | bytes 1572872 | tf_op jit(solution)/shard_map/cond/branch_0_fun/ppermute | solution.py:41
  65.8 2.2 copy-start.8
  73.7 12.7 %collective-permute-start.5 = (bf16[128,2048]{1,0:T(8,128)(2,1)S(1)}, bf16[128,2048]{1,0:T(8,128)(2,1)S(1)}, u32[]{:S(2)}, u32[]{:S(2)}) collective-permute-start(bf16[128,2048]{1,0:T(8,128)(2,1)S(1)} %slice.389), channel_id=1, source_target_pairs={{128,132},{129,133},{130,134},{131,135},{132,128},{133,129},{134,1... | collective-permute-start | bytes 1572872 | tf_op jit(solution)/shard_map/cond/branch_0_fun/ppermute | solution.py:41
  77.4 25.4 %collective-permute-start.10 = (bf16[256,512]{1,0:T(8,128)(2,1)S(1)}, bf16[256,512]{1,0:T(8,128)(2,1)S(1)}, u32[]{:S(2)}, u32[]{:S(2)}) collective-permute-start(bf16[256,512]{1,0:T(8,128)(2,1)S(1)} %get-tuple-element.139), channel_id=1, source_target_pairs={{128,129},{129,128},{130,131},{131,130},{132,133},{133,132},{134,1... | collective-permute-start | bytes 786440 | tf_op jit(solution)/shard_map/cond/branch_0_fun/ppermute | solution.py:41
  80.6 22.2 %collective-permute-start.9 = (bf16[256,512]{1,0:T(8,128)(2,1)S(1)}, bf16[256,512]{1,0:T(8,128)(2,1)}, u32[]{:S(2)}, u32[]{:S(2)}) collective-permute-start(bf16[256,512]{1,0:T(8,128)(2,1)S(1)} %get-tuple-element.139), channel_id=1, source_target_pairs={{128,130},{129,131},{130,128},{131,129},{132,134},{133,135},{134,1... | collective-permute-start | bytes 786440 | tf_op jit(solution)/shard_map/cond/branch_0_fun/ppermute | solution.py:41
  86.6 12.2 %collective-permute-start.6 = (bf16[32,2048]{1,0:T(8,128)(2,1)S(1)}, bf16[32,2048]{1,0:T(8,128)(2,1)S(1)}, u32[]{:S(2)}, u32[]{:S(2)}) collective-permute-start(bf16[32,2048]{1,0:T(8,128)(2,1)S(1)} %get-tuple-element.252), channel_id=1, source_target_pairs={{128,144},{129,145},{130,146},{131,147},{132,148},{133,149},{134,1... | collective-permute-start | bytes 393224 | tf_op jit(solution)/shard_map/cond/branch_0_fun/ppermute | solution.py:41
  88.8 10.1 %collective-permute-start.7 = (bf16[32,2048]{1,0:T(8,128)(2,1)S(1)}, bf16[32,2048]{1,0:T(8,128)(2,1)S(1)}, u32[]{:S(2)}, u32[]{:S(2)}) collective-permute-start(bf16[32,2048]{1,0:T(8,128)(2,1)S(1)} %get-tuple-element.254), channel_id=1, source_target_pairs={{128,160},{129,161},{130,162},{131,163},{132,164},{133,165},{134,1... | collective-permute-start | bytes 393224 | tf_op jit(solution)/shard_map/cond/branch_0_fun/ppermute | solution.py:41
  94.6 8.1 %collective-permute-start.8 = (bf16[32,2048]{1,0:T(8,128)(2,1)S(1)}, bf16[32,2048]{1,0:T(8,128)(2,1)S(1)}, u32[]{:S(2)}, u32[]{:S(2)}) collective-permute-start(bf16[32,2048]{1,0:T(8,128)(2,1)S(1)} %get-tuple-element.253), channel_id=1, source_target_pairs={{128,176},{129,177},{130,178},{131,179},{132,180},{133,181},{134,1... | collective-permute-start | bytes 393224 | tf_op jit(solution)/shard_map/cond/branch_0_fun/ppermute | solution.py:41
  102.8 6.2 %collective-permute-start.11 = (bf16[32,1024]{1,0:T(8,128)(2,1)S(1)}, bf16[32,1024]{1,0:T(8,128)(2,1)S(1)}, u32[]{:S(2)}, u32[]{:S(2)}) collective-permute-start(bf16[32,1024]{1,0:T(8,128)(2,1)S(1)} %slice.638), channel_id=1, source_target_pairs={{128,129},{129,128},{130,131},{131,130},{132,133},{133,132},{134,1... | collective-permute-start | bytes 196616 | tf_op jit(solution)/shard_map/cond/branch_0_fun/ppermute | solution.py:41
  109.2 0.7 copy-start.25
  109.2 5.2 %collective-permute-start.53 = (bf16[32,512]{1,0:T(8,128)(2,1)}, bf16[32,512]{1,0:T(8,128)(2,1)S(1)}, u32[]{:S(2)}, u32[]{:S(2)}) collective-permute-start(bf16[32,512]{1,0:T(8,128)(2,1)} %get-tuple-element.231), channel_id=1, source_target_pairs={{72,128},{73,129},{74,130},{75,131},{76,132},{77,133},{78,134},{79... | collective-permute-start | bytes 98312 | tf_op jit(solution)/shard_map/ppermute | solution.py:41
  109.9 19.5 %collective-permute-start.51 = (bf16[32,1024]{1,0:T(8,128)(2,1)}, bf16[32,1024]{1,0:T(8,128)(2,1)S(1)}, u32[]{:S(2)}, u32[]{:S(2)}) collective-permute-start(bf16[32,1024]{1,0:T(8,128)(2,1)} %copy-done.25), channel_id=1, source_target_pairs={{128,64},{129,65},{130,66},{131,67},{132,68},{133,69},{134,70},{13... | collective-permute-start | bytes 196616 | tf_op jit(solution)/shard_map/ppermute | solution.py:41
  110.6 18.8 %collective-permute-start.52 = (bf16[32,1024]{1,0:T(8,128)(2,1)}, bf16[32,1024]{1,0:T(8,128)(2,1)}, u32[]{:S(2)}, u32[]{:S(2)}) collective-permute-start(bf16[32,1024]{1,0:T(8,128)(2,1)} %copy-done.25), channel_id=1, source_target_pairs={{192,64},{193,65},{194,66},{195,67},{196,68},{197,69},{198,70},{19... | collective-permute-start | bytes 196616 | tf_op jit(solution)/shard_map/ppermute | solution.py:41
  112.5 4.6 %collective-permute-start.54 = (bf16[32,512]{1,0:T(8,128)(2,1)}, bf16[32,512]{1,0:T(8,128)(2,1)S(1)}, u32[]{:S(2)}, u32[]{:S(2)}) collective-permute-start(bf16[32,512]{1,0:T(8,128)(2,1)} %get-tuple-element.231), channel_id=1, source_target_pairs={{72,136},{73,137},{74,138},{75,139},{76,140},{77,141},{78,142},{79... | collective-permute-start | bytes 98312 | tf_op jit(solution)/shard_map/ppermute | solution.py:41
  113.2 16.2 %collective-permute-start.55 = (bf16[32,512]{1,0:T(8,128)(2,1)}, bf16[32,512]{1,0:T(8,128)(2,1)}, u32[]{:S(2)}, u32[]{:S(2)}) collective-permute-start(bf16[32,512]{1,0:T(8,128)(2,1)} %get-tuple-element.231), channel_id=1, source_target_pairs={{72,192},{73,193},{74,194},{75,195},{76,196},{77,197},{78,198},{79... | collective-permute-start | bytes 98312 | tf_op jit(solution)/shard_map/ppermute | solution.py:41
  114.5 14.9 %collective-permute-start.56 = (bf16[32,512]{1,0:T(8,128)(2,1)}, bf16[32,512]{1,0:T(8,128)(2,1)}, u32[]{:S(2)}, u32[]{:S(2)}) collective-permute-start(bf16[32,512]{1,0:T(8,128)(2,1)} %get-tuple-element.231), channel_id=1, source_target_pairs={{72,200},{73,201},{74,202},{75,203},{76,204},{77,205},{78,206},{79... | collective-permute-start | bytes 98312 | tf_op jit(solution)/shard_map/ppermute | solution.py:41
  130.2 6.9 %collective-permute-start.34 = (bf16[32,512]{1,0:T(8,128)(2,1)S(1)}, bf16[32,512]{1,0:T(8,128)(2,1)S(1)}, u32[]{:S(2)}, u32[]{:S(2)}) collective-permute-start(bf16[32,512]{1,0:T(8,128)(2,1)S(1)} %add_add_fusion.1), channel_id=1, source_target_pairs={{128,130},{129,131},{130,128},{131,129},{132,134},{133,135},{134,1... | collective-permute-start | bytes 98312 | tf_op jit(solution)/shard_map/cond/branch_1_fun/ppermute | solution.py:41
  137.1 6.1 %collective-permute-start.35 = (bf16[32,1024]{1,0:T(8,128)(2,1)S(1)}, bf16[32,1024]{1,0:T(8,128)(2,1)S(1)}, u32[]{:S(2)}, u32[]{:S(2)}) collective-permute-start(bf16[32,1024]{1,0:T(8,128)(2,1)S(1)} %pad_maximum_fusion.17), channel_id=1, source_target_pairs={{128,129},{129,128},{130,131},{131,130},{132,133},{133,132},{134,1... | collective-permute-start | bytes 196616 | tf_op jit(solution)/shard_map/cond/branch_1_fun/ppermute | solution.py:41
  143.6 18.6 %collective-permute-start.38 = (bf16[32,2048]{1,0:T(8,128)(2,1)S(1)}, bf16[32,2048]{1,0:T(8,128)(2,1)S(1)}, u32[]{:S(2)}, u32[]{:S(2)}) collective-permute-start(bf16[32,2048]{1,0:T(8,128)(2,1)S(1)} %get-tuple-element.247), channel_id=1, source_target_pairs={{128,144},{129,145},{130,146},{131,147},{132,148},{133,149},{134,1... | collective-permute-start | bytes 393224 | tf_op jit(solution)/shard_map/cond/branch_1_fun/ppermute | solution.py:41
  145.5 16.7 %collective-permute-start.39 = (bf16[32,2048]{1,0:T(8,128)(2,1)S(1)}, bf16[32,2048]{1,0:T(8,128)(2,1)S(1)}, u32[]{:S(2)}, u32[]{:S(2)}) collective-permute-start(bf16[32,2048]{1,0:T(8,128)(2,1)S(1)} %get-tuple-element.247), channel_id=1, source_target_pairs={{128,160},{129,161},{130,162},{131,163},{132,164},{133,165},{134,1... | collective-permute-start | bytes 393224 | tf_op jit(solution)/shard_map/cond/branch_1_fun/ppermute | solution.py:41
  149.2 12.9 %collective-permute-start.40 = (bf16[32,2048]{1,0:T(8,128)(2,1)S(1)}, bf16[32,2048]{1,0:T(8,128)(2,1)S(1)}, u32[]{:S(2)}, u32[]{:S(2)}) collective-permute-start(bf16[32,2048]{1,0:T(8,128)(2,1)S(1)} %get-tuple-element.247), channel_id=1, source_target_pairs={{128,176},{129,177},{130,178},{131,179},{132,180},{133,181},{134,1... | collective-permute-start | bytes 393224 | tf_op jit(solution)/shard_map/cond/branch_1_fun/ppermute | solution.py:41
  155.0 9.5 %collective-permute-start.37 = (bf16[256,512]{1,0:T(8,128)(2,1)}, bf16[256,512]{1,0:T(8,128)(2,1)S(1)}, u32[]{:S(2)}, u32[]{:S(2)}) collective-permute-start(bf16[256,512]{1,0:T(8,128)(2,1)} %get-tuple-element.194), channel_id=1, source_target_pairs={{128,129},{129,128},{130,131},{131,130},{132,133},{133,132},{134,1... | collective-permute-start | bytes 786440 | tf_op jit(solution)/shard_map/cond/branch_1_fun/ppermute | solution.py:41
  158.3 7.4 %copy-start.7 = (bf16[2048,512]{1,0:T(8,128)(2,1)S(1)}, bf16[2048,512]{1,0:T(8,128)(2,1)}, u32[]{:S(2)}) copy-start(bf16[2048,512]{1,0:T(8,128)(2,1)} %get-tuple-element.195) | copy-start | bytes 6291460 | tf_op jit(solution)/shard_map/conditional.1
  158.4 11.4 %collective-permute-start.36 = (bf16[257,1024]{1,0:T(8,128)(2,1)S(1)}, bf16[257,1024]{1,0:T(8,128)(2,1)S(1)}, u32[]{:S(2)}, u32[]{:S(2)}) collective-permute-start(bf16[257,1024]{1,0:T(8,128)(2,1)S(1)} %pad_maximum_fusion.13), channel_id=1, source_target_pairs={{128,129},{129,128},{130,131},{131,130},{132,133},{133,132},{134,1... | collective-permute-start | bytes 1579016 | tf_op jit(solution)/shard_map/cond/branch_1_fun/ppermute | solution.py:41
  162.2 9.0 %collective-permute-start.41 = (bf16[128,2048]{1,0:T(8,128)(2,1)S(1)}, bf16[128,2048]{1,0:T(8,128)(2,1)S(1)}, u32[]{:S(2)}, u32[]{:S(2)}) collective-permute-start(bf16[128,2048]{1,0:T(8,128)(2,1)S(1)} %pad_maximum_fusion.14), channel_id=1, source_target_pairs={{128,132},{129,133},{130,134},{131,135},{132,128},{133,129},{134,1... | collective-permute-start | bytes 1572872 | tf_op jit(solution)/shard_map/cond/branch_1_fun/ppermute | solution.py:41
  171.3 1.6 copy-start.4
  173.6 1.6 copy-start.11
  175.9 22.0 %copy-start.15 = (bf16[256,512]{1,0:T(8,128)(2,1)S(1)}, bf16[256,512]{1,0:T(8,128)(2,1)}, u32[]{:S(2)}) copy-start(bf16[256,512]{1,0:T(8,128)(2,1)} %get-tuple-element.207) | copy-start | bytes 786436 | tf_op jit(solution)/shard_map/conditional.1
  176.0 12.3 %collective-permute-start.42 = (bf16[256,512]{1,0:T(8,128)(2,1)S(1)}, bf16[256,512]{1,0:T(8,128)(2,1)S(1)}, u32[]{:S(2)}, u32[]{:S(2)}) collective-permute-start(bf16[256,512]{1,0:T(8,128)(2,1)S(1)} %get-tuple-element.289), channel_id=1, source_target_pairs={{128,129},{129,128},{130,131},{131,130},{132,133},{133,132},{134,1... | collective-permute-start | bytes 786440 | tf_op jit(solution)/shard_map/cond/branch_1_fun/ppermute | solution.py:41
  179.7 13.6 %collective-permute-start.44 = (bf16[257,512]{1,0:T(8,128)(2,1)S(1)}, bf16[257,512]{1,0:T(8,128)(2,1)S(1)}, u32[]{:S(2)}, u32[]{:S(2)}) collective-permute-start(bf16[257,512]{1,0:T(8,128)(2,1)S(1)} %pad_maximum_fusion.15), channel_id=1, source_target_pairs={{128,130},{129,131},{130,128},{131,129},{132,134},{133,135},{134,1... | collective-permute-start | bytes 789512 | tf_op jit(solution)/shard_map/cond/branch_1_fun/ppermute | solution.py:41
  188.3 9.7 %collective-permute-start.43 = (bf16[256,512]{1,0:T(8,128)(2,1)S(1)}, bf16[256,512]{1,0:T(8,128)(2,1)S(1)}, u32[]{:S(2)}, u32[]{:S(2)}) collective-permute-start(bf16[256,512]{1,0:T(8,128)(2,1)S(1)} %get-tuple-element.202), channel_id=1, source_target_pairs={{128,129},{129,128},{130,131},{131,130},{132,133},{133,132},{134,1... | collective-permute-start | bytes 786440 | tf_op jit(solution)/shard_map/cond/branch_1_fun/ppermute | solution.py:41
  193.4 12.1 %collective-permute-start.45 = (bf16[256,512]{1,0:T(8,128)(2,1)S(1)}, bf16[256,512]{1,0:T(8,128)(2,1)S(1)}, u32[]{:S(2)}, u32[]{:S(2)}) collective-permute-start(bf16[256,512]{1,0:T(8,128)(2,1)S(1)} %add_convert_fusion.5), channel_id=1, source_target_pairs={{128,130},{129,131},{130,128},{131,129},{132,134},{133,135},{134,1... | collective-permute-start | bytes 786440 | tf_op jit(solution)/shard_map/cond/branch_1_fun/ppermute | solution.py:41
  206.4 15.7 %copy-start.1 = (bf16[256,512]{1,0:T(8,128)(2,1)S(1)}, bf16[256,512]{1,0:T(8,128)(2,1)}, u32[]{:S(2)}) copy-start(bf16[256,512]{1,0:T(8,128)(2,1)} %param.15) | copy-start | bytes 786436
  206.4 14.9 %collective-permute-start.57 = (bf16[256,512]{1,0:T(8,128)(2,1)}, bf16[256,512]{1,0:T(8,128)(2,1)S(1)}, u32[]{:S(2)}, u32[]{:S(2)}) collective-permute-start(bf16[256,512]{1,0:T(8,128)(2,1)} %get-tuple-element.233), channel_id=1, source_target_pairs={{128,132},{129,133},{130,134},{131,135},{132,136},{133,137},{134,1... | collective-permute-start | bytes 786440 | tf_op jit(solution)/shard_map/ppermute | solution.py:41

commit v5 on v4

--- a/solution.py
+++ b/solution.py
@@ -254,8 +254,8 @@
         c_far = swap_t(cot_shard, 2, encoders)
         a_normed = normed_a()
         out = attend_out(*project(a_normed, a_normed), w_o).astype(bf16)
-        out, b_last = tie(out, b_last)
-        summed, _, c_far = scatter(out, None, encoders, c_far)
+        out, b_last, c_far = lax.optimization_barrier((out, b_last, c_far))
+        summed, _, _ = scatter(out, None, encoders)
         enc_y = (fwd_shard.astype(f32) + summed).astype(bf16)
         blocks = enc_y.reshape(NX, NC, part, width)
         blocks = jnp.where(core == 1, blocks[:, 1], swap_core(blocks[:, 0], top_row))

time: 224 us -> 224 us (level)
  no operation moved by 1% of the time
where the time goes in v5:
time: 224 us; the launch traced here: 222 us
  starting transfers between devices  90.1 us (40%)
  waiting for transfers between devices  74.8 us (33%)
  other arithmetic  26.4 us (12%)
  matrix products  14.6 us (7%)
  local copies, waits for them, and re-layouts  14.1 us (6%)
    ppermute x36, starting transfers between devices, move(): return lax.ppermute(value, ('section', 'tensor'), pairs)  90.1 us
    ppermute x36, waiting for transfers between devices, move(): return lax.ppermute(value, ('section', 'tensor'), pairs)  74.8 us
    dot_general x11, matrix products, mm(): return jnp.dot(a, b, preferred_element_type=f32)  8.27 us
    dot_general x10, matrix products, mm_t(): lax.dot_general(a, b, (((1,), (1,)), ((), ())), preferred_element_type=f32)  5.57 us
    reduce_sum x5, other arithmetic, inverse_rms(): jnp.mean(values * values, axis=-1, keepdims=True) + epsilon  5.12 us
  transfers between devices with their start and end apart: 36, of which 17 were waited for; matrix products, arithmetic and copies ran while one was open for 15% of the time, Pallas kernels for 0%

profile of v5, /device:TPU:24, one launch (start us, length us, event | category | flops | bytes accessed | tf_op | source)
XLA Modules:
  0.0 221.9 jit_solution(4362575636640814020)
XLA Ops:
  2.7 1.4 pad_maximum_fusion.25
  4.2 1.9 collective-permute-start.47
  6.1 3.3 %collective-permute-start.46 = (bf16[290,512]{1,0:T(8,128)(2,1)}, bf16[290,512]{1,0:T(8,128)(2,1)}, u32[]{:S(2)}, u32[]{:S(2)}) collective-permute-start(bf16[290,512]{1,0:T(8,128)(2,1)} %pad_maximum_fusion.25), channel_id=1, source_target_pairs={{0,2},{1,3},{2,0},{3,1},{4,6},{5,7},{6,4},{7,5},{8,10},{9,11},{10,... | collective-permute-start | bytes 890888 | tf_op jit(solution)/shard_map/ppermute | solution.py:41
  9.4 3.2 %dynamic-slice_bitcast_fusion.3 = (bf16[512,3,512]{2,0,1:T(8,128)(2,1)S(1)}, bf16[512,3,512]{2,0,1:T(8,128)(2,1)S(1)}, bf16[512,3,512]{2,0,1:T(8,128)(2,1)S(1)}, bf16[512,3,512]{2,0,1:T(8,128)(2,1)S(1)}) fusion(bf16[1,2048,3,512]{3,1,2,0:T(8,128)(2,1)} %param.18, s32[]{:T(128)S(6)} %select_n.96, s32[]{:T(128)S(6)} %select_n.97, s32[]{:T(128)S(6)} %select_n.99, ...), kind=kLoop, calls=%fused_computation.310 | loop fusion | bytes 12582928 | tf_op jit(solution)/shard_map/dynamic_slice | solution.py:242
  13.0 1.5 pad_maximum_fusion.22
  14.7 1.4 copy-done.18
  16.4 1.5 pad_maximum_fusion.19
  17.8 2.0 collective-permute-done.47
  19.8 3.5 %collective-permute-done.46 = bf16[290,512]{1,0:T(8,128)(2,1)} collective-permute-done((bf16[290,512]{1,0:T(8,128)(2,1)}, bf16[290,512]{1,0:T(8,128)(2,1)}, u32[]{:S(2)}, u32[]{:S(2)}) %collective-permute-start.46) | collective-permute-done | bytes 296992 | tf_op jit(solution)/shard_map/ppermute | solution.py:41
  23.3 2.7 %collective-permute-start.50 = (bf16[256,512]{1,0:T(8,128)(2,1)S(1)}, bf16[256,512]{1,0:T(8,128)(2,1)}, u32[]{:S(2)}, u32[]{:S(2)}) collective-permute-start(bf16[256,512]{1,0:T(8,128)(2,1)S(1)} %get-tuple-element.225), channel_id=1, source_target_pairs={{0,1},{1,0},{2,3},{3,2},{4,5},{5,4},{6,7},{7,6},{8,9},{9,8},{10,11... | collective-permute-start | bytes 786440 | tf_op jit(solution)/shard_map/ppermute | solution.py:41
  26.1 1.7 pad_maximum_fusion.21
  27.7 6.6 %collective-permute-done.49 = bf16[256,512]{1,0:T(8,128)(2,1)S(1)} collective-permute-done((bf16[256,512]{1,0:T(8,128)(2,1)S(1)}, bf16[256,512]{1,0:T(8,128)(2,1)S(1)}, u32[]{:S(2)}, u32[]{:S(2)}) %collective-permute-start.49) | collective-permute-done | bytes 262176 | tf_op jit(solution)/shard_map/ppermute | solution.py:41
  35.1 1.4 collective-permute-done.50
  37.7 3.2 %collective-permute-done.48 = bf16[290,512]{1,0:T(8,128)(2,1)} collective-permute-done((bf16[290,512]{1,0:T(8,128)(2,1)}, bf16[290,512]{1,0:T(8,128)(2,1)}, u32[]{:S(2)}, u32[]{:S(2)}) %collective-permute-start.48) | collective-permute-done | bytes 296992 | tf_op jit(solution)/shard_map/ppermute | solution.py:41
  40.9 2.3 %pad_maximum_fusion.23 = bf16[290,2048]{1,0:T(8,128)(2,1)} fusion(bf16[290,512]{1,0:T(8,128)(2,1)} %collective-permute-done.48, bf16[290,512]{1,0:T(8,128)(2,1)} %collective-permute-done.47, bf16[290,512]{1,0:T(8,128)(2,1)} %collective-permute-done.46, bf16[1,512]{1,0:T(2,128)(2,1)S(1)} %broadcast_in_dim.6, bf16[1,512]{1,0:T(2,128)(2,1)S(1)} %copy-done.26, ...), kind=kLoop, calls=%fused_computation.311 | loop fusion | flops 8314880 | bytes 2375680 | tf_op jit(solution)/shard_map/concatenate | solution.py:234
  44.9 64.3 %conditional.4 = (bf16[256,512]{1,0:T(8,128)(2,1)}, bf16[32,512]{1,0:T(8,128)(2,1)}, bf16[256,1024]{1,0:T(8,128)(2,1)}, bf16[256,512]{1,0:T(8,128)(2,1)}, bf16[2...) conditional(s32[]{:T(128)} %convert_element_type.372, (bf16[256,512]{1,0:T(8,128)(2,1)S(1)}, ...), branch_computations={%region_0.7_spmd, %region_7.11_spmd} | conditional | flops 4110056704 | bytes 64717868 | solution.py:293
  45.1 3.4 %collective-permute-start = (bf16[32,2048]{1,0:T(8,128)(2,1)S(1)}, bf16[32,2048]{1,0:T(8,128)(2,1)S(1)}, u32[]{:S(2)}, u32[]{:S(2)}) collective-permute-start(bf16[32,2048]{1,0:T(8,128)(2,1)S(1)} %multiply_convert_fusion.2), channel_id=1, source_target_pairs={{128,144},{129,145},{130,146},{131,147},{132,148},{133,149},{134,1... | collective-permute-start | bytes 393224 | tf_op jit(solution)/shard_map/cond/branch_0_fun/ppermute | solution.py:41
  48.5 4.6 %collective-permute-start.1 = (bf16[32,2048]{1,0:T(8,128)(2,1)S(1)}, bf16[32,2048]{1,0:T(8,128)(2,1)S(1)}, u32[]{:S(2)}, u32[]{:S(2)}) collective-permute-start(bf16[32,2048]{1,0:T(8,128)(2,1)S(1)} %multiply_convert_fusion.2), channel_id=1, source_target_pairs={{128,160},{129,161},{130,162},{131,163},{132,164},{133,165},{134,1... | collective-permute-start | bytes 393224 | tf_op jit(solution)/shard_map/cond/branch_0_fun/ppermute | solution.py:41
  53.2 2.4 %collective-permute-start.2 = (bf16[32,2048]{1,0:T(8,128)(2,1)S(1)}, bf16[32,2048]{1,0:T(8,128)(2,1)S(1)}, u32[]{:S(2)}, u32[]{:S(2)}) collective-permute-start(bf16[32,2048]{1,0:T(8,128)(2,1)S(1)} %multiply_convert_fusion.2), channel_id=1, source_target_pairs={{128,176},{129,177},{130,178},{131,179},{132,180},{133,181},{134,1... | collective-permute-start | bytes 393224 | tf_op jit(solution)/shard_map/cond/branch_0_fun/ppermute | solution.py:41
  55.6 3.2 %collective-permute-start.3 = (bf16[256,512]{1,0:T(8,128)(2,1)S(1)}, bf16[256,512]{1,0:T(8,128)(2,1)S(1)}, u32[]{:S(2)}, u32[]{:S(2)}) collective-permute-start(bf16[256,512]{1,0:T(8,128)(2,1)S(1)} %get-tuple-element.131), channel_id=1, source_target_pairs={{128,129},{129,128},{130,131},{131,130},{132,133},{133,132},{134,1... | collective-permute-start | bytes 786440 | tf_op jit(solution)/shard_map/cond/branch_0_fun/ppermute | solution.py:41
  58.8 1.5 fusion.1
  61.3 2.5 %collective-permute-done.3 = bf16[256,512]{1,0:T(8,128)(2,1)S(1)} collective-permute-done((bf16[256,512]{1,0:T(8,128)(2,1)S(1)}, bf16[256,512]{1,0:T(8,128)(2,1)S(1)}, u32[]{:S(2)}, u32[]{:S(2)}) %collective-permute-start.3) | collective-permute-done | bytes 262176 | tf_op jit(solution)/shard_map/cond/branch_0_fun/ppermute | solution.py:41
  63.8 1.9 collective-permute-start.4
  65.8 2.1 convolution_convert_fusion.4
  73.7 2.4 %collective-permute-start.5 = (bf16[128,2048]{1,0:T(8,128)(2,1)S(1)}, bf16[128,2048]{1,0:T(8,128)(2,1)S(1)}, u32[]{:S(2)}, u32[]{:S(2)}) collective-permute-start(bf16[128,2048]{1,0:T(8,128)(2,1)S(1)} %slice.389), channel_id=1, source_target_pairs={{128,132},{129,133},{130,134},{131,135},{132,128},{133,129},{134,1... | collective-permute-start | bytes 1572872 | tf_op jit(solution)/shard_map/cond/branch_0_fun/ppermute | solution.py:41
  77.4 3.2 %collective-permute-start.10 = (bf16[256,512]{1,0:T(8,128)(2,1)S(1)}, bf16[256,512]{1,0:T(8,128)(2,1)S(1)}, u32[]{:S(2)}, u32[]{:S(2)}) collective-permute-start(bf16[256,512]{1,0:T(8,128)(2,1)S(1)} %get-tuple-element.139), channel_id=1, source_target_pairs={{128,129},{129,128},{130,131},{131,130},{132,133},{133,132},{134,1... | collective-permute-start | bytes 786440 | tf_op jit(solution)/shard_map/cond/branch_0_fun/ppermute | solution.py:41
  80.6 5.4 %collective-permute-start.9 = (bf16[256,512]{1,0:T(8,128)(2,1)S(1)}, bf16[256,512]{1,0:T(8,128)(2,1)}, u32[]{:S(2)}, u32[]{:S(2)}) collective-permute-start(bf16[256,512]{1,0:T(8,128)(2,1)S(1)} %get-tuple-element.139), channel_id=1, source_target_pairs={{128,130},{129,131},{130,128},{131,129},{132,134},{133,135},{134,1... | collective-permute-start | bytes 786440 | tf_op jit(solution)/shard_map/cond/branch_0_fun/ppermute | solution.py:41
  86.6 2.2 collective-permute-start.6
  88.8 5.9 %collective-permute-start.7 = (bf16[32,2048]{1,0:T(8,128)(2,1)S(1)}, bf16[32,2048]{1,0:T(8,128)(2,1)S(1)}, u32[]{:S(2)}, u32[]{:S(2)}) collective-permute-start(bf16[32,2048]{1,0:T(8,128)(2,1)S(1)} %get-tuple-element.253), channel_id=1, source_target_pairs={{128,160},{129,161},{130,162},{131,163},{132,164},{133,165},{134,1... | collective-permute-start | bytes 393224 | tf_op jit(solution)/shard_map/cond/branch_0_fun/ppermute | solution.py:41
  94.6 2.4 %collective-permute-start.8 = (bf16[32,2048]{1,0:T(8,128)(2,1)S(1)}, bf16[32,2048]{1,0:T(8,128)(2,1)S(1)}, u32[]{:S(2)}, u32[]{:S(2)}) collective-permute-start(bf16[32,2048]{1,0:T(8,128)(2,1)S(1)} %get-tuple-element.252), channel_id=1, source_target_pairs={{128,176},{129,177},{130,178},{131,179},{132,180},{133,181},{134,1... | collective-permute-start | bytes 393224 | tf_op jit(solution)/shard_map/cond/branch_0_fun/ppermute | solution.py:41
  97.0 1.8 convolution_convert_fusion
  98.8 3.9 %collective-permute-done.8 = bf16[32,2048]{1,0:T(8,128)(2,1)S(1)} collective-permute-done((bf16[32,2048]{1,0:T(8,128)(2,1)S(1)}, bf16[32,2048]{1,0:T(8,128)(2,1)S(1)}, u32[]{:S(2)}, u32[]{:S(2)}) %collective-permute-start.8) | collective-permute-done | bytes 131104 | tf_op jit(solution)/shard_map/cond/branch_0_fun/ppermute | solution.py:41
  102.8 2.2 %collective-permute-start.11 = (bf16[32,1024]{1,0:T(8,128)(2,1)S(1)}, bf16[32,1024]{1,0:T(8,128)(2,1)S(1)}, u32[]{:S(2)}, u32[]{:S(2)}) collective-permute-start(bf16[32,1024]{1,0:T(8,128)(2,1)S(1)} %slice.638), channel_id=1, source_target_pairs={{128,129},{129,128},{130,131},{131,130},{132,133},{133,132},{134,1... | collective-permute-start | bytes 196616 | tf_op jit(solution)/shard_map/cond/branch_0_fun/ppermute | solution.py:41
  105.9 3.1 %collective-permute-done.11 = bf16[32,1024]{1,0:T(8,128)(2,1)S(1)} collective-permute-done((bf16[32,1024]{1,0:T(8,128)(2,1)S(1)}, bf16[32,1024]{1,0:T(8,128)(2,1)S(1)}, u32[]{:S(2)}, u32[]{:S(2)}) %collective-permute-start.11) | collective-permute-done | bytes 65568 | tf_op jit(solution)/shard_map/cond/branch_0_fun/ppermute | solution.py:41
  110.6 1.9 collective-permute-start.52
  113.2 1.3 collective-permute-start.55
  114.5 1.3 collective-permute-start.56
  115.8 1.3 slice.458
  117.1 12.3 %collective-permute-done.55 = bf16[32,512]{1,0:T(8,128)(2,1)} collective-permute-done((bf16[32,512]{1,0:T(8,128)(2,1)}, bf16[32,512]{1,0:T(8,128)(2,1)}, u32[]{:S(2)}, u32[]{:S(2)}) %collective-permute-start.55) | collective-permute-done | bytes 32800 | tf_op jit(solution)/shard_map/ppermute | solution.py:41
  129.4 76.8 %conditional.5 = (bf16[256,512]{1,0:T(8,128)(2,1)}, f32[256,512]{1,0:T(8,128)S(1)}, f32[256,1]{0,1:T(1,128)S(1)}, f32[256,1]{0,1:T(1,128)}, f32[256,512]{1,0:T(8,128)S(1)}, /*index=5*/f32[256,1]{0,1:T(1,128)S(1)}) conditional(s32[]{:T(128)} %convert_element_type.371, (bf16[256,1024]{1,0:T(8,128)(2,1)}, bf16[256,1536]{1,0:T(8,128)(2,1)S(1)}, ...), branch_computations={%region_11.20_spmd, %region_20.27_spmd} | conditional | flops 4127371008 | bytes 97863712
  130.2 1.9 collective-permute-start.34
  132.2 2.1 fusion.119
  134.3 2.9 %collective-permute-done.34 = bf16[32,512]{1,0:T(8,128)(2,1)S(1)} collective-permute-done((bf16[32,512]{1,0:T(8,128)(2,1)S(1)}, bf16[32,512]{1,0:T(8,128)(2,1)S(1)}, u32[]{:S(2)}, u32[]{:S(2)}) %collective-permute-start.34) | collective-permute-done | bytes 32800 | tf_op jit(solution)/shard_map/cond/branch_1_fun/ppermute | solution.py:41
  137.1 2.2 %collective-permute-start.35 = (bf16[32,1024]{1,0:T(8,128)(2,1)S(1)}, bf16[32,1024]{1,0:T(8,128)(2,1)S(1)}, u32[]{:S(2)}, u32[]{:S(2)}) collective-permute-start(bf16[32,1024]{1,0:T(8,128)(2,1)S(1)} %pad_maximum_fusion.17), channel_id=1, source_target_pairs={{128,129},{129,128},{130,131},{131,130},{132,133},{133,132},{134,1... | collective-permute-start | bytes 196616 | tf_op jit(solution)/shard_map/cond/branch_1_fun/ppermute | solution.py:41
  139.4 3.9 %collective-permute-done.35 = bf16[32,1024]{1,0:T(8,128)(2,1)S(1)} collective-permute-done((bf16[32,1024]{1,0:T(8,128)(2,1)S(1)}, bf16[32,1024]{1,0:T(8,128)(2,1)S(1)}, u32[]{:S(2)}, u32[]{:S(2)}) %collective-permute-start.35) | collective-permute-done | bytes 65568 | tf_op jit(solution)/shard_map/cond/branch_1_fun/ppermute | solution.py:41
  143.6 1.9 collective-permute-start.38
  145.5 3.9 %collective-permute-start.39 = (bf16[32,2048]{1,0:T(8,128)(2,1)S(1)}, bf16[32,2048]{1,0:T(8,128)(2,1)S(1)}, u32[]{:S(2)}, u32[]{:S(2)}) collective-permute-start(bf16[32,2048]{1,0:T(8,128)(2,1)S(1)} %get-tuple-element.246), channel_id=1, source_target_pairs={{128,160},{129,161},{130,162},{131,163},{132,164},{133,165},{134,1... | collective-permute-start | bytes 393224 | tf_op jit(solution)/shard_map/cond/branch_1_fun/ppermute | solution.py:41
  149.4 4.6 %collective-permute-start.40 = (bf16[32,2048]{1,0:T(8,128)(2,1)S(1)}, bf16[32,2048]{1,0:T(8,128)(2,1)S(1)}, u32[]{:S(2)}, u32[]{:S(2)}) collective-permute-start(bf16[32,2048]{1,0:T(8,128)(2,1)S(1)} %get-tuple-element.246), channel_id=1, source_target_pairs={{128,176},{129,177},{130,178},{131,179},{132,180},{133,181},{134,1... | collective-permute-start | bytes 393224 | tf_op jit(solution)/shard_map/cond/branch_1_fun/ppermute | solution.py:41
  155.0 2.2 %collective-permute-start.37 = (bf16[256,512]{1,0:T(8,128)(2,1)}, bf16[256,512]{1,0:T(8,128)(2,1)S(1)}, u32[]{:S(2)}, u32[]{:S(2)}) collective-permute-start(bf16[256,512]{1,0:T(8,128)(2,1)} %get-tuple-element.193), channel_id=1, source_target_pairs={{128,129},{129,128},{130,131},{131,130},{132,133},{133,132},{134,1... | collective-permute-start | bytes 786440 | tf_op jit(solution)/shard_map/cond/branch_1_fun/ppermute | solution.py:41
  158.4 3.7 %collective-permute-start.36 = (bf16[257,1024]{1,0:T(8,128)(2,1)S(1)}, bf16[257,1024]{1,0:T(8,128)(2,1)S(1)}, u32[]{:S(2)}, u32[]{:S(2)}) collective-permute-start(bf16[257,1024]{1,0:T(8,128)(2,1)S(1)} %pad_maximum_fusion.13), channel_id=1, source_target_pairs={{128,129},{129,128},{130,131},{131,130},{132,133},{133,132},{134,1... | collective-permute-start | bytes 1579016 | tf_op jit(solution)/shard_map/cond/branch_1_fun/ppermute | solution.py:41
  162.2 2.2 collective-permute-start.41
  164.5 1.2 fusion.120
  165.7 1.7 convolution_convert_fusion.30
  167.4 2.3 %collective-permute-done.36 = bf16[257,1024]{1,0:T(8,128)(2,1)S(1)} collective-permute-done((bf16[257,1024]{1,0:T(8,128)(2,1)S(1)}, bf16[257,1024]{1,0:T(8,128)(2,1)S(1)}, u32[]{:S(2)}, u32[]{:S(2)}) %collective-permute-start.36) | collective-permute-done | bytes 526368 | tf_op jit(solution)/shard_map/cond/branch_1_fun/ppermute | solution.py:41
  176.0 3.7 %collective-permute-start.42 = (bf16[256,512]{1,0:T(8,128)(2,1)S(1)}, bf16[256,512]{1,0:T(8,128)(2,1)S(1)}, u32[]{:S(2)}, u32[]{:S(2)}) collective-permute-start(bf16[256,512]{1,0:T(8,128)(2,1)S(1)} %get-tuple-element.288), channel_id=1, source_target_pairs={{128,129},{129,128},{130,131},{131,130},{132,133},{133,132},{134,1... | collective-permute-start | bytes 786440 | tf_op jit(solution)/shard_map/cond/branch_1_fun/ppermute | solution.py:41
  179.7 2.4 %collective-permute-start.44 = (bf16[257,512]{1,0:T(8,128)(2,1)S(1)}, bf16[257,512]{1,0:T(8,128)(2,1)S(1)}, u32[]{:S(2)}, u32[]{:S(2)}) collective-permute-start(bf16[257,512]{1,0:T(8,128)(2,1)S(1)} %pad_maximum_fusion.15), channel_id=1, source_target_pairs={{128,130},{129,131},{130,128},{131,129},{132,134},{133,135},{134,1... | collective-permute-start | bytes 789512 | tf_op jit(solution)/shard_map/cond/branch_1_fun/ppermute | solution.py:41
  182.1 6.1 %collective-permute-done.42 = bf16[256,512]{1,0:T(8,128)(2,1)S(1)} collective-permute-done((bf16[256,512]{1,0:T(8,128)(2,1)S(1)}, bf16[256,512]{1,0:T(8,128)(2,1)S(1)}, u32[]{:S(2)}, u32[]{:S(2)}) %collective-permute-start.42) | collective-permute-done | bytes 262176 | tf_op jit(solution)/shard_map/cond/branch_1_fun/ppermute | solution.py:41
  188.2 2.6 %collective-permute-start.43 = (bf16[256,512]{1,0:T(8,128)(2,1)S(1)}, bf16[256,512]{1,0:T(8,128)(2,1)S(1)}, u32[]{:S(2)}, u32[]{:S(2)}) collective-permute-start(bf16[256,512]{1,0:T(8,128)(2,1)S(1)} %get-tuple-element.201), channel_id=1, source_target_pairs={{128,129},{129,128},{130,131},{131,130},{132,133},{133,132},{134,1... | collective-permute-start | bytes 786440 | tf_op jit(solution)/shard_map/cond/branch_1_fun/ppermute | solution.py:41
  190.9 2.4 %collective-permute-done.44 = bf16[257,512]{1,0:T(8,128)(2,1)S(1)} collective-permute-done((bf16[257,512]{1,0:T(8,128)(2,1)S(1)}, bf16[257,512]{1,0:T(8,128)(2,1)S(1)}, u32[]{:S(2)}, u32[]{:S(2)}) %collective-permute-start.44) | collective-permute-done | bytes 263200 | tf_op jit(solution)/shard_map/cond/branch_1_fun/ppermute | solution.py:41
  193.4 3.1 %collective-permute-start.45 = (bf16[256,512]{1,0:T(8,128)(2,1)S(1)}, bf16[256,512]{1,0:T(8,128)(2,1)S(1)}, u32[]{:S(2)}, u32[]{:S(2)}) collective-permute-start(bf16[256,512]{1,0:T(8,128)(2,1)S(1)} %add_convert_fusion.5), channel_id=1, source_target_pairs={{128,130},{129,131},{130,128},{131,129},{132,134},{133,135},{134,1... | collective-permute-start | bytes 786440 | tf_op jit(solution)/shard_map/cond/branch_1_fun/ppermute | solution.py:41
  198.0 7.4 %collective-permute-done.45 = bf16[256,512]{1,0:T(8,128)(2,1)S(1)} collective-permute-done((bf16[256,512]{1,0:T(8,128)(2,1)S(1)}, bf16[256,512]{1,0:T(8,128)(2,1)S(1)}, u32[]{:S(2)}, u32[]{:S(2)}) %collective-permute-start.45) | collective-permute-done | bytes 262176 | tf_op jit(solution)/shard_map/cond/branch_1_fun/ppermute | solution.py:41
  206.2 2.0 collective-permute-start.57
  209.0 1.9 fusion.147
  210.8 10.4 %collective-permute-done.57 = bf16[256,512]{1,0:T(8,128)(2,1)S(1)} collective-permute-done((bf16[256,512]{1,0:T(8,128)(2,1)}, bf16[256,512]{1,0:T(8,128)(2,1)S(1)}, u32[]{:S(2)}, u32[]{:S(2)}) %collective-permute-start.57) | collective-permute-done | bytes 262176 | tf_op jit(solution)/shard_map/ppermute | solution.py:41
  (147 shorter events, 31.4 us)
Async XLA Ops:
  0.6 1.0 copy-start
  4.2 15.6 %collective-permute-start.47 = (bf16[290,512]{1,0:T(8,128)(2,1)}, bf16[290,512]{1,0:T(8,128)(2,1)}, u32[]{:S(2)}, u32[]{:S(2)}) collective-permute-start(bf16[290,512]{1,0:T(8,128)(2,1)} %pad_maximum_fusion.25), channel_id=1, source_target_pairs={{0,1},{1,0},{2,3},{3,2},{4,5},{5,4},{6,7},{7,6},{8,9},{9,8},{10,11... | collective-permute-start | bytes 890888 | tf_op jit(solution)/shard_map/ppermute | solution.py:41
  6.1 17.3 %collective-permute-start.46 = (bf16[290,512]{1,0:T(8,128)(2,1)}, bf16[290,512]{1,0:T(8,128)(2,1)}, u32[]{:S(2)}, u32[]{:S(2)}) collective-permute-start(bf16[290,512]{1,0:T(8,128)(2,1)} %pad_maximum_fusion.25), channel_id=1, source_target_pairs={{0,2},{1,3},{2,0},{3,1},{4,6},{5,7},{6,4},{7,5},{8,10},{9,11},{10,... | collective-permute-start | bytes 890888 | tf_op jit(solution)/shard_map/ppermute | solution.py:41
  14.5 1.6 copy-start.18
  23.3 11.0 %collective-permute-start.49 = (bf16[256,512]{1,0:T(8,128)(2,1)S(1)}, bf16[256,512]{1,0:T(8,128)(2,1)S(1)}, u32[]{:S(2)}, u32[]{:S(2)}) collective-permute-start(bf16[256,512]{1,0:T(8,128)(2,1)S(1)} %get-tuple-element.225), channel_id=1, source_target_pairs={{0,2},{1,3},{2,0},{3,1},{4,6},{5,7},{6,4},{7,5},{8,10},{9,11},{10,... | collective-permute-start | bytes 786440 | tf_op jit(solution)/shard_map/ppermute | solution.py:41
  23.3 13.1 %collective-permute-start.50 = (bf16[256,512]{1,0:T(8,128)(2,1)S(1)}, bf16[256,512]{1,0:T(8,128)(2,1)}, u32[]{:S(2)}, u32[]{:S(2)}) collective-permute-start(bf16[256,512]{1,0:T(8,128)(2,1)S(1)} %get-tuple-element.225), channel_id=1, source_target_pairs={{0,1},{1,0},{2,3},{3,2},{4,5},{5,4},{6,7},{7,6},{8,9},{9,8},{10,11... | collective-permute-start | bytes 786440 | tf_op jit(solution)/shard_map/ppermute | solution.py:41
  26.0 14.8 %collective-permute-start.48 = (bf16[290,512]{1,0:T(8,128)(2,1)}, bf16[290,512]{1,0:T(8,128)(2,1)}, u32[]{:S(2)}, u32[]{:S(2)}) collective-permute-start(bf16[290,512]{1,0:T(8,128)(2,1)} %collective-permute-done.46), channel_id=1, source_target_pairs={{0,1},{1,0},{2,3},{3,2},{4,5},{5,4},{6,7},{7,6},{8,9},{9,8},{10,11... | collective-permute-start | bytes 890888 | tf_op jit(solution)/shard_map/ppermute | solution.py:41
  26.1 14.8 %copy-start.26 = (bf16[1,512]{1,0:T(2,128)(2,1)S(1)}, bf16[1,512]{1,0:T(2,128)(2,1)}, u32[]{:S(2)}) copy-start(bf16[1,512]{1,0:T(2,128)(2,1)} %param.16) | copy-start | bytes 3076
  34.4 0.7 copy-start.23
  36.5 7.8 %copy-start.5 = (bf16[2048,512]{1,0:T(8,128)(2,1)S(1)}, bf16[2048,512]{1,0:T(8,128)(2,1)}, u32[]{:S(2)}) copy-start(bf16[2048,512]{1,0:T(8,128)(2,1)} %pad_maximum_fusion.19) | copy-start | bytes 6291460
  37.7 6.5 %copy-start.2 = (bf16[2048,512]{1,0:T(8,128)(2,1)S(1)}, bf16[2048,512]{1,0:T(8,128)(2,1)}, u32[]{:S(2)}) copy-start(bf16[2048,512]{1,0:T(8,128)(2,1)} %pad_maximum_fusion.22) | copy-start | bytes 6291460
  37.7 6.5 %copy-start.12 = (bf16[1,256,512]{2,1,0:T(8,128)(2,1)S(1)}, bf16[1,256,512]{2,1,0:T(8,128)(2,1)}, u32[]{:S(2)}) copy-start(bf16[1,256,512]{2,1,0:T(8,128)(2,1)} %param.12) | copy-start | bytes 786436
  37.7 6.5 %copy-start.13 = (bf16[1,256,512]{2,1,0:T(8,128)(2,1)S(1)}, bf16[1,256,512]{2,1,0:T(8,128)(2,1)}, u32[]{:S(2)}) copy-start(bf16[1,256,512]{2,1,0:T(8,128)(2,1)} %param.14) | copy-start | bytes 786436
  37.7 6.5 %copy-start.24 = (bf16[256,512]{1,0:T(8,128)(2,1)S(1)}, bf16[256,512]{1,0:T(8,128)(2,1)}, u32[]{:S(2)}) copy-start(bf16[256,512]{1,0:T(8,128)(2,1)} %copy-done.23) | copy-start | bytes 786436
  44.2 0.7 copy-start.19
  45.1 15.2 %collective-permute-start = (bf16[32,2048]{1,0:T(8,128)(2,1)S(1)}, bf16[32,2048]{1,0:T(8,128)(2,1)S(1)}, u32[]{:S(2)}, u32[]{:S(2)}) collective-permute-start(bf16[32,2048]{1,0:T(8,128)(2,1)S(1)} %multiply_convert_fusion.2), channel_id=1, source_target_pairs={{128,144},{129,145},{130,146},{131,147},{132,148},{133,149},{134,1... | collective-permute-start | bytes 393224 | tf_op jit(solution)/shard_map/cond/branch_0_fun/ppermute | solution.py:41
  48.5 11.8 %collective-permute-start.1 = (bf16[32,2048]{1,0:T(8,128)(2,1)S(1)}, bf16[32,2048]{1,0:T(8,128)(2,1)S(1)}, u32[]{:S(2)}, u32[]{:S(2)}) collective-permute-start(bf16[32,2048]{1,0:T(8,128)(2,1)S(1)} %multiply_convert_fusion.2), channel_id=1, source_target_pairs={{128,160},{129,161},{130,162},{131,163},{132,164},{133,165},{134,1... | collective-permute-start | bytes 393224 | tf_op jit(solution)/shard_map/cond/branch_0_fun/ppermute | solution.py:41
  53.2 8.1 %collective-permute-start.2 = (bf16[32,2048]{1,0:T(8,128)(2,1)S(1)}, bf16[32,2048]{1,0:T(8,128)(2,1)S(1)}, u32[]{:S(2)}, u32[]{:S(2)}) collective-permute-start(bf16[32,2048]{1,0:T(8,128)(2,1)S(1)} %multiply_convert_fusion.2), channel_id=1, source_target_pairs={{128,176},{129,177},{130,178},{131,179},{132,180},{133,181},{134,1... | collective-permute-start | bytes 393224 | tf_op jit(solution)/shard_map/cond/branch_0_fun/ppermute | solution.py:41
  55.6 8.3 %collective-permute-start.3 = (bf16[256,512]{1,0:T(8,128)(2,1)S(1)}, bf16[256,512]{1,0:T(8,128)(2,1)S(1)}, u32[]{:S(2)}, u32[]{:S(2)}) collective-permute-start(bf16[256,512]{1,0:T(8,128)(2,1)S(1)} %get-tuple-element.131), channel_id=1, source_target_pairs={{128,129},{129,128},{130,131},{131,130},{132,133},{133,132},{134,1... | collective-permute-start | bytes 786440 | tf_op jit(solution)/shard_map/cond/branch_0_fun/ppermute | solution.py:41
  63.8 4.9 %collective-permute-start.4 = (bf16[128,2048]{1,0:T(8,128)(2,1)S(1)}, bf16[128,2048]{1,0:T(8,128)(2,1)S(1)}, u32[]{:S(2)}, u32[]{:S(2)}) collective-permute-start(bf16[128,2048]{1,0:T(8,128)(2,1)S(1)} %pad_maximum_fusion), channel_id=1, source_target_pairs={{128,132},{129,133},{130,134},{131,135},{132,128},{133,129},{134,1... | collective-permute-start | bytes 1572872 | tf_op jit(solution)/shard_map/cond/branch_0_fun/ppermute | solution.py:41
  65.8 2.2 copy-start.8
  73.7 12.7 %collective-permute-start.5 = (bf16[128,2048]{1,0:T(8,128)(2,1)S(1)}, bf16[128,2048]{1,0:T(8,128)(2,1)S(1)}, u32[]{:S(2)}, u32[]{:S(2)}) collective-permute-start(bf16[128,2048]{1,0:T(8,128)(2,1)S(1)} %slice.389), channel_id=1, source_target_pairs={{128,132},{129,133},{130,134},{131,135},{132,128},{133,129},{134,1... | collective-permute-start | bytes 1572872 | tf_op jit(solution)/shard_map/cond/branch_0_fun/ppermute | solution.py:41
  77.4 25.4 %collective-permute-start.10 = (bf16[256,512]{1,0:T(8,128)(2,1)S(1)}, bf16[256,512]{1,0:T(8,128)(2,1)S(1)}, u32[]{:S(2)}, u32[]{:S(2)}) collective-permute-start(bf16[256,512]{1,0:T(8,128)(2,1)S(1)} %get-tuple-element.139), channel_id=1, source_target_pairs={{128,129},{129,128},{130,131},{131,130},{132,133},{133,132},{134,1... | collective-permute-start | bytes 786440 | tf_op jit(solution)/shard_map/cond/branch_0_fun/ppermute | solution.py:41
  80.6 22.2 %collective-permute-start.9 = (bf16[256,512]{1,0:T(8,128)(2,1)S(1)}, bf16[256,512]{1,0:T(8,128)(2,1)}, u32[]{:S(2)}, u32[]{:S(2)}) collective-permute-start(bf16[256,512]{1,0:T(8,128)(2,1)S(1)} %get-tuple-element.139), channel_id=1, source_target_pairs={{128,130},{129,131},{130,128},{131,129},{132,134},{133,135},{134,1... | collective-permute-start | bytes 786440 | tf_op jit(solution)/shard_map/cond/branch_0_fun/ppermute | solution.py:41
  86.6 12.2 %collective-permute-start.6 = (bf16[32,2048]{1,0:T(8,128)(2,1)S(1)}, bf16[32,2048]{1,0:T(8,128)(2,1)S(1)}, u32[]{:S(2)}, u32[]{:S(2)}) collective-permute-start(bf16[32,2048]{1,0:T(8,128)(2,1)S(1)} %get-tuple-element.251), channel_id=1, source_target_pairs={{128,144},{129,145},{130,146},{131,147},{132,148},{133,149},{134,1... | collective-permute-start | bytes 393224 | tf_op jit(solution)/shard_map/cond/branch_0_fun/ppermute | solution.py:41
  88.8 10.1 %collective-permute-start.7 = (bf16[32,2048]{1,0:T(8,128)(2,1)S(1)}, bf16[32,2048]{1,0:T(8,128)(2,1)S(1)}, u32[]{:S(2)}, u32[]{:S(2)}) collective-permute-start(bf16[32,2048]{1,0:T(8,128)(2,1)S(1)} %get-tuple-element.253), channel_id=1, source_target_pairs={{128,160},{129,161},{130,162},{131,163},{132,164},{133,165},{134,1... | collective-permute-start | bytes 393224 | tf_op jit(solution)/shard_map/cond/branch_0_fun/ppermute | solution.py:41
  94.6 8.1 %collective-permute-start.8 = (bf16[32,2048]{1,0:T(8,128)(2,1)S(1)}, bf16[32,2048]{1,0:T(8,128)(2,1)S(1)}, u32[]{:S(2)}, u32[]{:S(2)}) collective-permute-start(bf16[32,2048]{1,0:T(8,128)(2,1)S(1)} %get-tuple-element.252), channel_id=1, source_target_pairs={{128,176},{129,177},{130,178},{131,179},{132,180},{133,181},{134,1... | collective-permute-start | bytes 393224 | tf_op jit(solution)/shard_map/cond/branch_0_fun/ppermute | solution.py:41
  102.8 6.2 %collective-permute-start.11 = (bf16[32,1024]{1,0:T(8,128)(2,1)S(1)}, bf16[32,1024]{1,0:T(8,128)(2,1)S(1)}, u32[]{:S(2)}, u32[]{:S(2)}) collective-permute-start(bf16[32,1024]{1,0:T(8,128)(2,1)S(1)} %slice.638), channel_id=1, source_target_pairs={{128,129},{129,128},{130,131},{131,130},{132,133},{133,132},{134,1... | collective-permute-start | bytes 196616 | tf_op jit(solution)/shard_map/cond/branch_0_fun/ppermute | solution.py:41
  109.2 0.7 copy-start.25
  109.2 5.2 %collective-permute-start.53 = (bf16[32,512]{1,0:T(8,128)(2,1)}, bf16[32,512]{1,0:T(8,128)(2,1)S(1)}, u32[]{:S(2)}, u32[]{:S(2)}) collective-permute-start(bf16[32,512]{1,0:T(8,128)(2,1)} %get-tuple-element.230), channel_id=1, source_target_pairs={{72,128},{73,129},{74,130},{75,131},{76,132},{77,133},{78,134},{79... | collective-permute-start | bytes 98312 | tf_op jit(solution)/shard_map/ppermute | solution.py:41
  109.9 19.5 %collective-permute-start.51 = (bf16[32,1024]{1,0:T(8,128)(2,1)}, bf16[32,1024]{1,0:T(8,128)(2,1)S(1)}, u32[]{:S(2)}, u32[]{:S(2)}) collective-permute-start(bf16[32,1024]{1,0:T(8,128)(2,1)} %copy-done.25), channel_id=1, source_target_pairs={{128,64},{129,65},{130,66},{131,67},{132,68},{133,69},{134,70},{13... | collective-permute-start | bytes 196616 | tf_op jit(solution)/shard_map/ppermute | solution.py:41
  110.6 18.8 %collective-permute-start.52 = (bf16[32,1024]{1,0:T(8,128)(2,1)}, bf16[32,1024]{1,0:T(8,128)(2,1)}, u32[]{:S(2)}, u32[]{:S(2)}) collective-permute-start(bf16[32,1024]{1,0:T(8,128)(2,1)} %copy-done.25), channel_id=1, source_target_pairs={{192,64},{193,65},{194,66},{195,67},{196,68},{197,69},{198,70},{19... | collective-permute-start | bytes 196616 | tf_op jit(solution)/shard_map/ppermute | solution.py:41
  112.5 4.6 %collective-permute-start.54 = (bf16[32,512]{1,0:T(8,128)(2,1)}, bf16[32,512]{1,0:T(8,128)(2,1)S(1)}, u32[]{:S(2)}, u32[]{:S(2)}) collective-permute-start(bf16[32,512]{1,0:T(8,128)(2,1)} %get-tuple-element.230), channel_id=1, source_target_pairs={{72,136},{73,137},{74,138},{75,139},{76,140},{77,141},{78,142},{79... | collective-permute-start | bytes 98312 | tf_op jit(solution)/shard_map/ppermute | solution.py:41
  113.2 16.2 %collective-permute-start.55 = (bf16[32,512]{1,0:T(8,128)(2,1)}, bf16[32,512]{1,0:T(8,128)(2,1)}, u32[]{:S(2)}, u32[]{:S(2)}) collective-permute-start(bf16[32,512]{1,0:T(8,128)(2,1)} %get-tuple-element.230), channel_id=1, source_target_pairs={{72,192},{73,193},{74,194},{75,195},{76,196},{77,197},{78,198},{79... | collective-permute-start | bytes 98312 | tf_op jit(solution)/shard_map/ppermute | solution.py:41
  114.5 14.9 %collective-permute-start.56 = (bf16[32,512]{1,0:T(8,128)(2,1)}, bf16[32,512]{1,0:T(8,128)(2,1)}, u32[]{:S(2)}, u32[]{:S(2)}) collective-permute-start(bf16[32,512]{1,0:T(8,128)(2,1)} %get-tuple-element.230), channel_id=1, source_target_pairs={{72,200},{73,201},{74,202},{75,203},{76,204},{77,205},{78,206},{79... | collective-permute-start | bytes 98312 | tf_op jit(solution)/shard_map/ppermute | solution.py:41
  130.2 6.9 %collective-permute-start.34 = (bf16[32,512]{1,0:T(8,128)(2,1)S(1)}, bf16[32,512]{1,0:T(8,128)(2,1)S(1)}, u32[]{:S(2)}, u32[]{:S(2)}) collective-permute-start(bf16[32,512]{1,0:T(8,128)(2,1)S(1)} %add_add_fusion.1), channel_id=1, source_target_pairs={{128,130},{129,131},{130,128},{131,129},{132,134},{133,135},{134,1... | collective-permute-start | bytes 98312 | tf_op jit(solution)/shard_map/cond/branch_1_fun/ppermute | solution.py:41
  137.1 6.1 %collective-permute-start.35 = (bf16[32,1024]{1,0:T(8,128)(2,1)S(1)}, bf16[32,1024]{1,0:T(8,128)(2,1)S(1)}, u32[]{:S(2)}, u32[]{:S(2)}) collective-permute-start(bf16[32,1024]{1,0:T(8,128)(2,1)S(1)} %pad_maximum_fusion.17), channel_id=1, source_target_pairs={{128,129},{129,128},{130,131},{131,130},{132,133},{133,132},{134,1... | collective-permute-start | bytes 196616 | tf_op jit(solution)/shard_map/cond/branch_1_fun/ppermute | solution.py:41
  143.6 18.6 %collective-permute-start.38 = (bf16[32,2048]{1,0:T(8,128)(2,1)S(1)}, bf16[32,2048]{1,0:T(8,128)(2,1)S(1)}, u32[]{:S(2)}, u32[]{:S(2)}) collective-permute-start(bf16[32,2048]{1,0:T(8,128)(2,1)S(1)} %get-tuple-element.246), channel_id=1, source_target_pairs={{128,144},{129,145},{130,146},{131,147},{132,148},{133,149},{134,1... | collective-permute-start | bytes 393224 | tf_op jit(solution)/shard_map/cond/branch_1_fun/ppermute | solution.py:41
  145.5 16.7 %collective-permute-start.39 = (bf16[32,2048]{1,0:T(8,128)(2,1)S(1)}, bf16[32,2048]{1,0:T(8,128)(2,1)S(1)}, u32[]{:S(2)}, u32[]{:S(2)}) collective-permute-start(bf16[32,2048]{1,0:T(8,128)(2,1)S(1)} %get-tuple-element.246), channel_id=1, source_target_pairs={{128,160},{129,161},{130,162},{131,163},{132,164},{133,165},{134,1... | collective-permute-start | bytes 393224 | tf_op jit(solution)/shard_map/cond/branch_1_fun/ppermute | solution.py:41
  149.4 12.8 %collective-permute-start.40 = (bf16[32,2048]{1,0:T(8,128)(2,1)S(1)}, bf16[32,2048]{1,0:T(8,128)(2,1)S(1)}, u32[]{:S(2)}, u32[]{:S(2)}) collective-permute-start(bf16[32,2048]{1,0:T(8,128)(2,1)S(1)} %get-tuple-element.246), channel_id=1, source_target_pairs={{128,176},{129,177},{130,178},{131,179},{132,180},{133,181},{134,1... | collective-permute-start | bytes 393224 | tf_op jit(solution)/shard_map/cond/branch_1_fun/ppermute | solution.py:41
  155.0 9.5 %collective-permute-start.37 = (bf16[256,512]{1,0:T(8,128)(2,1)}, bf16[256,512]{1,0:T(8,128)(2,1)S(1)}, u32[]{:S(2)}, u32[]{:S(2)}) collective-permute-start(bf16[256,512]{1,0:T(8,128)(2,1)} %get-tuple-element.193), channel_id=1, source_target_pairs={{128,129},{129,128},{130,131},{131,130},{132,133},{133,132},{134,1... | collective-permute-start | bytes 786440 | tf_op jit(solution)/shard_map/cond/branch_1_fun/ppermute | solution.py:41
  158.3 7.4 %copy-start.7 = (bf16[2048,512]{1,0:T(8,128)(2,1)S(1)}, bf16[2048,512]{1,0:T(8,128)(2,1)}, u32[]{:S(2)}) copy-start(bf16[2048,512]{1,0:T(8,128)(2,1)} %get-tuple-element.194) | copy-start | bytes 6291460 | tf_op jit(solution)/shard_map/conditional.1
  158.4 11.4 %collective-permute-start.36 = (bf16[257,1024]{1,0:T(8,128)(2,1)S(1)}, bf16[257,1024]{1,0:T(8,128)(2,1)S(1)}, u32[]{:S(2)}, u32[]{:S(2)}) collective-permute-start(bf16[257,1024]{1,0:T(8,128)(2,1)S(1)} %pad_maximum_fusion.13), channel_id=1, source_target_pairs={{128,129},{129,128},{130,131},{131,130},{132,133},{133,132},{134,1... | collective-permute-start | bytes 1579016 | tf_op jit(solution)/shard_map/cond/branch_1_fun/ppermute | solution.py:41
  162.2 9.0 %collective-permute-start.41 = (bf16[128,2048]{1,0:T(8,128)(2,1)S(1)}, bf16[128,2048]{1,0:T(8,128)(2,1)S(1)}, u32[]{:S(2)}, u32[]{:S(2)}) collective-permute-start(bf16[128,2048]{1,0:T(8,128)(2,1)S(1)} %pad_maximum_fusion.14), channel_id=1, source_target_pairs={{128,132},{129,133},{130,134},{131,135},{132,128},{133,129},{134,1... | collective-permute-start | bytes 1572872 | tf_op jit(solution)/shard_map/cond/branch_1_fun/ppermute | solution.py:41
  171.3 1.6 copy-start.4
  173.6 1.6 copy-start.11
  175.9 22.0 %copy-start.15 = (bf16[256,512]{1,0:T(8,128)(2,1)S(1)}, bf16[256,512]{1,0:T(8,128)(2,1)}, u32[]{:S(2)}) copy-start(bf16[256,512]{1,0:T(8,128)(2,1)} %get-tuple-element.206) | copy-start | bytes 786436 | tf_op jit(solution)/shard_map/conditional.1
  176.0 12.2 %collective-permute-start.42 = (bf16[256,512]{1,0:T(8,128)(2,1)S(1)}, bf16[256,512]{1,0:T(8,128)(2,1)S(1)}, u32[]{:S(2)}, u32[]{:S(2)}) collective-permute-start(bf16[256,512]{1,0:T(8,128)(2,1)S(1)} %get-tuple-element.288), channel_id=1, source_target_pairs={{128,129},{129,128},{130,131},{131,130},{132,133},{133,132},{134,1... | collective-permute-start | bytes 786440 | tf_op jit(solution)/shard_map/cond/branch_1_fun/ppermute | solution.py:41
  179.7 13.6 %collective-permute-start.44 = (bf16[257,512]{1,0:T(8,128)(2,1)S(1)}, bf16[257,512]{1,0:T(8,128)(2,1)S(1)}, u32[]{:S(2)}, u32[]{:S(2)}) collective-permute-start(bf16[257,512]{1,0:T(8,128)(2,1)S(1)} %pad_maximum_fusion.15), channel_id=1, source_target_pairs={{128,130},{129,131},{130,128},{131,129},{132,134},{133,135},{134,1... | collective-permute-start | bytes 789512 | tf_op jit(solution)/shard_map/cond/branch_1_fun/ppermute | solution.py:41
  188.2 9.8 %collective-permute-start.43 = (bf16[256,512]{1,0:T(8,128)(2,1)S(1)}, bf16[256,512]{1,0:T(8,128)(2,1)S(1)}, u32[]{:S(2)}, u32[]{:S(2)}) collective-permute-start(bf16[256,512]{1,0:T(8,128)(2,1)S(1)} %get-tuple-element.201), channel_id=1, source_target_pairs={{128,129},{129,128},{130,131},{131,130},{132,133},{133,132},{134,1... | collective-permute-start | bytes 786440 | tf_op jit(solution)/shard_map/cond/branch_1_fun/ppermute | solution.py:41
  193.4 11.9 %collective-permute-start.45 = (bf16[256,512]{1,0:T(8,128)(2,1)S(1)}, bf16[256,512]{1,0:T(8,128)(2,1)S(1)}, u32[]{:S(2)}, u32[]{:S(2)}) collective-permute-start(bf16[256,512]{1,0:T(8,128)(2,1)S(1)} %add_convert_fusion.5), channel_id=1, source_target_pairs={{128,130},{129,131},{130,128},{131,129},{132,134},{133,135},{134,1... | collective-permute-start | bytes 786440 | tf_op jit(solution)/shard_map/cond/branch_1_fun/ppermute | solution.py:41
  206.2 15.7 %copy-start.1 = (bf16[256,512]{1,0:T(8,128)(2,1)S(1)}, bf16[256,512]{1,0:T(8,128)(2,1)}, u32[]{:S(2)}) copy-start(bf16[256,512]{1,0:T(8,128)(2,1)} %param.15) | copy-start | bytes 786436
  206.2 14.9 %collective-permute-start.57 = (bf16[256,512]{1,0:T(8,128)(2,1)}, bf16[256,512]{1,0:T(8,128)(2,1)S(1)}, u32[]{:S(2)}, u32[]{:S(2)}) collective-permute-start(bf16[256,512]{1,0:T(8,128)(2,1)} %get-tuple-element.232), channel_id=1, source_target_pairs={{128,132},{129,133},{130,134},{131,135},{132,136},{133,137},{134,1... | collective-permute-start | bytes 786440 | tf_op jit(solution)/shard_map/ppermute | solution.py:41
